TPU v7x, 128 devices: a whole 4x4x4 slice. The times are simulated.
128 devices in a mesh: seq: 32 (over z, x, core), head: 4 (over y).
Axes of the slice: x: 4, y: 4, z: 4, core: 2. Of those that a mesh axis runs over, the one named last changes fastest.
Arguments:
- queries: bfloat16 [32768, 1024], P('seq', 'head'), may hold values from -0.14941406 to 0.14941406
- key_rows: bfloat16 [32768, 1024], P('seq', 'head'), may hold values from -0.14941406 to 0.14941406
- value_rows: bfloat16 [32768, 1024], P('seq', 'head'), may hold values from -0.14941406 to 0.14941406
- grad_out: bfloat16 [32768, 1024], P('seq', 'head'), may hold values from -6 to 6
- accepted: int32 [32768], P('seq'), may hold values 0 or 1
- decay_code: int32 [8], P('head'), may hold values from 14 to 40
- w_query: bfloat16 [6144, 1024], P(None, 'head'), may hold values from -0.078125 to 0.078125
- w_key: bfloat16 [6144, 1024], P(None, 'head'), may hold values from -0.078125 to 0.078125
- w_value: bfloat16 [6144, 1024], P(None, 'head'), may hold values from -0.078125 to 0.078125
Outputs:
- input_grad: bfloat16 [32768, 6144], P('seq', 'head')
All inputs are finite; a program needn't handle non-finite values. No bound on the sum of `accepted` on one device may be relied on, other than what follows from the above.
Results may differ from a plain program's by a relative error of at most 0.015.
Values may be sent and summed in bfloat16 or wider, within the bound.
No kernel may reach another device: no remote copies, remote signals or barrier semaphores. Data moves between devices by JAX's collectives and lax.ppermute only.
A program may use at most 192 MiB of HBM per device.

v0:
```python
import jax
import jax.numpy as jnp
from jax import lax
from jax.sharding import PartitionSpec as P

GROUP = 256


PRECISION_HIGH = lax.Precision.HIGHEST


def entering(part, axis, combine, identity, reverse):
    count = lax.axis_size(axis)
    place = lax.axis_index(axis)
    ahead = count - 1 - place if reverse else place
    gathered = jax.tree.map(lambda a: lax.all_gather(a, axis), part)
    state = jax.tree.map(lambda a, e: jnp.zeros_like(a) + jnp.asarray(e, a.dtype), part, identity)

    def one(hop, state):
        source = count - 1 - hop if reverse else hop
        return combine(
            state, jax.tree.map(lambda a: lax.dynamic_index_in_dim(a, source, 0, False), gathered)
        )

    return lax.fori_loop(0, ahead, one, state)


def split_heads(array, heads, width, block):
    rows = array.shape[0]
    shaped = array.reshape(rows // block, block, heads, width)
    return shaped.transpose(0, 2, 1, 3)


def join_heads(array):
    count, heads, block, width = array.shape
    return array.transpose(0, 2, 1, 3).reshape(count * block, heads * width)


def decay_tables(rate, block):
    where_pos = jnp.arange(block, dtype=jnp.float32)
    diff = where_pos[:, None] - where_pos[None, :]
    inside = jnp.where(
        diff[None] >= 0, jnp.exp(-rate[:, None, None] * jnp.maximum(diff, 0.0)[None]), 0.0
    )
    leading_decay = jnp.exp(-rate[:, None] * (where_pos + 1.0)[None])
    segment_begin = jnp.exp(-rate[:, None] * where_pos[None])
    lag = jnp.exp(-rate[:, None] * (block - where_pos)[None])
    tail = jnp.exp(-rate[:, None] * (block - 1.0 - where_pos)[None])
    whole = jnp.exp(-rate * block)
    return (inside, leading_decay, segment_begin, lag, tail, whole)


def pair_products(left, right):
    return jnp.einsum("hid,hjd->hij", left, right, preferred_element_type=jnp.float32)


def forward_sweep(qs, ks, vs, gs, tables, state_in):
    inside, leading_decay, segment_begin, lag, tail, whole = tables

    def forward_step(running_state, parts):
        query_segment, kc, vc, gradient_segment = parts
        scores = pair_products(gradient_segment, vc) * inside
        k_wide = kc.astype(jnp.float32)
        gradient_wide_rows = gradient_segment.astype(jnp.float32)
        query_gradient = jnp.einsum("hij,hjd->hid", scores, k_wide, precision=PRECISION_HIGH)
        query_gradient = query_gradient + leading_decay[:, :, None] * jnp.einsum(
            "pkv,pqv->pkq", gradient_wide_rows, running_state, precision=PRECISION_HIGH
        )
        state_increment = jnp.einsum(
            "hja,hjb->hab",
            k_wide * tail[:, :, None],
            vc.astype(jnp.float32),
            precision=PRECISION_HIGH,
        )
        return (whole[:, None, None] * running_state + state_increment, query_gradient)

    final, query_gradient = lax.scan(forward_step, state_in, (qs, ks, vs, gs))
    return query_gradient


def backward_sweep(qs, ks, vs, gs, tables, state_in):
    inside, leading_decay, segment_begin, lag, tail, whole = tables

    def backward_step(running_state, parts):
        query_segment, kc, vc, gradient_segment = parts
        scores = pair_products(gradient_segment, vc) * inside
        match = pair_products(query_segment, kc) * inside
        query_wide_rows = query_segment.astype(jnp.float32)
        k_wide = kc.astype(jnp.float32)
        v_wide = vc.astype(jnp.float32)
        gradient_wide_rows = gradient_segment.astype(jnp.float32)
        grad_v = jnp.einsum("hij,hid->hjd", match, gradient_wide_rows, precision=PRECISION_HIGH)
        grad_v = grad_v + lag[:, :, None] * jnp.einsum(
            "hja,hab->hjb", k_wide, running_state, precision=PRECISION_HIGH
        )
        grad_k = jnp.einsum("hij,hid->hjd", scores, query_wide_rows, precision=PRECISION_HIGH)
        grad_k = grad_k + lag[:, :, None] * jnp.einsum(
            "hjb,hab->hja", v_wide, running_state, precision=PRECISION_HIGH
        )
        state_increment = jnp.einsum(
            "rek,rem->rkm",
            query_wide_rows * segment_begin[:, :, None],
            gradient_wide_rows,
            precision=PRECISION_HIGH,
        )
        return (whole[:, None, None] * running_state + state_increment, (grad_k, grad_v))

    final, grads = lax.scan(backward_step, state_in, (qs, ks, vs, gs), reverse=True)
    return grads


def combine_states(earlier, later):
    return (earlier[0] * later[0], earlier[1] * later[0][:, None, None] + later[1])


def contract_rows(weight_rows, grads):
    return lax.dot_general(
        weight_rows, grads, (((1,), (1,)), ((), ())), preferred_element_type=jnp.float32
    )


def shards(queries, key_rows, value_rows, grad_out, accepted, decay_code, w_query, w_key, w_value):
    heads_here = decay_code.shape[0]
    width = queries.shape[1] // heads_here
    tok_rows = queries.shape[0]
    rate = jnp.exp2(-0.5 * decay_code.astype(jnp.float32))
    masked = grad_out * accepted[:, None].astype(jnp.bfloat16)
    qs = split_heads(queries, heads_here, width, GROUP)
    ks = split_heads(key_rows, heads_here, width, GROUP)
    vs = split_heads(value_rows, heads_here, width, GROUP)
    gs = split_heads(masked, heads_here, width, GROUP)
    tables = decay_tables(rate, GROUP)
    where_tok = jnp.arange(tok_rows, dtype=jnp.float32)
    k_flat = ks.transpose(1, 0, 2, 3).reshape(heads_here, tok_rows, width).astype(jnp.float32)
    v_flat = vs.transpose(1, 0, 2, 3).reshape(heads_here, tok_rows, width).astype(jnp.float32)
    q_flat = qs.transpose(1, 0, 2, 3).reshape(heads_here, tok_rows, width).astype(jnp.float32)
    g_flat = gs.transpose(1, 0, 2, 3).reshape(heads_here, tok_rows, width).astype(jnp.float32)
    to_end = jnp.exp(-rate[:, None] * (tok_rows - 1.0 - where_tok)[None])
    from_start = jnp.exp(-rate[:, None] * where_tok[None])
    end_state = jnp.einsum(
        "hsa,hsb->hab", k_flat * to_end[:, :, None], v_flat, precision=PRECISION_HIGH
    )
    start_state = jnp.einsum(
        "hta,htb->hab", q_flat * from_start[:, :, None], g_flat, precision=PRECISION_HIGH
    )
    span = jnp.exp(-rate * tok_rows)
    empty = jnp.zeros((heads_here, width, width), jnp.float32)
    identity = (jnp.ones((heads_here,), jnp.float32), empty)
    state_in = entering((span, end_state), "seq", combine_states, identity, False)[1]
    later_in = entering((span, start_state), "seq", combine_states, identity, True)[1]
    query_gradient = forward_sweep(qs, ks, vs, gs, tables, state_in)
    grad_k, grad_v = backward_sweep(qs, ks, vs, gs, tables, later_in)
    query_gradient = join_heads(query_gradient).astype(jnp.bfloat16)
    grad_k = join_heads(grad_k).astype(jnp.bfloat16)
    grad_v = join_heads(grad_v).astype(jnp.bfloat16)
    summed = lax.psum_scatter(
        (
            contract_rows(w_query, query_gradient)
            + contract_rows(w_key, grad_k)
            + contract_rows(w_value, grad_v)
        ).astype(jnp.bfloat16),
        "head",
        scatter_dimension=0,
        tiled=True,
    ).astype(jnp.float32)
    return summed.T.astype(jnp.bfloat16)


def solution(mesh):
    in_specs = (
        P("seq", "head"),
        P("seq", "head"),
        P("seq", "head"),
        P("seq", "head"),
        P("seq"),
        P("head"),
        P(None, "head"),
        P(None, "head"),
        P(None, "head"),
    )
    out_specs = P("seq", "head")
    return jax.shard_map(shards, mesh=mesh, in_specs=in_specs, out_specs=out_specs, check_vma=False)
```

profile of v0, /device:TPU:1, one launch (start us, length us, event | category | flops | bytes accessed | tf_op | source)
XLA Modules:
  0.0 396.5 jit_solution(7805511286182037714)
XLA Ops:
  6.6 2.1 reshape.134
  8.7 2.0 reshape.135
  10.7 1.9 copy.39
  18.1 2.7 fusion.77
  20.9 2.0 broadcast_multiply_fusion
  22.9 2.0 reshape.137
  24.9 2.0 reshape.138
  29.8 1.7 fusion.78
  31.6 65.1 %all-reduce = f32[64]{0:T(128)S(1)} all-reduce(f32[64]{0:T(128)S(1)} %get-tuple-element.705), channel_id=2, replica_groups=mesh['seq'=32,'head'=4] {'seq'}, use_global_device_ids=true, to_apply=%add | all-reduce | flops 64 | bytes 512
  97.3 1.9 copy.43
  99.2 1.9 copy.41
  101.1 1.9 copy.42
  104.4 1.7 while.60
  107.0 23.9 %while.62 = (s32[]{:T(128)}, f32[2,128,128]{2,1,0:T(8,128)S(1)}, bf16[4,2,256,128]{3,2,1,0:T(8,128)(2,1)}, f32[2]{0:T(128)S(1)}, bf16[4,2,256,128]{3,2,1,0:T(8,1...) while((s32[]{:T(128)}, f32[2,128,128]{2,1,0:T(8,128)S(1)}, ...), condition=%wide.region_3.4_spmd.clone.clone, body=%wide.region_2.3_spmd.clone.clone.sunk | while | flops 436929536 | bytes 3355809 | solution.py:77
  109.6 1.9 fusion.127
  115.6 1.9 fusion.127
  121.5 1.9 fusion.127
  127.5 1.9 fusion.127
  130.9 2.4 copy.44
  133.4 51.2 %while.61 = (s32[]{:T(128)}, f32[2,128,128]{2,1,0:T(8,128)S(1)}, s32[]{:T(128)}, f32[32,2]{1,0:T(8,128)}, f32[32,2,128,128]{3,2,1,0:T(8,128)}, /*index=5*/s32[]{:T(128)}, s32[]{:T(128)}, s32[]{:T(128)}, s32[]{:T(128)}) while((s32[]{:T(128)}, f32[2,128,128]{2,1,0:T(8,128)S(1)}, s32[]{:T(128)}, f32[32,2]{1,0:T(8,128)}, ...), condition=%wide.region_5.6_spmd, body=%wide.region_4.5_spmd.sunk | while | flops 65542 | bytes 393395 | solution.py:25
  186.3 41.8 %while.63 = (s32[]{:T(128)}, f32[2,128,128]{2,1,0:T(8,128)S(1)}, bf16[4,2,256,128]{3,2,1,0:T(8,128)(2,1)}, bf16[4,2,256,128]{3,2,1,0:T(8,128)(2,1)}, f32[2]{0:T(...) while((s32[]{:T(128)}, f32[2,128,128]{2,1,0:T(8,128)S(1)}, ...), condition=%wide.region_7.8_spmd.clone.clone, body=%wide.region_6.7_spmd.clone.clone.sunk | while | flops 772998144 | bytes 10631425 | solution.py:108
  190.2 1.8 fusion.143
  195.1 1.6 convolution_add_fusion.5
  200.6 1.8 fusion.143
  205.5 1.6 convolution_add_fusion.5
  211.1 1.8 fusion.143
  221.5 1.8 fusion.143
  229.7 2.4 copy.53
  232.1 10.2 %fusion.69 = f32[1024,6144]{1,0:T(8,128)} fusion(bf16[6144,256]{1,0:T(8,128)(2,1)S(1)} %copy-done, bf16[128,8,2,128]{3,2,1,0:T(2,128)(2,1)S(1)} %bitcast.186), kind=kOutput, calls=%fused_computation.87 | convolution fusion | flops 3221225472 | bytes 28835840 | tf_op jit(solution)/shard_map/dot_general | solution.py:117
  242.3 10.1 %fusion.72 = f32[1024,6144]{1,0:T(8,128)} fusion(bf16[6144,256]{1,0:T(8,128)(2,1)S(1)} %copy-done.3, bf16[128,8,2,128]{3,2,1,0:T(2,128)(2,1)S(1)} %bitcast.185), kind=kOutput, calls=%fused_computation.90 | convolution fusion | flops 3221225472 | bytes 28835840 | tf_op jit(solution)/shard_map/dot_general | solution.py:117
  252.4 22.0 %fusion.66 = bf16[6144,1024]{0,1:T(8,128)(2,1)} fusion(f32[1024,6144]{1,0:T(8,128)} %fusion.72, f32[1024,6144]{1,0:T(8,128)} %fusion.69, bf16[6144,256]{1,0:T(8,128)(2,1)S(1)} %copy-done.2, bf16[128,8,2,128]{3,2,1,0:T(2,128)(2,1)} %bitcast.184), kind=kOutput, calls=%fused_computation.80 | convolution fusion | flops 3240099840 | bytes 66584576 | tf_op jit(solution)/shard_map/dot_general | solution.py:117
  274.4 115.6 %reduce-scatter.2.cloned.1.call-done = bf16[1536,1024]{0,1:T(8,128)(2,1)} async-done(((bf16[6144,1024]{0,1:T(8,128)(2,1)}), bf16[1536,1024]{0,1:T(8,128)(2,1)}) %reduce-scatter.2.cloned.1.call-update) | async-done | bytes 3145744 | tf_op jit(solution)/shard_map/reduce_scatter | solution.py:156
  (174 shorter events, 113.3 us)
Async XLA Ops:
  6.5 225.5 %copy-start = (bf16[6144,256]{1,0:T(8,128)(2,1)S(1)}, bf16[6144,256]{1,0:T(8,128)(2,1)}, u32[]{:S(2)}) copy-start(bf16[6144,256]{1,0:T(8,128)(2,1)} %param.24) | copy-start | bytes 9437188
  6.5 8.5 %copy-start.10 = (u32[128]{0:T(128)S(1)}, u32[128]{0:T(128)}, u32[]{:S(2)}) copy-start(u32[128]{0:T(128)} %constant.132) | copy-start | bytes 1540
  6.5 9.7 %copy-start.9 = (s32[2]{0:T(128)S(1)}, s32[2]{0:T(128)}, u32[]{:S(2)}) copy-start(s32[2]{0:T(128)} %param.22) | copy-start | bytes 28
  6.5 97.8 %all-gather.6.cloned.1.call-start = ((), (), s32[]{:S(2)}) async-start(), calls=%async_computation.2 | async-start | bytes 4325376 | tf_op jit(solution)/shard_map/all_gather | solution.py:16
  10.7 10.2 %copy-start.8 = (s32[1024]{0:T(1024)S(1)}, s32[1024]{0:T(1024)}, u32[]{:S(2)}) copy-start(s32[1024]{0:T(1024)} %param.21) | copy-start | bytes 12292
  20.8 112.6 %all-gather.8.cloned.1.call-start = ((), (), s32[]{:S(2)}) async-start(), calls=%async_computation.3 | async-start | bytes 4325376 | tf_op jit(solution)/shard_map/all_gather | solution.py:16
  31.5 358.5 %reduce-scatter.2.cloned.1.call-start = ((), (), s32[]{:S(2)}) async-start(), calls=%async_computation.1 | async-start | bytes 15728640 | tf_op jit(solution)/shard_map/reduce_scatter | solution.py:156
  130.9 55.4 %copy-start.7 = (f32[256]{0:T(256)S(1)}, f32[256]{0:T(256)}, u32[]{:S(2)}) copy-start(f32[256]{0:T(256)} %iota_subtract_fusion.2) | copy-start | bytes 3076
  186.3 7.5 %copy-start.5 = (bf16[4,2,256,128]{3,2,1,0:T(8,128)(2,1)S(1)}, bf16[4,2,256,128]{3,2,1,0:T(8,128)(2,1)}, u32[]{:S(2)}) copy-start(bf16[4,2,256,128]{3,2,1,0:T(8,128)(2,1)} %get-tuple-element.1040) | copy-start | bytes 1572868 | tf_op jit(solution)/shard_map/while
  195.1 1.6 copy-start.6
  196.8 7.5 %copy-start.5 = (bf16[4,2,256,128]{3,2,1,0:T(8,128)(2,1)S(1)}, bf16[4,2,256,128]{3,2,1,0:T(8,128)(2,1)}, u32[]{:S(2)}) copy-start(bf16[4,2,256,128]{3,2,1,0:T(8,128)(2,1)} %get-tuple-element.1040) | copy-start | bytes 1572868 | tf_op jit(solution)/shard_map/while
  205.5 1.6 copy-start.6
  207.2 7.6 %copy-start.5 = (bf16[4,2,256,128]{3,2,1,0:T(8,128)(2,1)S(1)}, bf16[4,2,256,128]{3,2,1,0:T(8,128)(2,1)}, u32[]{:S(2)}) copy-start(bf16[4,2,256,128]{3,2,1,0:T(8,128)(2,1)} %get-tuple-element.1040) | copy-start | bytes 1572868 | tf_op jit(solution)/shard_map/while
  216.0 1.6 copy-start.6
  217.6 7.6 %copy-start.5 = (bf16[4,2,256,128]{3,2,1,0:T(8,128)(2,1)S(1)}, bf16[4,2,256,128]{3,2,1,0:T(8,128)(2,1)}, u32[]{:S(2)}) copy-start(bf16[4,2,256,128]{3,2,1,0:T(8,128)(2,1)} %get-tuple-element.1040) | copy-start | bytes 1572868 | tf_op jit(solution)/shard_map/while
  226.4 1.6 copy-start.6
  232.0 10.2 %copy-start.3 = (bf16[6144,256]{1,0:T(8,128)(2,1)S(1)}, bf16[6144,256]{1,0:T(8,128)(2,1)}, u32[]{:S(2)}) copy-start(bf16[6144,256]{1,0:T(8,128)(2,1)} %param.23) | copy-start | bytes 9437188
  232.0 10.2 %copy-start.4 = (bf16[4,256,2,128]{3,2,1,0:T(2,128)(2,1)S(1)}, bf16[4,256,2,128]{3,2,1,0:T(2,128)(2,1)}, u32[]{:S(2)}) copy-start(bf16[4,256,2,128]{3,2,1,0:T(2,128)(2,1)} %copy.44) | copy-start | bytes 1572868
  242.3 10.1 %copy-start.2 = (bf16[6144,256]{1,0:T(8,128)(2,1)S(1)}, bf16[6144,256]{1,0:T(8,128)(2,1)}, u32[]{:S(2)}) copy-start(bf16[6144,256]{1,0:T(8,128)(2,1)} %param.25) | copy-start | bytes 9437188
  274.4 115.6 %copy-start.1 = (bf16[6144,256]{1,0:T(8,128)(2,1)S(1)}, bf16[6144,256]{1,0:T(8,128)(2,1)}, u32[]{:S(2)}) copy-start(bf16[6144,256]{1,0:T(8,128)(2,1)} %param.24) | copy-start | bytes 9437188
Sparse Core Ops, SparseCore 0:
  20.9 50.0 all-gather.5
  73.3 45.6 all-gather.7
  274.5 115.4 reduce-scatter.1
where the time goes:
time: 400 us; the launch traced here: 397 us
  waiting for transfers between devices  116 us (29%)
  matrix products  107 us (27%)
  blocking collectives  65.1 us (16%)
  local copies, waits for them, and re-layouts  53.9 us (13%)
  other arithmetic  39.5 us (10%)
  between operations  13.9 us (3%)
    reduce_scatter x1, waiting for transfers between devices, shards(): lax.psum_scatter((contract_rows(w_query, query_gradient) + contract_rows(...  116 us
    unnamed x1, blocking collectives  65.1 us
    dot_general x3, matrix products, contract_rows(): lax.dot_general(weight_rows, grads, (((1,), (1,)), ((), ())), preferred_e...  42.3 us
    add x31, other arithmetic, combine_states(): earlier[1] * later[0][:, None, None] + later[1]  30.7 us
    mul x31, local copies, waits for them, and re-layouts, combine_states(): earlier[1] * later[0][:, None, None] + later[1]  21.3 us
    dot_general x12, matrix products, pair_products(): jnp.einsum('hid,hjd->hij', left, right, preferred_element_type=jnp.float32)  14.2 us
    reshape x4, local copies, waits for them, and re-layouts, split_heads(): shaped = array.reshape(rows // block, block, heads, width)  8.09 us
  transfers between devices with their start and end apart: 3, of which 1 were waited for; matrix products, arithmetic and copies ran while one was open for 12% of the time, Pallas kernels for 0%

commit v1 on v0

v1 whole, which is shorter than its diff:
```python
import jax
import jax.numpy as jnp
from jax import lax
from jax.experimental import pallas as pl
from jax.experimental.pallas import tpu as pltpu
from jax.sharding import PartitionSpec as P

BLK = 256
HDIM = 128
bf16 = jnp.bfloat16
f32 = jnp.float32
VMEM_LIMIT = 48 * 1024 * 1024

SEQ = 32


def place(z, x, c):
    return (z % 4) * 8 + (x % 4) * 2 + c % 2


CORE_SWAP = [(place(z, x, c), place(z, x, 1 - c)) for z in range(4) for x in range(4) for c in range(2)]
X_GROUPS = [[place(z, x, c) for x in range(4)] for z in range(4) for c in range(2)]
Z_GROUPS = [[place(z, x, c) for z in range(4)] for x in range(4) for c in range(2)]


def nt(a, b):
    return lax.dot_general(a, b, (((1,), (1,)), ((), ())), preferred_element_type=f32)


def nn(a, b):
    return lax.dot_general(a, b, (((1,), (0,)), ((), ())), preferred_element_type=f32)


def tn(a, b):
    return lax.dot_general(a, b, (((0,), (0,)), ((), ())), preferred_element_type=f32)


def spec(*shape):
    return jax.ShapeDtypeStruct(shape, bf16)


def params():
    return pltpu.CompilerParams(vmem_limit_bytes=VMEM_LIMIT)


def whole(count):
    return [pl.BlockSpec(memory_space=pltpu.VMEM)] * count


def stack_kernel(q, k, v, g, acc, first, second):
    rows = first.shape[0]
    width = q.shape[1]
    for half, out in enumerate((first, second)):
        at = pl.ds(half * rows, rows)
        out[:, 0:width] = q[at]
        out[:, width : 2 * width] = k[at]
        out[:, 2 * width : 3 * width] = v[at]
        keep = acc[0:1, half * rows : (half + 1) * rows].astype(f32)
        column = jnp.broadcast_to(keep, (HDIM, rows)).T
        wide = jnp.concatenate([column] * (width // HDIM), axis=1)
        out[:, 3 * width :] = (g[at].astype(f32) * wide).astype(bf16)


def stack(q, k, v, g, accepted):
    rows, width = q.shape
    return pl.pallas_call(
        stack_kernel,
        out_shape=[spec(rows // 2, 4 * width)] * 2,
        in_specs=whole(5),
        out_specs=whole(2),
        compiler_params=params(),
        cost_estimate=pl.CostEstimate(flops=0, bytes_accessed=16 * rows * width, transcendentals=0),
        name="stack",
    )(q, k, v, g, accepted.reshape(1, rows))


def sums_kernel(codes, first, second, out):
    rows = first.shape[0]
    heads = out.shape[2]
    width = heads * HDIM
    where = lax.broadcasted_iota(jnp.int32, (rows, HDIM), 0).astype(f32)
    for head in range(heads):
        rate = jnp.exp2(-0.5 * codes[head : head + 1, :].astype(f32))
        to_end = jnp.exp(-rate * (rows - 1.0 - where))
        from_start = jnp.exp(-rate * where)
        for half, raw in enumerate((first, second)):
            q, k, v, g = (raw[:, part * width + head * HDIM : part * width + (head + 1) * HDIM] for part in range(4))
            out[half, 0, head] = tn((k.astype(f32) * to_end).astype(bf16), v)
            out[half, 1, head] = tn((q.astype(f32) * from_start).astype(bf16), g)


def sums(codes, first, second, heads):
    return pl.pallas_call(
        sums_kernel,
        out_shape=jax.ShapeDtypeStruct((2, 2, heads, HDIM, HDIM), f32),
        in_specs=whole(3),
        out_specs=pl.BlockSpec(memory_space=pltpu.VMEM),
        compiler_params=params(),
        cost_estimate=pl.CostEstimate(flops=10**9, bytes_accessed=4 * 10**6, transcendentals=0),
        name="sums",
    )(codes, first, second)


def attend_kernel(upper, lower, state, out):
    heads = (state.shape[0] - 16) // (2 * HDIM)
    width = heads * HDIM
    row = lax.broadcasted_iota(jnp.int32, (BLK, BLK), 0)
    col = lax.broadcasted_iota(jnp.int32, (BLK, BLK), 1)
    below = row >= col
    above = col >= row
    row_pos = row.astype(f32)
    col_pos = col.astype(f32)
    where = lax.broadcasted_iota(jnp.int32, (BLK, HDIM), 0).astype(f32)
    for head in range(heads):
        code = state[2 * width + head : 2 * width + head + 1, :].astype(f32)
        rate1 = jnp.exp2(-0.5 * code)
        rate = jnp.concatenate([rate1, rate1], axis=1)
        inside = jnp.where(below, jnp.exp(-rate * jnp.maximum(row_pos - col_pos, 0.0)), 0.0)
        inside_t = jnp.where(above, jnp.exp(-rate * jnp.maximum(col_pos - row_pos, 0.0)), 0.0)
        across = jnp.exp(-rate * (BLK + row_pos - col_pos))
        across_t = jnp.exp(-rate * (BLK + col_pos - row_pos))
        lead = jnp.exp(-rate1 * (where + 1.0))
        lag = jnp.exp(-rate1 * (BLK - where))
        whole_block = jnp.exp(-rate1 * BLK)
        at = lambda raw, part: raw[:, part * width + head * HDIM : part * width + (head + 1) * HDIM]
        q0, k0, v0, g0 = (at(upper, part) for part in range(4))
        q1, k1, v1, g1 = (at(lower, part) for part in range(4))
        kv = state[head * HDIM : (head + 1) * HDIM, :]
        qg = state[width + head * HDIM : width + (head + 1) * HDIM, :]
        cut = lambda a, d: (a * d).astype(bf16)
        p00 = cut(nt(g0, v0), inside)
        p10 = cut(nt(g1, v0), across)
        p11 = cut(nt(g1, v1), inside)
        t00 = cut(nt(v0, g0), inside_t)
        t01 = cut(nt(v0, g1), across_t)
        t11 = cut(nt(v1, g1), inside_t)
        m00 = cut(nt(k0, q0), inside_t)
        m01 = cut(nt(k0, q1), across_t)
        m11 = cut(nt(k1, q1), inside_t)
        dq0 = nn(p00, k0) + lead * nt(g0, kv)
        dq1 = nn(p10, k0) + nn(p11, k1) + (lead * whole_block) * nt(g1, kv)
        dk0 = nn(t00, q0) + nn(t01, q1) + (lag * whole_block) * nt(v0, qg)
        dk1 = nn(t11, q1) + lag * nt(v1, qg)
        dv0 = nn(m00, g0) + nn(m01, g1) + (lag * whole_block) * nn(k0, qg)
        dv1 = nn(m11, g1) + lag * nn(k1, qg)
        for part, pair in enumerate(((dq0, dq1), (dk0, dk1), (dv0, dv1))):
            here = pl.ds(part * width + head * HDIM, HDIM)
            out[0:BLK, here] = pair[0].astype(bf16)
            out[BLK:, here] = pair[1].astype(bf16)


def attend(upper, lower, state):
    wide = upper.shape[1]
    return pl.pallas_call(
        attend_kernel,
        out_shape=spec(2 * BLK, wide // 4 * 3),
        in_specs=whole(3),
        out_specs=pl.BlockSpec(memory_space=pltpu.VMEM),
        compiler_params=params(),
        cost_estimate=pl.CostEstimate(flops=2 * 10**9, bytes_accessed=2 * 10**6, transcendentals=0),
        name="attend",
    )(upper, lower, state)


def pieces_kernel(at, a, b, c, out):
    width = a.shape[-1]
    for part, w in enumerate((a, b, c)):
        out[:, :, part * width : (part + 1) * width] = w[:, 0]


def pieces(at, weights, groups):
    rows, width = weights[0].shape
    share = rows // (groups * SEQ)
    shaped = [w.reshape(groups, SEQ, share, width) for w in weights]
    block = pl.BlockSpec((groups, 1, share, width), lambda i, at: (0, at[0], 0, 0))
    return pl.pallas_call(
        pieces_kernel,
        out_shape=spec(groups, share, 3 * width),
        grid_spec=pltpu.PrefetchScalarGridSpec(
            num_scalar_prefetch=1,
            grid=(1,),
            in_specs=[block] * 3,
            out_specs=pl.BlockSpec((groups, share, 3 * width), lambda i, at: (0, 0, 0)),
        ),
        compiler_params=params(),
        name="pieces",
    )(at, *shaped)


def project_kernel(order, g0, a0, b0, c0, g1, a1, b1, c10, c11, w, out):
    cols = out.shape[1]
    depth = g0.shape[1]
    load = lambda src: w[:, pl.ds(order[src], 1)].reshape(cols, depth)
    half = g0.shape[0]
    total = None
    for src, part in enumerate((g0, a0, b0, c0)):
        term = nt(part[...], load(src))
        total = term if total is None else total + term
    out[0:half] = total.astype(bf16)
    total = None
    for src, part in enumerate((g1, a1, b1)):
        term = nt(part[...], load(src))
        total = term if total is None else total + term
    last = load(3)
    quarter = half // 2
    out[half : half + quarter] = (total[0:quarter] + nt(c10[...], last)).astype(bf16)
    out[half + quarter :] = (total[quarter:] + nt(c11[...], last)).astype(bf16)


def project(order, parts, w):
    steps = 4
    rows = 2 * parts[0].shape[0]
    seq, groups, share, depth = w.shape
    cols = seq * share // steps
    full = lambda a: pl.BlockSpec(a.shape, lambda i, order: (0, 0))
    return pl.pallas_call(
        project_kernel,
        out_shape=spec(rows, seq * share),
        grid_spec=pltpu.PrefetchScalarGridSpec(
            num_scalar_prefetch=1,
            grid=(steps,),
            in_specs=[full(a) for a in parts]
            + [pl.BlockSpec((seq // steps, groups, share, depth), lambda i, order: (i, 0, 0, 0))],
            out_specs=pl.BlockSpec((rows, cols), lambda i, order: (0, i)),
        ),
        compiler_params=params(),
        cost_estimate=pl.CostEstimate(flops=10**10, bytes_accessed=19 * 10**6, transcendentals=0),
        name="project",
    )(order, *parts, w)


def turn(a, by):
    return lax.ppermute(a, "head", [(i, (i + by) % 4) for i in range(4)])


def ring(a):
    half = a.shape[0] // 2
    left = turn(a, 1)
    right = turn(a, -1)
    return left, right, turn(left[:half], 1), turn(right[half:], -1)


def powers(rate, span, counts):
    return jnp.exp(-rate * span * counts)


def enter(local, rate):
    seq = lax.axis_index("seq")
    z, x, c = seq // 8, (seq // 2) % 4, seq % 2
    late = (c == 1)
    rows = 1024.0
    r = rate[:, None, None]
    one = jnp.exp(-r * rows)
    two = jnp.exp(-r * (2 * rows))
    message = local.astype(bf16)
    other = lax.ppermute(message, "seq", CORE_SWAP).astype(f32)
    mine = message.astype(f32)
    first = jnp.where(late, other, mine)
    second = jnp.where(late, mine, other)
    chip = jnp.stack([one * first[0] + second[0], first[1] + one * second[1]]).astype(bf16)
    line = lax.all_to_all(
        jnp.broadcast_to(chip[None], (4, *chip.shape)), "seq", 0, 0, axis_index_groups=X_GROUPS
    ).astype(f32)
    there = jnp.arange(4)
    step = lambda gap, span: jnp.where(
        gap[:, None] >= 0, jnp.exp(-rate[None] * (span * jnp.maximum(gap, 0).astype(f32)[:, None])), 0.0
    )[:, :, None, None]
    span2, span8 = 2 * rows, 8 * rows
    before = (step(x - 1 - there, span2) * line[:, 0]).sum(0)
    after = (step(there - x - 1, span2) * line[:, 1]).sum(0)
    line_kv = (step(3 - there, span2) * line[:, 0]).sum(0)
    line_qg = (step(there, span2) * line[:, 1]).sum(0)
    up = (there > z)[:, None, None, None]
    send = jnp.where(up, line_kv[None], line_qg[None]).astype(bf16)
    column = lax.all_to_all(send, "seq", 0, 0, axis_index_groups=Z_GROUPS).astype(f32)
    far_kv = (step(z - 1 - there, span8) * column).sum(0)
    far_qg = (step(there - z - 1, span8) * column).sum(0)
    xf = x.astype(f32)
    kv = before + jnp.exp(-r * (span2 * xf)) * far_kv
    qg = after + jnp.exp(-r * (span2 * (3.0 - xf))) * far_qg
    kv = jnp.where(late, one * kv + other[0], kv)
    qg = jnp.where(late, qg, one * qg + other[1])
    return kv, qg


def shards(queries, key_rows, value_rows, grad_out, accepted, decay_code, w_query, w_key, w_value):
    heads = decay_code.shape[0]
    seq = lax.axis_index("seq").astype(jnp.int32)
    y = lax.axis_index("head").astype(jnp.int32)
    rate = jnp.exp2(-0.5 * decay_code.astype(f32))
    first, second = stack(queries, key_rows, value_rows, grad_out, accepted)
    a0, b0, c00, c01 = ring(first)

    own = pieces(seq.reshape(1), (w_query, w_key, w_value), 4)
    got = lax.all_to_all(own, "head", 0, 0)
    w = lax.all_gather(got, "seq")

    codes = jnp.broadcast_to(decay_code.astype(bf16)[:, None], (heads, HDIM))
    code_rows = jnp.pad(codes, ((0, 16 - heads), (0, 0)))
    local = sums(code_rows, first, second, heads)
    half = jnp.exp(-rate * first.shape[0])[:, None, None]
    kv_all = half * local[0, 0] + local[1, 0]
    qg_all = local[0, 1] + half * local[1, 1]
    kv_in, qg_in = enter(jnp.stack([kv_all, qg_all]), rate)
    kv_mid = half * kv_in + local[0, 0]
    qg_mid = half * qg_in + local[1, 1]

    def pack(kv, qg):
        return jnp.concatenate([kv.astype(bf16).reshape(-1, HDIM), qg.astype(bf16).reshape(-1, HDIM), code_rows], 0)

    state0 = pack(kv_in, qg_mid)
    state1 = pack(kv_mid, qg_in)
    states = lax.all_to_all(jnp.broadcast_to(state0[None], (4, *state0.shape)), "head", 0, 0)
    pick = lambda by: lax.dynamic_index_in_dim(states, (y + by) % 4, 0, False)

    done1 = attend(second[:BLK], second[BLK:], state1)
    a1, b1, c10, c11 = ring(done1)
    done0 = attend(first[:BLK], first[BLK:], state0)
    left0 = attend(a0[:BLK], a0[BLK:], pick(3))
    right0 = attend(b0[:BLK], b0[BLK:], pick(1))
    far0 = attend(c00, c01, pick(2))
    order = (y + jnp.array([0, 3, 1, 2], jnp.int32)) % 4
    return project(order, (done0, left0, right0, far0, done1, a1, b1, c10, c11), w)


def solution(mesh):
    in_specs = (P("seq", "head"),) * 4 + (P("seq"), P("head")) + (P(None, "head"),) * 3
    return jax.shard_map(shards, mesh=mesh, in_specs=in_specs, out_specs=P("seq", "head"), check_vma=False)
```

time: 400 us -> 145 us (0.36)
  matrix products: 107 us -> 0 us
  waiting for transfers between devices: 116 us -> 34.6 us
  blocking collectives: 65.1 us -> 10.7 us
  local copies, waits for them, and re-layouts: 53.9 us -> 20.7 us
  other arithmetic: 39.5 us -> 7.62 us
  Pallas kernels: 0 us -> 30.2 us
  starting transfers between devices: 0.09 us -> 24.2 us
    reduce_scatter x1 -> x0, waiting for transfers between devices: 116 us -> none  [shards(): lax.psum_scatter((contract_rows(w_query, query_gradient) + contract_rows(...]
    dot_general x49 -> x0, matrix products: 107 us -> none  [the longest x3 42.3 us: contract_rows(): lax.dot_general(weight_rows, grads, (((1,), (1,)), ((), ())), preferred_e...]
    unnamed x1 -> x0, blocking collectives: 65.1 us -> none
    add x32 -> x0, other arithmetic: 30.7 us -> none  [the longest x31 30.7 us: combine_states(): earlier[1] * later[0][:, None, None] + later[1]]
    pallas_call x0 -> x9, Pallas kernels: none -> 30.2 us  [the longest x1 17.5 us: project(): pl.pallas_call(project_kernel, out_shape=spec(rows, seq * share), grid_sp...]
    all_to_all x0 -> x3, waiting for transfers between devices: none -> 27.5 us  [the longest x1 10.3 us: enter(): lax.all_to_all(jnp.broadcast_to(chip[None], (4, *chip.shape)), 'seq', 0,...]
    mul x31 -> x3, local copies, waits for them, and re-layouts: 21.3 us -> 1.86 us  [the longest x1 0.65 us: shards(): kv_all = half * local[0, 0] + local[1, 0]]
    ppermute x0 -> x9, starting transfers between devices: none -> 12.3 us  [the longest x8 9.53 us: turn(): return lax.ppermute(a, 'head', [(i, (i + by) % 4) for i in range(4)])]
  transfers between devices with their start and end apart: 3 -> 13, of which waited for: 1 -> 6; matrix products, arithmetic and copies ran while one was open for 12% -> 13% of each run, Pallas kernels for 0% -> 8%
where the time goes in v1:
time: 145 us; the launch traced here: 142 us
  waiting for transfers between devices  34.6 us (24%)
  Pallas kernels  30.2 us (21%)
  starting transfers between devices  24.2 us (17%)
  local copies, waits for them, and re-layouts  20.7 us (14%)
  between operations  13.7 us (9%)
  blocking collectives  10.7 us (7%)
  other arithmetic  7.62 us (5%)
    pallas_call x1, Pallas kernels, project(): pl.pallas_call(project_kernel, out_shape=spec(rows, seq * share), grid_sp...  17.5 us
    all_to_all x1, blocking collectives, shards(): got = lax.all_to_all(own, 'head', 0, 0)  10.7 us
    pallas_call x5, Pallas kernels, attend(): pl.pallas_call(attend_kernel, out_shape=spec(2 * BLK, wide // 4 * 3), in_...  10.6 us
    all_to_all x1, waiting for transfers between devices, enter(): lax.all_to_all(jnp.broadcast_to(chip[None], (4, *chip.shape)), 'seq', 0,...  10.3 us
    unnamed x36, local copies, waits for them, and re-layouts  9.94 us
    ppermute x8, starting transfers between devices, turn(): return lax.ppermute(a, 'head', [(i, (i + by) % 4) for i in range(4)])  9.53 us
    all_to_all x1, waiting for transfers between devices, enter(): lax.all_to_all(send, 'seq', 0, 0, axis_index_groups=Z_GROUPS).astype(f32)  9.51 us
    all_to_all x1, waiting for transfers between devices, shards(): lax.all_to_all(jnp.broadcast_to(state0[None], (4, *state0.shape)), 'head'...  7.66 us
  transfers between devices with their start and end apart: 13, of which 6 were waited for; matrix products, arithmetic and copies ran while one was open for 13% of the time, Pallas kernels for 8%

profile of v1, /device:TPU:1, one launch (start us, length us, event | category | flops | bytes accessed | tf_op | source)
XLA Modules:
  0.0 141.8 jit_solution(14863162817770727223)
XLA Ops:
  6.5 1.9 %copy-done = bf16[6144,256]{1,0:T(8,128)(2,1)S(1)} copy-done((bf16[6144,256]{1,0:T(8,128)(2,1)S(1)}, bf16[6144,256]{1,0:T(8,128)(2,1)}, u32[]{:S(2)}) %copy-start) | copy-done | bytes 3145752
  8.4 1.1 pieces.1
  9.5 10.7 %all_to_all.20 = bf16[4,48,768]{2,1,0:T(8,128)(2,1)} all-to-all(bf16[4,48,768]{2,1,0:T(8,128)(2,1)S(1)} %pieces.1), channel_id=1, replica_groups=mesh['seq'=32,'head'=4] {'head'}, dimensions={0} | all-to-all | bytes 589824 | tf_op jit(solution)/shard_map/all_to_all | solution.py:295
  23.1 2.4 %collective-permute-start.2 = (bf16[512,1024]{1,0:T(8,128)(2,1)S(1)}, bf16[512,1024]{1,0:T(8,128)(2,1)}, u32[]{:S(2)}, u32[]{:S(2)}) collective-permute-start(bf16[512,1024]{1,0:T(8,128)(2,1)S(1)} %get-tuple-element.7.first), channel_id=1, source_target_pairs={{0,3},{1,0},{2,1},{3,2},{4,7},{5,4},{6,5},{7,6},{8,11},{9,8},{10,9... | collective-permute-start | bytes 3145736 | tf_op jit(solution)/shard_map/ppermute | solution.py:233
  26.4 2.8 %collective-permute-start = (bf16[2,2,128,128]{3,2,1,0:T(8,128)(2,1)S(1)}, bf16[2,2,128,128]{3,2,1,0:T(8,128)(2,1)S(1)}, u32[]{:S(2)}, u32[]{:S(2)}) collective-permute-start(bf16[2,2,128,128]{3,2,1,0:T(8,128)(2,1)S(1)} %pad_maximum_fusion.2), channel_id=1, source_target_pairs={{0,4},{4,0},{8,12},{12,8},{16,20},{20,16},{24,28},{28,24},{32,36},... | collective-permute-start | bytes 393224 | tf_op jit(solution)/shard_map/ppermute | solution.py:256
  33.5 4.0 %all-to-all-start = ((bf16[4,2,2,128,128]{4,3,2,1,0:T(8,128)(2,1)}), bf16[4,2,2,128,128]{4,3,2,1,0:T(8,128)(2,1)S(1)}, u32[]{:S(2)}, u32[]{:S(2)}) async-start(bf16[4,2,2,128,128]{4,3,2,1,0:T(8,128)(2,1)} %broadcast_in_dim.111), calls=%async_computation | async-start | bytes 1048576 | tf_op jit(solution)/shard_map/all_to_all | solution.py:261
  38.2 1.2 fusion.24
  39.4 10.3 %all-to-all-done = bf16[4,2,2,128,128]{4,3,2,1,0:T(8,128)(2,1)S(1)} async-done(((bf16[4,2,2,128,128]{4,3,2,1,0:T(8,128)(2,1)}), bf16[4,2,2,128,128]{4,3,2,1,0:T(8,128)(2,1)S(1)}, u32[]{:S(2)}, u32[]{:S(2)}) %all-to-all-start) | async-done | bytes 524320 | tf_op jit(solution)/shard_map/all_to_all | solution.py:261
  49.8 1.7 %multiply_reduce_fusion.3 = (f32[2,128,128]{2,1,0:T(8,128)}, f32[2,128,128]{2,1,0:T(8,128)}, bf16[2,128,128]{2,1,0:T(8,128)(2,1)S(1)}, bf16[2,128,128]{2,1,0:T(8,128)(2,1)S(1)}) fusion(f32[4,2,2,128,128]{4,3,2,1,0:T(8,128)S(1)} %convert_element_type.95, f32[4,2]{1,0:T(4,128)} %get-tuple-element.54, f32[4,2]{1,0:T(4,128)} %get-tuple-element.52, ...), kind=kLoop, calls=%fused_computation.10 | loop fusion | flops 917504 | bytes 1441920 | tf_op jit(solution)/shard_map/reduce_sum | solution.py:269
  51.5 1.4 select_convert_fusion
  53.0 3.7 %all-to-all-start.1 = ((bf16[4,2,128,128]{3,2,1,0:T(8,128)(2,1)}), bf16[4,2,128,128]{3,2,1,0:T(8,128)(2,1)S(1)}, u32[]{:S(2)}, u32[]{:S(2)}) async-start(bf16[4,2,128,128]{3,2,1,0:T(8,128)(2,1)} %select_convert_fusion), calls=%async_computation.1 | async-start | bytes 524288 | tf_op jit(solution)/shard_map/all_to_all | solution.py:275
  56.7 9.5 %all-to-all-done.1 = bf16[4,2,128,128]{3,2,1,0:T(8,128)(2,1)S(1)} async-done(((bf16[4,2,128,128]{3,2,1,0:T(8,128)(2,1)}), bf16[4,2,128,128]{3,2,1,0:T(8,128)(2,1)S(1)}, u32[]{:S(2)}, u32[]{:S(2)}) %all-to-all-start.1) | async-done | bytes 262176 | tf_op jit(solution)/shard_map/all_to_all | solution.py:275
  66.4 1.2 fusion.9
  68.4 2.6 %attend.9.g1 = bf16[512,768]{1,0:T(8,128)(2,1)} custom-call(bf16[256,1024]{1,0:T(8,128)(2,1)S(1)} %copy-done.7, bf16[256,1024]{1,0:T(8,128)(2,1)S(1)} %copy-done.6, bf16[528,128]{1,0:T(8,128)(2,1)S(1)} %get-tuple-element.42.state), custom_call_target="tpu_custom_call" | custom-call | flops 2000000000 | bytes 2000000 | tf_op jit(solution)/shard_map/attend/pallas_call | solution.py:154
  73.4 4.1 %all-to-all-start.2 = ((bf16[4,528,128]{2,1,0:T(8,128)(2,1)}), bf16[4,528,128]{2,1,0:T(8,128)(2,1)}, u32[]{:S(2)}, u32[]{:S(2)}) async-start(bf16[4,528,128]{2,1,0:T(8,128)(2,1)} %broadcast_in_dim.119), calls=%async_computation.2 | async-start | bytes 1081344 | tf_op jit(solution)/shard_map/all_to_all | solution.py:313
  77.6 1.4 fusion.26
  79.0 1.4 collective-permute-start.3
  80.4 1.3 fusion.25
  81.6 1.5 %collective-permute-start.4 = (bf16[256,1024]{1,0:T(8,128)(2,1)S(1)}, bf16[256,1024]{1,0:T(8,128)(2,1)}, u32[]{:S(2)}, u32[]{:S(2)}) collective-permute-start(bf16[256,1024]{1,0:T(8,128)(2,1)S(1)} %get-tuple-element.23.lower), channel_id=1, source_target_pairs={{0,3},{1,0},{2,1},{3,2},{4,7},{5,4},{6,5},{7,6},{8,11},{9,8},{10,9... | collective-permute-start | bytes 1572872 | tf_op jit(solution)/shard_map/ppermute | solution.py:233
  84.2 1.7 %attend.5.g0 = bf16[512,768]{1,0:T(8,128)(2,1)S(1)} custom-call(bf16[256,1024]{1,0:T(8,128)(2,1)S(1)} %get-tuple-element.55.upper, bf16[256,1024]{1,0:T(8,128)(2,1)S(1)} %copy-done.5, bf16[528,128]{1,0:T(8,128)(2,1)S(1)} %get-tuple-element.43.state), custom_call_target="tpu_custom_call" | custom-call | flops 2000000000 | bytes 2000000 | tf_op jit(solution)/shard_map/attend/pallas_call | solution.py:154
  86.7 7.7 %all-to-all-done.2 = bf16[4,528,128]{2,1,0:T(8,128)(2,1)} async-done(((bf16[4,528,128]{2,1,0:T(8,128)(2,1)}), bf16[4,528,128]{2,1,0:T(8,128)(2,1)}, u32[]{:S(2)}, u32[]{:S(2)}) %all-to-all-start.2) | async-done | bytes 540704 | tf_op jit(solution)/shard_map/all_to_all | solution.py:313
  94.4 1.1 dynamic-slice_bitcast_fusion
  96.5 2.2 %collective-permute-start.8 = (bf16[256,768]{1,0:T(8,128)(2,1)S(1)}, bf16[256,768]{1,0:T(8,128)(2,1)S(1)}, u32[]{:S(2)}, u32[]{:S(2)}) collective-permute-start(bf16[256,768]{1,0:T(8,128)(2,1)S(1)} %slice.111), channel_id=1, source_target_pairs={{0,3},{1,0},{2,1},{3,2},{4,7},{5,4},{6,5},{7,6},{8,11},{9,8},{10,9... | collective-permute-start | bytes 1179656 | tf_op jit(solution)/shard_map/ppermute | solution.py:233
  100.0 1.7 %attend.6.a0 = bf16[512,768]{1,0:T(8,128)(2,1)S(1)} custom-call(bf16[256,1024]{1,0:T(8,128)(2,1)S(1)} %get-tuple-element.26.upper, bf16[256,1024]{1,0:T(8,128)(2,1)S(1)} %get-tuple-element.25.lower, bf16[528,128]{1,0:T(8,128)(2,1)S(1)} %get-tuple-element.31.state), custom_call_target="tpu_custom_call" | custom-call | flops 2000000000 | bytes 2000000 | tf_op jit(solution)/shard_map/attend/pallas_call | solution.py:154
  101.6 1.7 %attend.7.b0 = bf16[512,768]{1,0:T(8,128)(2,1)S(1)} custom-call(bf16[256,1024]{1,0:T(8,128)(2,1)S(1)} %get-tuple-element.24.upper, bf16[256,1024]{1,0:T(8,128)(2,1)S(1)} %get-tuple-element.23.lower, bf16[528,128]{1,0:T(8,128)(2,1)S(1)} %get-tuple-element.30.state), custom_call_target="tpu_custom_call" | custom-call | flops 2000000000 | bytes 2000000 | tf_op jit(solution)/shard_map/attend/pallas_call | solution.py:154
  104.2 2.6 %collective-permute-done.3.upper = bf16[256,1024]{1,0:T(8,128)(2,1)} collective-permute-done((bf16[256,1024]{1,0:T(8,128)(2,1)S(1)}, bf16[256,1024]{1,0:T(8,128)(2,1)}, u32[]{:S(2)}, u32[]{:S(2)}) %collective-permute-start.3) | collective-permute-done | bytes 524320 | tf_op jit(solution)/shard_map/ppermute | solution.py:233
  106.8 3.0 %attend.8.c0 = bf16[512,768]{1,0:T(8,128)(2,1)S(1)} custom-call(bf16[256,1024]{1,0:T(8,128)(2,1)} %collective-permute-done.3.upper, bf16[256,1024]{1,0:T(8,128)(2,1)} %collective-permute-done.4.lower, bf16[528,128]{1,0:T(8,128)(2,1)S(1)} %get-tuple-element.29.state), custom_call_target="tpu_custom_call" | custom-call | flops 2000000000 | bytes 2000000 | tf_op jit(solution)/shard_map/attend/pallas_call | solution.py:154
  110.7 3.3 %collective-permute-done.8.c11 = bf16[256,768]{1,0:T(8,128)(2,1)S(1)} collective-permute-done((bf16[256,768]{1,0:T(8,128)(2,1)S(1)}, bf16[256,768]{1,0:T(8,128)(2,1)S(1)}, u32[]{:S(2)}, u32[]{:S(2)}) %collective-permute-start.8) | collective-permute-done | bytes 393248 | tf_op jit(solution)/shard_map/ppermute | solution.py:233
  114.0 1.2 collective-permute-done.7.c10
  115.2 1.1 copy-done.14
  116.3 1.1 copy-done.16
  117.4 17.5 %project.1 = bf16[1024,1536]{1,0:T(8,128)(2,1)} custom-call(s32[4]{0:T(128)S(1)} %and_select_fusion.order, bf16[512,768]{1,0:T(8,128)(2,1)S(1)} %copy-done.10, bf16[512,768]{1,0:T(8,128)(2,1)S(1)} %copy-done.12, bf16[512,768]{1,0:T(8,128)(2,1)S(1)} %copy-done.14, bf16[512,768]{1,0:T(8,128)(2,1)S(1)} %copy-done.16, bf16[512,768]{1,0:T(8,128)(2,1)} %attend.9.g1, ...), custom_call_target="tpu_custom_call" | custom-call | flops 10000000000 | bytes 19000000 | tf_op jit(solution)/shard_map/project/pallas_call | solution.py:216
  (79 shorter events, 18.0 us)
Async XLA Ops:
  6.5 108.6 %all-gather.3.cloned.1.call-start = ((), (), s32[]{:S(2)}) async-start(), calls=%async_computation.4 | async-start | bytes 9732096 | tf_op jit(solution)/shard_map/all_gather | solution.py:296
  6.5 1.9 %copy-start = (bf16[6144,256]{1,0:T(8,128)(2,1)S(1)}, bf16[6144,256]{1,0:T(8,128)(2,1)}, u32[]{:S(2)}) copy-start(bf16[6144,256]{1,0:T(8,128)(2,1)} %param.16) | copy-start | bytes 9437188
  8.4 11.8 %copy-start.1 = (bf16[1024,256]{1,0:T(8,128)(2,1)S(1)}, bf16[1024,256]{1,0:T(8,128)(2,1)}, u32[]{:S(2)}) copy-start(bf16[1024,256]{1,0:T(8,128)(2,1)} %q.1) | copy-start | bytes 1572868
  8.4 11.8 %copy-start.2 = (bf16[1024,256]{1,0:T(8,128)(2,1)S(1)}, bf16[1024,256]{1,0:T(8,128)(2,1)}, u32[]{:S(2)}) copy-start(bf16[1024,256]{1,0:T(8,128)(2,1)} %k.1) | copy-start | bytes 1572868
  8.4 11.8 %copy-start.8 = (s32[1024]{0:T(1024)S(1)}, s32[1024]{0:T(1024)}, u32[]{:S(2)}) copy-start(s32[1024]{0:T(1024)} %param.14) | copy-start | bytes 12292
  8.4 17.0 %copy-start.17 = (s32[2]{0:T(128)S(1)}, s32[2]{0:T(128)}, u32[]{:S(2)}) copy-start(s32[2]{0:T(128)} %param.15) | copy-start | bytes 28
  20.3 1.0 copy-start.3
  21.3 1.0 copy-start.4
  22.7 54.9 %collective-permute-start.1 = (bf16[512,1024]{1,0:T(8,128)(2,1)S(1)}, bf16[512,1024]{1,0:T(8,128)(2,1)}, u32[]{:S(2)}, u32[]{:S(2)}) collective-permute-start(bf16[512,1024]{1,0:T(8,128)(2,1)S(1)} %get-tuple-element.7.first), channel_id=1, source_target_pairs={{0,1},{1,2},{2,3},{3,0},{4,5},{5,6},{6,7},{7,4},{8,9},{9,10},{10,1... | collective-permute-start | bytes 3145736 | tf_op jit(solution)/shard_map/ppermute | solution.py:233
  23.1 57.3 %collective-permute-start.2 = (bf16[512,1024]{1,0:T(8,128)(2,1)S(1)}, bf16[512,1024]{1,0:T(8,128)(2,1)}, u32[]{:S(2)}, u32[]{:S(2)}) collective-permute-start(bf16[512,1024]{1,0:T(8,128)(2,1)S(1)} %get-tuple-element.7.first), channel_id=1, source_target_pairs={{0,3},{1,0},{2,1},{3,2},{4,7},{5,4},{6,5},{7,6},{8,11},{9,8},{10,9... | collective-permute-start | bytes 3145736 | tf_op jit(solution)/shard_map/ppermute | solution.py:233
  26.4 6.0 %collective-permute-start = (bf16[2,2,128,128]{3,2,1,0:T(8,128)(2,1)S(1)}, bf16[2,2,128,128]{3,2,1,0:T(8,128)(2,1)S(1)}, u32[]{:S(2)}, u32[]{:S(2)}) collective-permute-start(bf16[2,2,128,128]{3,2,1,0:T(8,128)(2,1)S(1)} %pad_maximum_fusion.2), channel_id=1, source_target_pairs={{0,4},{4,0},{8,12},{12,8},{16,20},{20,16},{24,28},{28,24},{32,36},... | collective-permute-start | bytes 393224 | tf_op jit(solution)/shard_map/ppermute | solution.py:256
  33.5 16.2 %all-to-all-start = ((bf16[4,2,2,128,128]{4,3,2,1,0:T(8,128)(2,1)}), bf16[4,2,2,128,128]{4,3,2,1,0:T(8,128)(2,1)S(1)}, u32[]{:S(2)}, u32[]{:S(2)}) async-start(bf16[4,2,2,128,128]{4,3,2,1,0:T(8,128)(2,1)} %broadcast_in_dim.111), calls=%async_computation | async-start | bytes 1048576 | tf_op jit(solution)/shard_map/all_to_all | solution.py:261
  49.8 18.6 %copy-start.6 = (bf16[256,1024]{1,0:T(8,128)(2,1)S(1)}, bf16[256,1024]{1,0:T(8,128)(2,1)}, u32[]{:S(2)}) copy-start(bf16[256,1024]{1,0:T(8,128)(2,1)} %get-tuple-element.21.lower) | copy-start | bytes 1572868
  49.8 18.6 %copy-start.7 = (bf16[256,1024]{1,0:T(8,128)(2,1)S(1)}, bf16[256,1024]{1,0:T(8,128)(2,1)}, u32[]{:S(2)}) copy-start(bf16[256,1024]{1,0:T(8,128)(2,1)} %get-tuple-element.22.upper) | copy-start | bytes 1572868
  53.0 13.3 %all-to-all-start.1 = ((bf16[4,2,128,128]{3,2,1,0:T(8,128)(2,1)}), bf16[4,2,128,128]{3,2,1,0:T(8,128)(2,1)S(1)}, u32[]{:S(2)}, u32[]{:S(2)}) async-start(bf16[4,2,128,128]{3,2,1,0:T(8,128)(2,1)} %select_convert_fusion), calls=%async_computation.1 | async-start | bytes 524288 | tf_op jit(solution)/shard_map/all_to_all | solution.py:275
  71.1 24.4 %collective-permute-start.6 = (bf16[512,768]{1,0:T(8,128)(2,1)}, bf16[512,768]{1,0:T(8,128)(2,1)}, u32[]{:S(2)}, u32[]{:S(2)}) collective-permute-start(bf16[512,768]{1,0:T(8,128)(2,1)} %attend.9.g1), channel_id=1, source_target_pairs={{0,3},{1,0},{2,1},{3,2},{4,7},{5,4},{6,5},{7,6},{8,11},{9,8},{10,9... | collective-permute-start | bytes 2359304 | tf_op jit(solution)/shard_map/ppermute | solution.py:233
  71.7 26.9 %collective-permute-start.5 = (bf16[512,768]{1,0:T(8,128)(2,1)}, bf16[512,768]{1,0:T(8,128)(2,1)}, u32[]{:S(2)}, u32[]{:S(2)}) collective-permute-start(bf16[512,768]{1,0:T(8,128)(2,1)} %attend.9.g1), channel_id=1, source_target_pairs={{0,1},{1,2},{2,3},{3,0},{4,5},{5,6},{6,7},{7,4},{8,9},{9,10},{10,1... | collective-permute-start | bytes 2359304 | tf_op jit(solution)/shard_map/ppermute | solution.py:233
  73.4 21.0 %all-to-all-start.2 = ((bf16[4,528,128]{2,1,0:T(8,128)(2,1)}), bf16[4,528,128]{2,1,0:T(8,128)(2,1)}, u32[]{:S(2)}, u32[]{:S(2)}) async-start(bf16[4,528,128]{2,1,0:T(8,128)(2,1)} %broadcast_in_dim.119), calls=%async_computation.2 | async-start | bytes 1081344 | tf_op jit(solution)/shard_map/all_to_all | solution.py:313
  79.0 27.9 %collective-permute-start.3 = (bf16[256,1024]{1,0:T(8,128)(2,1)S(1)}, bf16[256,1024]{1,0:T(8,128)(2,1)}, u32[]{:S(2)}, u32[]{:S(2)}) collective-permute-start(bf16[256,1024]{1,0:T(8,128)(2,1)S(1)} %get-tuple-element.26.upper), channel_id=1, source_target_pairs={{0,1},{1,2},{2,3},{3,0},{4,5},{5,6},{6,7},{7,4},{8,9},{9,10},{10,1... | collective-permute-start | bytes 1572872 | tf_op jit(solution)/shard_map/ppermute | solution.py:233
  81.6 25.2 %collective-permute-start.4 = (bf16[256,1024]{1,0:T(8,128)(2,1)S(1)}, bf16[256,1024]{1,0:T(8,128)(2,1)}, u32[]{:S(2)}, u32[]{:S(2)}) collective-permute-start(bf16[256,1024]{1,0:T(8,128)(2,1)S(1)} %get-tuple-element.23.lower), channel_id=1, source_target_pairs={{0,3},{1,0},{2,1},{3,2},{4,7},{5,4},{6,5},{7,6},{8,11},{9,8},{10,9... | collective-permute-start | bytes 1572872 | tf_op jit(solution)/shard_map/ppermute | solution.py:233
  83.1 1.0 copy-start.5
  85.9 0.9 copy-start.9
  96.5 17.4 %collective-permute-start.8 = (bf16[256,768]{1,0:T(8,128)(2,1)S(1)}, bf16[256,768]{1,0:T(8,128)(2,1)S(1)}, u32[]{:S(2)}, u32[]{:S(2)}) collective-permute-start(bf16[256,768]{1,0:T(8,128)(2,1)S(1)} %slice.111), channel_id=1, source_target_pairs={{0,3},{1,0},{2,1},{3,2},{4,7},{5,4},{6,5},{7,6},{8,11},{9,8},{10,9... | collective-permute-start | bytes 1179656 | tf_op jit(solution)/shard_map/ppermute | solution.py:233
  99.7 15.4 %collective-permute-start.7 = (bf16[256,768]{1,0:T(8,128)(2,1)S(1)}, bf16[256,768]{1,0:T(8,128)(2,1)S(1)}, u32[]{:S(2)}, u32[]{:S(2)}) collective-permute-start(bf16[256,768]{1,0:T(8,128)(2,1)S(1)} %slice.110), channel_id=1, source_target_pairs={{0,1},{1,2},{2,3},{3,0},{4,5},{5,6},{6,7},{7,4},{8,9},{9,10},{10,1... | collective-permute-start | bytes 1179656 | tf_op jit(solution)/shard_map/ppermute | solution.py:233
  101.6 1.7 %copy-start.11 = (bf16[512,768]{1,0:T(8,128)(2,1)}, bf16[512,768]{1,0:T(8,128)(2,1)S(1)}, u32[]{:S(2)}) copy-start(bf16[512,768]{1,0:T(8,128)(2,1)S(1)} %attend.6.a0) | copy-start | bytes 2359300
  103.3 0.9 copy-start.13
  106.8 8.3 %copy-start.10 = (bf16[512,768]{1,0:T(8,128)(2,1)S(1)}, bf16[512,768]{1,0:T(8,128)(2,1)}, u32[]{:S(2)}) copy-start(bf16[512,768]{1,0:T(8,128)(2,1)} %copy-done.9) | copy-start | bytes 2359300
  106.8 8.3 %copy-start.12 = (bf16[512,768]{1,0:T(8,128)(2,1)S(1)}, bf16[512,768]{1,0:T(8,128)(2,1)}, u32[]{:S(2)}) copy-start(bf16[512,768]{1,0:T(8,128)(2,1)} %copy-done.11) | copy-start | bytes 2359300
  109.8 0.9 copy-start.15
  115.1 1.1 copy-start.14
  116.3 1.1 copy-start.16
Sparse Core Ops, SparseCore 0:
  20.4 62.3 all-gather.2

commit v2 on v0

v2 whole, which is shorter than its diff:
```python
import functools

import jax
import jax.numpy as jnp
from jax import lax
from jax.experimental import pallas as pl
from jax.experimental.pallas import tpu as pltpu
from jax.sharding import PartitionSpec as P

BLK = 256
EARLY = 512
HDIM = 128
bf16 = jnp.bfloat16
f32 = jnp.float32
VMEM_LIMIT = 24 * 1024 * 1024
VMEM_ALL = 62 * 1024 * 1024
LIGHT = pl.CostEstimate(flops=1, bytes_accessed=1, transcendentals=0)

SHARES = 8


def place(z, x, c):
    return (z % 4) * 8 + (x % 4) * 2 + c % 2


def nt(a, b):
    return lax.dot_general(a, b, (((1,), (1,)), ((), ())), preferred_element_type=f32)


def nn(a, b):
    return lax.dot_general(a, b, (((1,), (0,)), ((), ())), preferred_element_type=f32)


def tn(a, b):
    return lax.dot_general(a, b, (((0,), (0,)), ((), ())), preferred_element_type=f32)


def spec(*shape):
    return jax.ShapeDtypeStruct(shape, bf16)


def params():
    return pltpu.CompilerParams(vmem_limit_bytes=VMEM_LIMIT)


def whole(count):
    return [pl.BlockSpec(memory_space=pltpu.VMEM)] * count


def fetch(pairs, sems):
    copies = [pltpu.make_async_copy(source, target, sems.at[i]) for i, (source, target) in enumerate(pairs)]
    for copy in copies:
        copy.start()
    return copies


def begin_kernel(
    q, k, v, g, accepted, decay_code, wq, wk, wv, first, second, codes, local, message, s1, s2, s3, raw_g, keep, sems
):
    width = q.shape[1]
    cut = first.shape[0]
    parts = ((0, cut, first), (cut, second.shape[0], second))
    pairs = [(g, raw_g), (accepted, keep)]
    for part, ref in enumerate((q, k, v)):
        for start, rows, out in parts:
            pairs.append((ref.at[pl.ds(start, rows)], out.at[:, pl.ds(part * width, width)]))
    y = lax.axis_index("head")
    z, x, c = spot()
    piece = c * 4 + jnp.where(c == 0, z, x)
    for out, by in zip((s1, s2, s3), (1, 3, 2)):
        for part, w in enumerate((wq, wk, wv)):
            pairs.append((w.at[lax.rem(y + by, 4), piece], out.at[:, pl.ds(part * width, width)]))
    copies = fetch(pairs, sems)
    line = lax.broadcasted_iota(jnp.int32, codes.shape, 0)
    filled = jnp.zeros(codes.shape, f32)
    for head in range(decay_code.shape[0]):
        filled = jnp.where(line == head, decay_code[head].astype(f32), filled)
    codes[...] = filled.astype(bf16)
    for copy in copies[:2]:
        copy.wait()
    for start, rows, out in parts:
        column = jnp.broadcast_to(keep[0:1, start : start + rows].astype(f32), (HDIM, rows)).T
        wide = jnp.concatenate([column] * (width // HDIM), axis=1)
        out[:, 3 * width :] = (raw_g[start : start + rows].astype(f32) * wide).astype(bf16)
    for copy in copies[2:]:
        copy.wait()
    for head in range(local.shape[2]):
        rate = jnp.exp2(-0.5 * jnp.full((1, HDIM), decay_code[head], f32))
        found, spans = [], []
        for half, (begin_row, end_row) in enumerate(((0, cut), (cut, q.shape[0]))):
            spans.append(jnp.exp(-rate * (end_row - begin_row)))
            kv = qg = jnp.zeros((HDIM, HDIM), f32)
            for start, rows, raw in parts:
                if begin_row <= start < end_row:
                    where = lax.broadcasted_iota(jnp.int32, (rows, HDIM), 0).astype(f32) + (start - begin_row)
                    to_end = jnp.exp(-rate * (end_row - begin_row - 1.0 - where))
                    from_start = jnp.exp(-rate * where)
                    at = lambda part: raw[:, part * width + head * HDIM : part * width + (head + 1) * HDIM]
                    kv += tn((at(1).astype(f32) * to_end).astype(bf16), at(2))
                    qg += tn((at(0).astype(f32) * from_start).astype(bf16), at(3))
            found.append((kv, qg))
            local[half, 0, head] = kv
            local[half, 1, head] = qg
        message[0, head] = (spans[1] * found[0][0] + found[1][0]).astype(bf16)
        message[1, head] = (found[0][1] + spans[0] * found[1][1]).astype(bf16)


def begin(q, k, v, g, accepted, decay_code, weights, early):
    rows, width = q.shape
    out_rows = weights[0].shape[0]
    share = out_rows // (4 * SHARES)
    shaped = [w.reshape(4, SHARES, share, width) for w in weights]
    heads = decay_code.shape[0]
    far = pl.BlockSpec(memory_space=pl.ANY)
    return pl.pallas_call(
        begin_kernel,
        out_shape=[
            spec(early, 4 * width),
            spec(rows - early, 4 * width),
            spec(16, HDIM),
            jax.ShapeDtypeStruct((2, 2, heads, HDIM, HDIM), f32),
            spec(2, heads, HDIM, HDIM),
            *[spec(share, 3 * width)] * 3,
        ],
        in_specs=[far] * 5 + [pl.BlockSpec(memory_space=pltpu.SMEM)] + [far] * 3,
        out_specs=whole(8),
        scratch_shapes=[
            pltpu.VMEM((rows, width), bf16),
            pltpu.VMEM((1, rows), jnp.int32),
            pltpu.SemaphoreType.DMA((17,)),
        ],
        compiler_params=pltpu.CompilerParams(vmem_limit_bytes=VMEM_ALL),
        cost_estimate=LIGHT,
        name="begin",
    )(q, k, v, g, accepted.reshape(1, rows), decay_code, *shaped)


def spot():
    seq = lax.axis_index("seq")
    return lax.div(seq, 8), lax.rem(lax.div(seq, 2), 4), lax.rem(seq, 2)


def fade(codes, head, span, count):
    rate = jnp.exp2(-0.5 * codes[head : head + 1, :].astype(f32))
    faded = jnp.exp(-rate * (span * jnp.maximum(count, 0).astype(f32)))
    return jnp.where(count >= 0, faded, 0.0)


def join_kernel(rows, codes_at, mine_at, other_at, out, codes, mine, other, sems):
    z, x, c = spot()
    late = c == 1
    chip = z * 4 + x
    for copy in fetch([(codes_at, codes), (mine_at, mine), (other_at, other)], sems):
        copy.wait()
    for head in range(mine.shape[1]):
        one = fade(codes, head, rows, jnp.int32(1))
        near, far = mine[:, head].astype(f32), other[:, head].astype(f32)
        before, after = jnp.where(late, far, near), jnp.where(late, near, far)
        kv = (one * before[0] + after[0]).astype(bf16)
        qg = (before[1] + one * after[1]).astype(bf16)
        for to in range(out.shape[0]):
            out[to, head] = jnp.where(to > chip, kv, qg)


def join(rows, codes, mine, other):
    return pl.pallas_call(
        functools.partial(join_kernel, rows),
        out_shape=spec(16, *mine.shape[1:]),
        in_specs=[pl.BlockSpec(memory_space=pl.ANY)] * 3,
        out_specs=pl.BlockSpec(memory_space=pltpu.VMEM),
        scratch_shapes=[
            pltpu.VMEM(codes.shape, bf16),
            pltpu.VMEM(mine.shape, bf16),
            pltpu.VMEM(other.shape, bf16),
            pltpu.SemaphoreType.DMA((3,)),
        ],
        compiler_params=pltpu.CompilerParams(vmem_limit_bytes=VMEM_ALL),
        cost_estimate=LIGHT,
        name="join",
    )(codes, mine, other)


def enter_kernel(early, rows, codes, arrived, other, local, state0, state1):
    z, x, c = spot()
    late = c == 1
    chip = z * 4 + x
    heads = arrived.shape[1]
    width = heads * HDIM
    for head in range(heads):
        kv = qg = jnp.zeros((HDIM, HDIM), f32)
        for there in range(arrived.shape[0]):
            it = arrived[there, head].astype(f32)
            kv += it * fade(codes, head, 2 * rows, chip - 1 - there)
            qg += it * fade(codes, head, 2 * rows, there - chip - 1)
        one = fade(codes, head, rows, jnp.int32(1))
        start = fade(codes, head, early, jnp.int32(1))
        end = fade(codes, head, rows - early, jnp.int32(1))
        kv = jnp.where(late, one * kv + other[0, head].astype(f32), kv)
        qg = jnp.where(late, qg, one * qg + other[1, head].astype(f32))
        here = pl.ds(head * HDIM, HDIM)
        there = pl.ds(width + head * HDIM, HDIM)
        state0[here] = kv.astype(bf16)
        state0[there] = (end * qg + local[1, 1, head]).astype(bf16)
        state1[here] = (start * kv + local[0, 0, head]).astype(bf16)
        state1[there] = qg.astype(bf16)
    state0[2 * width :] = codes[...]
    state1[2 * width :] = codes[...]


def small(kernel, rows, operands, outs, name):
    return pl.pallas_call(
        functools.partial(kernel, rows),
        out_shape=outs,
        in_specs=whole(len(operands)),
        out_specs=whole(len(outs)),
        compiler_params=params(),
        cost_estimate=LIGHT,
        name=name,
    )(*operands)


def attend_rows(raws, state, out):
    heads = (state.shape[0] - 16) // (2 * HDIM)
    width = heads * HDIM
    rows = out.shape[0]
    starts = list(range(0, rows, BLK))
    sizes = [min(BLK, rows - start) for start in starts]
    count = len(starts)
    edges = [0]
    for raw in raws:
        edges.append(edges[-1] + raw.shape[0])

    def take(block, part, head):
        low, high = starts[block], starts[block] + sizes[block]
        here = slice(part * width + head * HDIM, part * width + (head + 1) * HDIM)
        found = []
        for raw, start, end in zip(raws, edges, edges[1:]):
            if max(low, start) < min(high, end):
                found.append(raw[max(low, start) - start : min(high, end) - start, here])
        return found[0] if len(found) == 1 else jnp.concatenate(found, axis=0)

    def table(rate1, later, earlier, flip):
        shape = (sizes[earlier], sizes[later]) if flip else (sizes[later], sizes[earlier])
        row = lax.broadcasted_iota(jnp.int32, shape, 0)
        col = lax.broadcasted_iota(jnp.int32, shape, 1)
        rate = rate1 if shape[1] == HDIM else jnp.concatenate([rate1] * (shape[1] // HDIM), axis=1)
        gap = (col - row if flip else row - col).astype(f32)
        if later == earlier:
            return jnp.where(gap >= 0, jnp.exp(-rate * jnp.maximum(gap, 0.0)), 0.0)
        return jnp.exp(-rate * (starts[later] - starts[earlier] + gap))

    cut = lambda a, d: (a * d).astype(bf16)
    for head in range(heads):
        code = state[2 * width + head : 2 * width + head + 1, :].astype(f32)
        rate = jnp.exp2(-0.5 * code)
        made = {}

        def decay(later, earlier, flip):
            key = (starts[later] - starts[earlier], sizes[later], sizes[earlier], flip)
            if key not in made:
                made[key] = table(rate, later, earlier, flip)
            return made[key]

        q, k, v, g = ([take(block, part, head) for block in range(count)] for part in range(4))
        kv = state[head * HDIM : (head + 1) * HDIM, :]
        qg = state[width + head * HDIM : width + (head + 1) * HDIM, :]
        for block in range(count):
            start, size = starts[block], sizes[block]
            where = lax.broadcasted_iota(jnp.int32, (size, HDIM), 0).astype(f32) + start
            lag = jnp.exp(-rate * (rows - where))
            dq = jnp.exp(-rate * (where + 1.0)) * nt(g[block], kv)
            dk = lag * nt(v[block], qg)
            dv = lag * nn(k[block], qg)
            for other in range(block + 1):
                dq += nn(cut(nt(g[block], v[other]), decay(block, other, False)), k[other])
            for other in range(block, count):
                dk += nn(cut(nt(v[block], g[other]), decay(other, block, True)), q[other])
                dv += nn(cut(nt(k[block], q[other]), decay(other, block, True)), g[other])
            for part, value in enumerate((dq, dk, dv)):
                here = pl.ds(part * width + head * HDIM, HDIM)
                out[start : start + size, here] = value.astype(bf16)


def attend_both(first, second, state0, state1, upper, lower):
    attend_rows([first], state0, upper)
    attend_rows([second], state1, lower)


def attend(first, second, state0, state1):
    depth = first.shape[1] // 4 * 3
    return pl.pallas_call(
        attend_both,
        out_shape=[spec(first.shape[0], depth), spec(second.shape[0], depth)],
        in_specs=whole(4),
        out_specs=whole(2),
        compiler_params=params(),
        cost_estimate=LIGHT,
        name="attend",
    )(first, second, state0, state1)


OWN_STEPS = 4


def own_kernel(upper, lower, wq, wk, wv, out, w, sems):
    y = lax.axis_index("head")
    cols, width = w.shape[1:]
    part = cols // OWN_STEPS
    pairs = []
    for step in range(OWN_STEPS):
        begins = pl.multiple_of(y * cols + step * part, part)
        pairs += [(ref.at[pl.ds(begins, part)], w.at[i, pl.ds(step * part, part)]) for i, ref in enumerate((wq, wk, wv))]
    copies = fetch(pairs, sems)
    cut = upper.shape[0]
    for step in range(OWN_STEPS):
        for copy in copies[3 * step : 3 * step + 3]:
            copy.wait()
        here = slice(step * part, (step + 1) * part)
        for rows, ref in ((slice(0, cut), upper), (slice(cut, None), lower)):
            total = None
            for i in range(3):
                term = nt(ref[:, i * width : (i + 1) * width], w[i, here])
                total = term if total is None else total + term
            out[rows, here] = total.astype(bf16)


def project_own(upper, lower, weights):
    rows = upper.shape[0] + lower.shape[0]
    cols, width = weights[0].shape[0] // 4, weights[0].shape[1]
    return pl.pallas_call(
        own_kernel,
        out_shape=spec(rows, cols),
        in_specs=whole(2) + [pl.BlockSpec(memory_space=pl.ANY)] * 3,
        out_specs=pl.BlockSpec(memory_space=pltpu.VMEM),
        scratch_shapes=[pltpu.VMEM((3, cols, width), bf16), pltpu.SemaphoreType.DMA((3 * OWN_STEPS,))],
        compiler_params=params(),
        cost_estimate=LIGHT,
        name="project_own",
    )(upper, lower, *weights)


def others_kernel(srcs, cores, last, *refs):
    refs = list(refs)
    take = lambda count: [refs.pop(0) for _ in range(count)]
    parts = [take(2) for _ in srcs]
    tables = take(len(cores))
    partial, out, w = take(3)
    z, x, c = spot()
    pieces, _, share, depth = tables[0].shape
    half = pieces * share
    tile = w.shape[1]
    made = []
    for table, mirrored in zip(tables, cores):
        core = 1 - c if mirrored else c
        outer = jnp.where(core == 0, z, x)
        for step in range(half // tile):
            at = pl.ds(pl.multiple_of(core * half + step * tile, tile), tile)
            for piece in range(tile // share):
                source = lax.rem(outer + 4 - (step * (tile // share) + piece), 4)
                for i, src in enumerate(srcs):
                    w[i, piece * share : (piece + 1) * share] = table[source, src - 1]
            start = 0
            for chunk in range(2):
                size = parts[0][chunk].shape[0]
                total = partial[start : start + size, at].astype(f32)
                for i in range(len(srcs)):
                    total = total + nt(parts[i][chunk][...], w[i])
                if last:
                    tiles, sems = refs
                    slot = len(made)
                    tiles[slot] = total.astype(bf16)
                    target = out.at[pl.ds(start, size), at]
                    made.append(pltpu.make_async_copy(tiles.at[slot], target, sems.at[slot]))
                    made[-1].start()
                else:
                    out[start : start + size, at] = total.astype(bf16)
                start += size
    for copy in made:
        copy.wait()


def project_others(srcs, parts, tables, mirrored, partial, last=False):
    rows, cols = partial.shape
    pieces, _, share, depth = tables[0].shape
    tile = 2 * share
    count = 2 * len(tables) * pieces * share // tile
    operands = [*sum(parts, []), *tables, partial]
    scratch = [pltpu.VMEM((len(srcs), tile, depth), bf16)]
    if last:
        scratch += [pltpu.VMEM((count, rows // 2, tile), bf16), pltpu.SemaphoreType.DMA((count,))]
    return pl.pallas_call(
        functools.partial(others_kernel, srcs, mirrored, last),
        out_shape=spec(rows, cols),
        in_specs=whole(len(operands)),
        out_specs=pl.BlockSpec(memory_space=pl.ANY if last else pltpu.VMEM),
        scratch_shapes=scratch,
        input_output_aliases={} if last else {len(operands) - 1: 0},
        compiler_params=params(),
        cost_estimate=LIGHT,
        name="project_others",
    )(*operands)


def turn(a, by):
    return lax.ppermute(a, "head", [(i, (i + by) % 4) for i in range(4)])


def move(a, where):
    pairs = [(place(z, x, c), place(*where(z, x, c))) for z in range(4) for x in range(4) for c in range(2)]
    return lax.ppermute(a, "seq", pairs)


def across(a):
    return move(a, lambda z, x, c: (z, x, 1 - c))


CHIPS = [[place(z, x, c) for z in range(4) for x in range(4)] for c in range(2)]
def major(a, by):
    return move(a, lambda z, x, c: (z + by, x, c) if c == 0 else (z, x + by, c))


def tie(*groups):
    return lax.optimization_barrier(groups)


def shards(queries, key_rows, value_rows, grad_out, accepted, decay_code, w_query, w_key, w_value):
    heads = decay_code.shape[0]
    count = queries.shape[0]
    rows = float(count)
    weights = (w_query, w_key, w_value)
    first, second, codes, local, message, *sent = begin(
        queries, key_rows, value_rows, grad_out, accepted, decay_code, weights, EARLY
    )
    other = across(message)
    leaving = join(rows, codes, message, other)
    share = jnp.stack([turn(sent[0], 1), turn(sent[1], -1), turn(sent[2], 2)])
    arrived = lax.all_to_all(leaving, "seq", 0, 0, axis_index_groups=CHIPS)
    share, _ = tie(share, leaving)
    half = [share] + [major(share, by) for by in (1, 2, 3)]
    state0, state1 = small(
        functools.partial(enter_kernel, float(EARLY)),
        rows,
        (codes, arrived, other, local),
        [spec(2 * heads * HDIM + 16, HDIM)] * 2,
        "enter",
    )
    upper, lower = attend(first, second, state0, state1)
    upper_left, lower_right = turn(upper, 1), turn(lower, -1)
    lower_left, upper_right = turn(lower, 1), turn(upper, -1)
    upper_far, lower_far = turn(upper_left, 1), turn(lower_right, -1)
    half, _, _ = tie(half, upper_left, lower_right)
    half = jnp.stack(half)
    other_half = across(half)
    total = project_own(upper, lower, weights)
    sides = [upper_left, lower_left], [upper_right, lower_right]
    total = project_others((1, 2), sides, (half,), (False,), total)
    total = project_others((1, 2), sides, (other_half,), (True,), total)
    return project_others((3,), ([upper_far, lower_far],), (half, other_half), (False, True), total, True)


def solution(mesh):
    in_specs = (P("seq", "head"),) * 4 + (P("seq"), P("head")) + (P(None, "head"),) * 3
    return jax.shard_map(shards, mesh=mesh, in_specs=in_specs, out_specs=P("seq", "head"), check_vma=False)
```

time: 400 us -> 111 us (0.28)
  matrix products: 107 us -> 0 us
  waiting for transfers between devices: 116 us -> 45.8 us
  blocking collectives: 65.1 us -> 0 us
  local copies, waits for them, and re-layouts: 53.9 us -> 1.9 us
  other arithmetic: 39.5 us -> 3.36 us
  Pallas kernels: 0 us -> 30 us
  starting transfers between devices: 0.09 us -> 29.4 us
  between operations: 13.9 us -> 0.31 us
    reduce_scatter x1 -> x0, waiting for transfers between devices: 116 us -> none  [shards(): lax.psum_scatter((contract_rows(w_query, query_gradient) + contract_rows(...]
    dot_general x49 -> x0, matrix products: 107 us -> none  [the longest x3 42.3 us: contract_rows(): lax.dot_general(weight_rows, grads, (((1,), (1,)), ((), ())), preferred_e...]
    unnamed x1 -> x0, blocking collectives: 65.1 us -> none
    ppermute x0 -> x14, waiting for transfers between devices: none -> 45.8 us  [the longest x9 31.6 us: turn(): return lax.ppermute(a, 'head', [(i, (i + by) % 4) for i in range(4)])]
    add x32 -> x0, other arithmetic: 30.7 us -> none  [the longest x31 30.7 us: combine_states(): earlier[1] * later[0][:, None, None] + later[1]]
    pallas_call x0 -> x8, Pallas kernels: none -> 30 us  [the longest x3 11.8 us: project_others(): pl.pallas_call(functools.partial(others_kernel, srcs, mirrored, last), ou...]
    ppermute x0 -> x14, starting transfers between devices: none -> 21.6 us  [the longest x9 12.6 us: turn(): return lax.ppermute(a, 'head', [(i, (i + by) % 4) for i in range(4)])]
    mul x31 -> x0, local copies, waits for them, and re-layouts: 21.3 us -> none  [combine_states(): earlier[1] * later[0][:, None, None] + later[1]]
  transfers between devices with their start and end apart: 3 -> 15, of which waited for: 1 -> 8; matrix products, arithmetic and copies ran while one was open for 12% -> 1% of each run, Pallas kernels for 0% -> 17%
where the time goes in v2:
time: 111 us
  waiting for transfers between devices  45.8 us (41%)
  Pallas kernels  30 us (27%)
  starting transfers between devices  29.4 us (26%)
  other arithmetic  3.36 us (3%)
  local copies, waits for them, and re-layouts  1.9 us (2%)
    ppermute x9, waiting for transfers between devices, turn(): return lax.ppermute(a, 'head', [(i, (i + by) % 4) for i in range(4)])  31.6 us
    ppermute x5, waiting for transfers between devices, move(): return lax.ppermute(a, 'seq', pairs)  14.2 us
    ppermute x9, starting transfers between devices, turn(): return lax.ppermute(a, 'head', [(i, (i + by) % 4) for i in range(4)])  12.6 us
    pallas_call x3, Pallas kernels, project_others(): pl.pallas_call(functools.partial(others_kernel, srcs, mirrored, last), ou...  11.8 us
    ppermute x5, starting transfers between devices, move(): return lax.ppermute(a, 'seq', pairs)  9.02 us
    all_to_all x1, starting transfers between devices, shards(): arrived = lax.all_to_all(leaving, 'seq', 0, 0, axis_index_groups=CHIPS)  7.82 us
    pallas_call x1, Pallas kernels, project_own(): pl.pallas_call(own_kernel, out_shape=spec(rows, cols), in_specs=whole(2)...  7.18 us
    pallas_call x1, Pallas kernels, begin(): pl.pallas_call(begin_kernel, out_shape=[spec(early, 4 * width), spec(rows...  4.42 us
  transfers between devices with their start and end apart: 15, of which 8 were waited for; matrix products, arithmetic and copies ran while one was open for 1% of the time, Pallas kernels for 17%

profile of v2, /device:TPU:1, one launch (start us, length us, event | category | flops | bytes accessed | tf_op | source)
XLA Modules:
  0.0 110.8 jit_solution(9245802808045815419)
XLA Ops:
  0.0 4.4 %begin.1 = (bf16[512,1024]{1,0:T(8,128)(2,1)}, bf16[512,1024]{1,0:T(8,128)(2,1)}, bf16[16,128]{1,0:T(8,128)(2,1)}, f32[2,2,2,128,128]{4,3,2,1,0:T(8,128)}, bf16[...) custom-call(bf16[1024,256]{1,0:T(8,128)(2,1)} %q.1, ...), custom_call_target="tpu_custom_call" | custom-call | flops 1 | bytes 1 | tf_op jit(solution)/shard_map/begin/pallas_call | solution.py:115
  4.5 1.5 %collective-permute-start = (bf16[2,2,128,128]{3,2,1,0:T(8,128)(2,1)}, bf16[2,2,128,128]{3,2,1,0:T(8,128)(2,1)S(1)}, u32[]{:S(2)}, u32[]{:S(2)}) collective-permute-start(bf16[2,2,128,128]{3,2,1,0:T(8,128)(2,1)} %get-tuple-element.25.mine_at), channel_id=1, source_target_pairs={{0,4},{4,0},{8,12},{12,8},{16,20},{20,16},{24,28},{28,24},{32,36},... | collective-permute-start | bytes 393224 | tf_op jit(solution)/shard_map/ppermute | solution.py:410
  6.0 1.2 %collective-permute-done.other_at.other = bf16[2,2,128,128]{3,2,1,0:T(8,128)(2,1)S(1)} collective-permute-done((bf16[2,2,128,128]{3,2,1,0:T(8,128)(2,1)}, bf16[2,2,128,128]{3,2,1,0:T(8,128)(2,1)S(1)}, u32[]{:S(2)}, u32[]{:S(2)}) %collective-permute-start) | collective-permute-done | bytes 131104 | tf_op jit(solution)/shard_map/ppermute | solution.py:410
  7.2 0.7 copy-done.6
  7.8 2.1 %join.1 = bf16[16,2,128,128]{3,2,1,0:T(8,128)(2,1)} custom-call(bf16[16,128]{1,0:T(8,128)(2,1)} %get-tuple-element.24.codes_at.codes, bf16[2,2,128,128]{3,2,1,0:T(8,128)(2,1)} %get-tuple-element.25.mine_at, bf16[2,2,128,128]{3,2,1,0:T(8,128)(2,1)} %copy-done.6), custom_call_target="tpu_custom_call" | custom-call | flops 1 | bytes 1 | tf_op jit(solution)/shard_map/join/pallas_call | solution.py:166
  10.0 7.8 %all-to-all-start = ((bf16[16,2,128,128]{3,2,1,0:T(8,128)(2,1)}), bf16[16,2,128,128]{3,2,1,0:T(8,128)(2,1)S(1)}, u32[]{:S(2)}, u32[]{:S(2)}) async-start(bf16[16,2,128,128]{3,2,1,0:T(8,128)(2,1)} %join.1), calls=%async_computation | async-start | bytes 2097152 | tf_op jit(solution)/shard_map/all_to_all | solution.py:437
  17.8 1.4 %collective-permute-start.5 = (bf16[192,768]{1,0:T(8,128)(2,1)}, bf16[192,768]{1,0:T(8,128)(2,1)S(1)}, u32[]{:S(2)}, u32[]{:S(2)}) collective-permute-start(bf16[192,768]{1,0:T(8,128)(2,1)} %get-tuple-element.31), channel_id=1, source_target_pairs={{0,1},{1,2},{2,3},{3,0},{4,5},{5,6},{6,7},{7,4},{8,9},{9,10},{10,1... | collective-permute-start | bytes 884744 | tf_op jit(solution)/shard_map/ppermute | solution.py:405
  19.2 1.5 %collective-permute-start.6 = (bf16[192,768]{1,0:T(8,128)(2,1)}, bf16[192,768]{1,0:T(8,128)(2,1)S(1)}, u32[]{:S(2)}, u32[]{:S(2)}) collective-permute-start(bf16[192,768]{1,0:T(8,128)(2,1)} %get-tuple-element.32), channel_id=1, source_target_pairs={{0,3},{1,0},{2,1},{3,2},{4,7},{5,4},{6,5},{7,6},{8,11},{9,8},{10,9... | collective-permute-start | bytes 884744 | tf_op jit(solution)/shard_map/ppermute | solution.py:405
  20.7 1.6 %collective-permute-start.7 = (bf16[192,768]{1,0:T(8,128)(2,1)}, bf16[192,768]{1,0:T(8,128)(2,1)S(1)}, u32[]{:S(2)}, u32[]{:S(2)}) collective-permute-start(bf16[192,768]{1,0:T(8,128)(2,1)} %get-tuple-element.33), channel_id=1, source_target_pairs={{0,2},{1,3},{2,0},{3,1},{4,6},{5,7},{6,4},{7,5},{8,10},{9,11},{10,... | collective-permute-start | bytes 884744 | tf_op jit(solution)/shard_map/ppermute | solution.py:405
  22.3 5.1 %collective-permute-done.5 = bf16[192,768]{1,0:T(8,128)(2,1)S(1)} collective-permute-done((bf16[192,768]{1,0:T(8,128)(2,1)}, bf16[192,768]{1,0:T(8,128)(2,1)S(1)}, u32[]{:S(2)}, u32[]{:S(2)}) %collective-permute-start.5) | collective-permute-done | bytes 294944 | tf_op jit(solution)/shard_map/ppermute | solution.py:405
  27.3 7.4 %collective-permute-done.7 = bf16[192,768]{1,0:T(8,128)(2,1)S(1)} collective-permute-done((bf16[192,768]{1,0:T(8,128)(2,1)}, bf16[192,768]{1,0:T(8,128)(2,1)S(1)}, u32[]{:S(2)}, u32[]{:S(2)}) %collective-permute-start.7) | collective-permute-done | bytes 294944 | tf_op jit(solution)/shard_map/ppermute | solution.py:405
  34.8 1.0 pad_maximum_fusion.1
  35.8 2.2 %collective-permute-start.10 = (bf16[3,192,768]{2,1,0:T(8,128)(2,1)}, bf16[3,192,768]{2,1,0:T(8,128)(2,1)}, u32[]{:S(2)}, u32[]{:S(2)}) collective-permute-start(bf16[3,192,768]{2,1,0:T(8,128)(2,1)} %pad_maximum_fusion.1), channel_id=1, source_target_pairs={{0,96},{4,28},{8,104},{12,4},{16,112},{20,12},{24,120},{28,20},{32... | collective-permute-start | bytes 2654216 | tf_op jit(solution)/shard_map/ppermute | solution.py:410
  38.0 1.8 %collective-permute-start.9 = (bf16[3,192,768]{2,1,0:T(8,128)(2,1)}, bf16[3,192,768]{2,1,0:T(8,128)(2,1)}, u32[]{:S(2)}, u32[]{:S(2)}) collective-permute-start(bf16[3,192,768]{2,1,0:T(8,128)(2,1)} %pad_maximum_fusion.1), channel_id=1, source_target_pairs={{0,64},{4,20},{8,72},{12,28},{16,80},{20,4},{24,88},{28,12},{32,96... | collective-permute-start | bytes 2654216 | tf_op jit(solution)/shard_map/ppermute | solution.py:410
  39.8 0.5 enter.1
  40.3 1.2 %copy-done.4 = bf16[512,1024]{1,0:T(8,128)(2,1)S(1)} copy-done((bf16[512,1024]{1,0:T(8,128)(2,1)S(1)}, bf16[512,1024]{1,0:T(8,128)(2,1)}, u32[]{:S(2)}) %copy-start.4) | copy-done | bytes 1048600
  41.5 3.9 %attend.1 = (bf16[512,768]{1,0:T(8,128)(2,1)S(1)}, bf16[512,768]{1,0:T(8,128)(2,1)S(1)}) custom-call(bf16[512,1024]{1,0:T(8,128)(2,1)S(1)} %copy-done.3, bf16[512,1024]{1,0:T(8,128)(2,1)S(1)} %copy-done.4, bf16[528,128]{1,0:T(8,128)(2,1)S(1)} %get-tuple-element.27.state0, bf16[528,128]{1,0:T(8,128)(2,1)S(1)} %get-tuple-element.28.state1), custom_call_target="tpu_custom_call" | custom-call | flops 1 | bytes 1 | tf_op jit(solution)/shard_map/attend/pallas_call | solution.py:291
  45.5 0.6 collective-permute-start.1
  46.1 2.1 %collective-permute-start.3 = (bf16[512,768]{1,0:T(8,128)(2,1)S(1)}, bf16[512,768]{1,0:T(8,128)(2,1)S(1)}, u32[]{:S(2)}, u32[]{:S(2)}) collective-permute-start(bf16[512,768]{1,0:T(8,128)(2,1)S(1)} %get-tuple-element.30.lower), channel_id=1, source_target_pairs={{0,3},{1,0},{2,1},{3,2},{4,7},{5,4},{6,5},{7,6},{8,11},{9,8},{10,9... | collective-permute-start | bytes 2359304 | tf_op jit(solution)/shard_map/ppermute | solution.py:405
  48.2 9.6 %collective-permute-done.10 = bf16[3,192,768]{2,1,0:T(8,128)(2,1)} collective-permute-done((bf16[3,192,768]{2,1,0:T(8,128)(2,1)}, bf16[3,192,768]{2,1,0:T(8,128)(2,1)}, u32[]{:S(2)}, u32[]{:S(2)}) %collective-permute-start.10) | collective-permute-done | bytes 884768 | tf_op jit(solution)/shard_map/ppermute | solution.py:410
  57.8 3.4 %collective-permute-done.8 = bf16[3,192,768]{2,1,0:T(8,128)(2,1)} collective-permute-done((bf16[3,192,768]{2,1,0:T(8,128)(2,1)}, bf16[3,192,768]{2,1,0:T(8,128)(2,1)}, u32[]{:S(2)}, u32[]{:S(2)}) %collective-permute-start.8) | collective-permute-done | bytes 884768 | tf_op jit(solution)/shard_map/ppermute | solution.py:410
  61.2 2.0 %collective-permute-done.1.refs_0_ = bf16[512,768]{1,0:T(8,128)(2,1)S(1)} collective-permute-done((bf16[512,768]{1,0:T(8,128)(2,1)S(1)}, bf16[512,768]{1,0:T(8,128)(2,1)S(1)}, u32[]{:S(2)}, u32[]{:S(2)}) %collective-permute-start.1) | collective-permute-done | bytes 786464 | tf_op jit(solution)/shard_map/ppermute | solution.py:405
  63.2 2.4 %pad_maximum_fusion.refs_4_.refs_2_ = bf16[4,3,192,768]{3,2,1,0:T(8,128)(2,1)S(1)} fusion(bf16[1,3,192,768]{3,2,1,0:T(8,128)(2,1)} %bitcast.10, bf16[1,3,192,768]{3,2,1,0:T(8,128)(2,1)} %bitcast.9, bf16[1,3,192,768]{3,2,1,0:T(8,128)(2,1)} %bitcast.8, bf16[1,3,192,768]{3,2,1,0:T(8,128)(2,1)} %bitcast.7), kind=kLoop, calls=%fused_computation | loop fusion | flops 5308416 | bytes 7077888 | tf_op jit(solution)/shard_map/stack | solution.py:452
  65.6 3.6 %collective-permute-start.11 = (bf16[4,3,192,768]{3,2,1,0:T(8,128)(2,1)S(1)}, bf16[4,3,192,768]{3,2,1,0:T(8,128)(2,1)S(1)}, u32[]{:S(2)}, u32[]{:S(2)}) collective-permute-start(bf16[4,3,192,768]{3,2,1,0:T(8,128)(2,1)S(1)} %pad_maximum_fusion.refs_4_.refs_2_), channel_id=1, source_target_pairs={{0,4},{4,0},{8,12},{12,8},{16,20},{20,16},{24,28},{28,24},{32,36},... | collective-permute-start | bytes 10616840 | tf_op jit(solution)/shard_map/ppermute | solution.py:410
  69.2 2.7 %collective-permute-start.13 = (bf16[512,768]{1,0:T(8,128)(2,1)S(1)}, bf16[512,768]{1,0:T(8,128)(2,1)S(1)}, u32[]{:S(2)}, u32[]{:S(2)}) collective-permute-start(bf16[512,768]{1,0:T(8,128)(2,1)S(1)} %get-tuple-element.29.upper), channel_id=1, source_target_pairs={{0,3},{1,0},{2,1},{3,2},{4,7},{5,4},{6,5},{7,6},{8,11},{9,8},{10,9... | collective-permute-start | bytes 2359304 | tf_op jit(solution)/shard_map/ppermute | solution.py:405
  71.9 2.7 %collective-permute-start.4 = (bf16[512,768]{1,0:T(8,128)(2,1)S(1)}, bf16[512,768]{1,0:T(8,128)(2,1)S(1)}, u32[]{:S(2)}, u32[]{:S(2)}) collective-permute-start(bf16[512,768]{1,0:T(8,128)(2,1)S(1)} %collective-permute-done.3.refs_3_), channel_id=1, source_target_pairs={{0,3},{1,0},{2,1},{3,2},{4,7},{5,4},{6,5},{7,6},{8,11},{9,8},{10,9... | collective-permute-start | bytes 2359304 | tf_op jit(solution)/shard_map/ppermute | solution.py:405
  74.5 7.2 %project_own.1.refs_5_ = bf16[1024,1536]{1,0:T(8,128)(2,1)S(1)} custom-call(bf16[512,768]{1,0:T(8,128)(2,1)S(1)} %get-tuple-element.29.upper, bf16[512,768]{1,0:T(8,128)(2,1)S(1)} %get-tuple-element.30.lower, bf16[6144,256]{1,0:T(8,128)(2,1)S(1)} %copy-done, bf16[6144,256]{1,0:T(8,128)(2,1)S(1)} %copy-done.1, bf16[6144,256]{1,0:T(8,128)(2,1)S(1)} %copy-done.2), custom_call_target="tpu_custom_call" | custom-call | flops 1 | bytes 1 | tf_op jit(solution)/shard_map/project_own/pallas_call | solution.py:330
  81.7 7.8 %collective-permute-done.12.refs_1_ = bf16[512,768]{1,0:T(8,128)(2,1)S(1)} collective-permute-done((bf16[512,768]{1,0:T(8,128)(2,1)S(1)}, bf16[512,768]{1,0:T(8,128)(2,1)S(1)}, u32[]{:S(2)}, u32[]{:S(2)}) %collective-permute-start.12) | collective-permute-done | bytes 786464 | tf_op jit(solution)/shard_map/ppermute | solution.py:405
  89.5 3.7 %project_others.3.refs_5_ = bf16[1024,1536]{1,0:T(8,128)(2,1)S(1)} custom-call(bf16[512,768]{1,0:T(8,128)(2,1)S(1)} %collective-permute-done.1.refs_0_, bf16[512,768]{1,0:T(8,128)(2,1)S(1)} %collective-permute-done.12.refs_1_, bf16[512,768]{1,0:T(8,128)(2,1)S(1)} %collective-permute-done.13.refs_2_, ...), custom_call_target="tpu_custom_call", output_to_operand_aliasing={{}: (5, {})} | custom-call | flops 1 | bytes 1 | tf_op jit(solution)/shard_map/project_others/pallas_call | solution.py:391
  93.3 3.8 %project_others.4.refs_4_ = bf16[1024,1536]{1,0:T(8,128)(2,1)S(1)} custom-call(bf16[512,768]{1,0:T(8,128)(2,1)S(1)} %collective-permute-done.1.refs_0_, bf16[512,768]{1,0:T(8,128)(2,1)S(1)} %collective-permute-done.12.refs_1_, bf16[512,768]{1,0:T(8,128)(2,1)S(1)} %collective-permute-done.13.refs_2_, ...), custom_call_target="tpu_custom_call", output_to_operand_aliasing={{}: (5, {})} | custom-call | flops 1 | bytes 1 | tf_op jit(solution)/shard_map/project_others/pallas_call | solution.py:391
  97.0 9.3 %collective-permute-done.2.refs_0_ = bf16[512,768]{1,0:T(8,128)(2,1)S(1)} collective-permute-done((bf16[512,768]{1,0:T(8,128)(2,1)S(1)}, bf16[512,768]{1,0:T(8,128)(2,1)S(1)}, u32[]{:S(2)}, u32[]{:S(2)}) %collective-permute-start.2) | collective-permute-done | bytes 786464 | tf_op jit(solution)/shard_map/ppermute | solution.py:405
  106.3 4.3 %project_others.5 = bf16[1024,1536]{1,0:T(8,128)(2,1)} custom-call(bf16[512,768]{1,0:T(8,128)(2,1)S(1)} %collective-permute-done.2.refs_0_, bf16[512,768]{1,0:T(8,128)(2,1)S(1)} %collective-permute-done.4.refs_1_, bf16[4,3,192,768]{3,2,1,0:T(8,128)(2,1)S(1)} %pad_maximum_fusion.refs_4_.refs_2_, ...), custom_call_target="tpu_custom_call" | custom-call | flops 1 | bytes 1 | tf_op jit(solution)/shard_map/project_others/pallas_call | solution.py:391
  (26 shorter events, 0.1 us)
Async XLA Ops:
  4.4 35.3 %copy-start.5 = (f32[2,2,2,128,128]{4,3,2,1,0:T(8,128)S(1)}, f32[2,2,2,128,128]{4,3,2,1,0:T(8,128)}, u32[]{:S(2)}) copy-start(f32[2,2,2,128,128]{4,3,2,1,0:T(8,128)} %get-tuple-element.26.local) | copy-start | bytes 1572868
  4.4 35.3 %copy-start.8 = (bf16[16,128]{1,0:T(8,128)(2,1)S(1)}, bf16[16,128]{1,0:T(8,128)(2,1)}, u32[]{:S(2)}) copy-start(bf16[16,128]{1,0:T(8,128)(2,1)} %get-tuple-element.24.codes_at.codes) | copy-start | bytes 12292
  4.5 35.9 %copy-start.3 = (bf16[512,1024]{1,0:T(8,128)(2,1)S(1)}, bf16[512,1024]{1,0:T(8,128)(2,1)}, u32[]{:S(2)}) copy-start(bf16[512,1024]{1,0:T(8,128)(2,1)} %get-tuple-element.22.first) | copy-start | bytes 3145732
  4.5 2.7 %collective-permute-start = (bf16[2,2,128,128]{3,2,1,0:T(8,128)(2,1)}, bf16[2,2,128,128]{3,2,1,0:T(8,128)(2,1)S(1)}, u32[]{:S(2)}, u32[]{:S(2)}) collective-permute-start(bf16[2,2,128,128]{3,2,1,0:T(8,128)(2,1)} %get-tuple-element.25.mine_at), channel_id=1, source_target_pairs={{0,4},{4,0},{8,12},{12,8},{16,20},{20,16},{24,28},{28,24},{32,36},... | collective-permute-start | bytes 393224 | tf_op jit(solution)/shard_map/ppermute | solution.py:410
  7.2 0.7 copy-start.6
  10.0 29.8 %copy-start.7 = (bf16[2,2,128,128]{3,2,1,0:T(8,128)(2,1)S(1)}, bf16[2,2,128,128]{3,2,1,0:T(8,128)(2,1)}, u32[]{:S(2)}) copy-start(bf16[2,2,128,128]{3,2,1,0:T(8,128)(2,1)} %copy-done.6) | copy-start | bytes 393220
  10.0 29.8 %all-to-all-start = ((bf16[16,2,128,128]{3,2,1,0:T(8,128)(2,1)}), bf16[16,2,128,128]{3,2,1,0:T(8,128)(2,1)S(1)}, u32[]{:S(2)}, u32[]{:S(2)}) async-start(bf16[16,2,128,128]{3,2,1,0:T(8,128)(2,1)} %join.1), calls=%async_computation | async-start | bytes 2097152 | tf_op jit(solution)/shard_map/all_to_all | solution.py:437
  17.8 9.5 %collective-permute-start.5 = (bf16[192,768]{1,0:T(8,128)(2,1)}, bf16[192,768]{1,0:T(8,128)(2,1)S(1)}, u32[]{:S(2)}, u32[]{:S(2)}) collective-permute-start(bf16[192,768]{1,0:T(8,128)(2,1)} %get-tuple-element.31), channel_id=1, source_target_pairs={{0,1},{1,2},{2,3},{3,0},{4,5},{5,6},{6,7},{7,4},{8,9},{9,10},{10,1... | collective-permute-start | bytes 884744 | tf_op jit(solution)/shard_map/ppermute | solution.py:405
  19.2 8.2 %collective-permute-start.6 = (bf16[192,768]{1,0:T(8,128)(2,1)}, bf16[192,768]{1,0:T(8,128)(2,1)S(1)}, u32[]{:S(2)}, u32[]{:S(2)}) collective-permute-start(bf16[192,768]{1,0:T(8,128)(2,1)} %get-tuple-element.32), channel_id=1, source_target_pairs={{0,3},{1,0},{2,1},{3,2},{4,7},{5,4},{6,5},{7,6},{8,11},{9,8},{10,9... | collective-permute-start | bytes 884744 | tf_op jit(solution)/shard_map/ppermute | solution.py:405
  20.7 14.1 %collective-permute-start.7 = (bf16[192,768]{1,0:T(8,128)(2,1)}, bf16[192,768]{1,0:T(8,128)(2,1)S(1)}, u32[]{:S(2)}, u32[]{:S(2)}) collective-permute-start(bf16[192,768]{1,0:T(8,128)(2,1)} %get-tuple-element.33), channel_id=1, source_target_pairs={{0,2},{1,3},{2,0},{3,1},{4,6},{5,7},{6,4},{7,5},{8,10},{9,11},{10,... | collective-permute-start | bytes 884744 | tf_op jit(solution)/shard_map/ppermute | solution.py:405
  35.8 22.0 %collective-permute-start.10 = (bf16[3,192,768]{2,1,0:T(8,128)(2,1)}, bf16[3,192,768]{2,1,0:T(8,128)(2,1)}, u32[]{:S(2)}, u32[]{:S(2)}) collective-permute-start(bf16[3,192,768]{2,1,0:T(8,128)(2,1)} %pad_maximum_fusion.1), channel_id=1, source_target_pairs={{0,96},{4,28},{8,104},{12,4},{16,112},{20,12},{24,120},{28,20},{32... | collective-permute-start | bytes 2654216 | tf_op jit(solution)/shard_map/ppermute | solution.py:410
  38.0 23.2 %collective-permute-start.8 = (bf16[3,192,768]{2,1,0:T(8,128)(2,1)}, bf16[3,192,768]{2,1,0:T(8,128)(2,1)}, u32[]{:S(2)}, u32[]{:S(2)}) collective-permute-start(bf16[3,192,768]{2,1,0:T(8,128)(2,1)} %pad_maximum_fusion.1), channel_id=1, source_target_pairs={{0,32},{4,12},{8,40},{12,20},{16,48},{20,28},{24,56},{28,4},{32,64... | collective-permute-start | bytes 2654216 | tf_op jit(solution)/shard_map/ppermute | solution.py:410
  38.0 23.2 %collective-permute-start.9 = (bf16[3,192,768]{2,1,0:T(8,128)(2,1)}, bf16[3,192,768]{2,1,0:T(8,128)(2,1)}, u32[]{:S(2)}, u32[]{:S(2)}) collective-permute-start(bf16[3,192,768]{2,1,0:T(8,128)(2,1)} %pad_maximum_fusion.1), channel_id=1, source_target_pairs={{0,64},{4,20},{8,72},{12,28},{16,80},{20,4},{24,88},{28,12},{32,96... | collective-permute-start | bytes 2654216 | tf_op jit(solution)/shard_map/ppermute | solution.py:410
  40.3 1.2 %copy-start.4 = (bf16[512,1024]{1,0:T(8,128)(2,1)S(1)}, bf16[512,1024]{1,0:T(8,128)(2,1)}, u32[]{:S(2)}) copy-start(bf16[512,1024]{1,0:T(8,128)(2,1)} %get-tuple-element.23.second) | copy-start | bytes 3145732
  41.5 33.0 %copy-start.2 = (bf16[6144,256]{1,0:T(8,128)(2,1)S(1)}, bf16[6144,256]{1,0:T(8,128)(2,1)}, u32[]{:S(2)}) copy-start(bf16[6144,256]{1,0:T(8,128)(2,1)} %wv.1) | copy-start | bytes 9437188
  45.5 17.7 %collective-permute-start.1 = (bf16[512,768]{1,0:T(8,128)(2,1)S(1)}, bf16[512,768]{1,0:T(8,128)(2,1)S(1)}, u32[]{:S(2)}, u32[]{:S(2)}) collective-permute-start(bf16[512,768]{1,0:T(8,128)(2,1)S(1)} %get-tuple-element.29.upper), channel_id=1, source_target_pairs={{0,1},{1,2},{2,3},{3,0},{4,5},{5,6},{6,7},{7,4},{8,9},{9,10},{10,1... | collective-permute-start | bytes 2359304 | tf_op jit(solution)/shard_map/ppermute | solution.py:405
  46.1 17.1 %collective-permute-start.3 = (bf16[512,768]{1,0:T(8,128)(2,1)S(1)}, bf16[512,768]{1,0:T(8,128)(2,1)S(1)}, u32[]{:S(2)}, u32[]{:S(2)}) collective-permute-start(bf16[512,768]{1,0:T(8,128)(2,1)S(1)} %get-tuple-element.30.lower), channel_id=1, source_target_pairs={{0,3},{1,0},{2,1},{3,2},{4,7},{5,4},{6,5},{7,6},{8,11},{9,8},{10,9... | collective-permute-start | bytes 2359304 | tf_op jit(solution)/shard_map/ppermute | solution.py:405
  63.2 11.3 %copy-start = (bf16[6144,256]{1,0:T(8,128)(2,1)S(1)}, bf16[6144,256]{1,0:T(8,128)(2,1)}, u32[]{:S(2)}) copy-start(bf16[6144,256]{1,0:T(8,128)(2,1)} %wq.1) | copy-start | bytes 9437188
  63.2 11.3 %copy-start.1 = (bf16[6144,256]{1,0:T(8,128)(2,1)S(1)}, bf16[6144,256]{1,0:T(8,128)(2,1)}, u32[]{:S(2)}) copy-start(bf16[6144,256]{1,0:T(8,128)(2,1)} %wk.1) | copy-start | bytes 9437188
  65.6 27.6 %collective-permute-start.11 = (bf16[4,3,192,768]{3,2,1,0:T(8,128)(2,1)S(1)}, bf16[4,3,192,768]{3,2,1,0:T(8,128)(2,1)S(1)}, u32[]{:S(2)}, u32[]{:S(2)}) collective-permute-start(bf16[4,3,192,768]{3,2,1,0:T(8,128)(2,1)S(1)} %pad_maximum_fusion.refs_4_.refs_2_), channel_id=1, source_target_pairs={{0,4},{4,0},{8,12},{12,8},{16,20},{20,16},{24,28},{28,24},{32,36},... | collective-permute-start | bytes 10616840 | tf_op jit(solution)/shard_map/ppermute | solution.py:410
  69.2 20.3 %collective-permute-start.12 = (bf16[512,768]{1,0:T(8,128)(2,1)S(1)}, bf16[512,768]{1,0:T(8,128)(2,1)S(1)}, u32[]{:S(2)}, u32[]{:S(2)}) collective-permute-start(bf16[512,768]{1,0:T(8,128)(2,1)S(1)} %get-tuple-element.30.lower), channel_id=1, source_target_pairs={{0,1},{1,2},{2,3},{3,0},{4,5},{5,6},{6,7},{7,4},{8,9},{9,10},{10,1... | collective-permute-start | bytes 2359304 | tf_op jit(solution)/shard_map/ppermute | solution.py:405
  69.2 20.3 %collective-permute-start.13 = (bf16[512,768]{1,0:T(8,128)(2,1)S(1)}, bf16[512,768]{1,0:T(8,128)(2,1)S(1)}, u32[]{:S(2)}, u32[]{:S(2)}) collective-permute-start(bf16[512,768]{1,0:T(8,128)(2,1)S(1)} %get-tuple-element.29.upper), channel_id=1, source_target_pairs={{0,3},{1,0},{2,1},{3,2},{4,7},{5,4},{6,5},{7,6},{8,11},{9,8},{10,9... | collective-permute-start | bytes 2359304 | tf_op jit(solution)/shard_map/ppermute | solution.py:405
  71.9 34.5 %collective-permute-start.2 = (bf16[512,768]{1,0:T(8,128)(2,1)S(1)}, bf16[512,768]{1,0:T(8,128)(2,1)S(1)}, u32[]{:S(2)}, u32[]{:S(2)}) collective-permute-start(bf16[512,768]{1,0:T(8,128)(2,1)S(1)} %collective-permute-done.1.refs_0_), channel_id=1, source_target_pairs={{0,1},{1,2},{2,3},{3,0},{4,5},{5,6},{6,7},{7,4},{8,9},{9,10},{10,1... | collective-permute-start | bytes 2359304 | tf_op jit(solution)/shard_map/ppermute | solution.py:405
  71.9 34.5 %collective-permute-start.4 = (bf16[512,768]{1,0:T(8,128)(2,1)S(1)}, bf16[512,768]{1,0:T(8,128)(2,1)S(1)}, u32[]{:S(2)}, u32[]{:S(2)}) collective-permute-start(bf16[512,768]{1,0:T(8,128)(2,1)S(1)} %collective-permute-done.3.refs_3_), channel_id=1, source_target_pairs={{0,3},{1,0},{2,1},{3,2},{4,7},{5,4},{6,5},{7,6},{8,11},{9,8},{10,9... | collective-permute-start | bytes 2359304 | tf_op jit(solution)/shard_map/ppermute | solution.py:405

commit v3 on v2

v3 whole, which is shorter than its diff:
```python
import functools

import jax
import jax.numpy as jnp
from jax import lax
from jax.experimental import pallas as pl
from jax.experimental.pallas import tpu as pltpu
from jax.sharding import PartitionSpec as P

BLK = 256
EARLY = 512
CHUNK = 256
HDIM = 128
bf16 = jnp.bfloat16
f32 = jnp.float32
VMEM_LIMIT = 24 * 1024 * 1024
VMEM_ALL = 62 * 1024 * 1024
LIGHT = pl.CostEstimate(flops=1, bytes_accessed=1, transcendentals=0)

SHARES = 8


def place(z, x, c):
    return (z % 4) * 8 + (x % 4) * 2 + c % 2


def nt(a, b):
    return lax.dot_general(a, b, (((1,), (1,)), ((), ())), preferred_element_type=f32)


def nn(a, b):
    return lax.dot_general(a, b, (((1,), (0,)), ((), ())), preferred_element_type=f32)


def tn(a, b):
    return lax.dot_general(a, b, (((0,), (0,)), ((), ())), preferred_element_type=f32)


def spec(*shape):
    return jax.ShapeDtypeStruct(shape, bf16)


def params():
    return pltpu.CompilerParams(vmem_limit_bytes=VMEM_LIMIT)


def whole(count):
    return [pl.BlockSpec(memory_space=pltpu.VMEM)] * count


def fetch(pairs, sems):
    copies = [pltpu.make_async_copy(source, target, sems.at[i]) for i, (source, target) in enumerate(pairs)]
    for copy in copies:
        copy.start()
    return copies


def begin_kernel(
    cut, q, k, v, g, accepted, decay_code, wq, wk, wv, raw, codes, local, message, s1, s2, s3, raw_g, keep, sems
):
    width = q.shape[1]
    rows = raw.shape[0]
    pairs = [(g, raw_g), (accepted, keep)]
    for part, ref in enumerate((q, k, v)):
        pairs.append((ref, raw.at[:, pl.ds(part * width, width)]))
    y = lax.axis_index("head")
    z, x, c = spot()
    piece = c * 4 + jnp.where(c == 0, z, x)
    for out, by in zip((s1, s2, s3), (1, 3, 2)):
        for part, w in enumerate((wq, wk, wv)):
            pairs.append((w.at[lax.rem(y + by, 4), piece], out.at[:, pl.ds(part * width, width)]))
    copies = fetch(pairs, sems)
    line = lax.broadcasted_iota(jnp.int32, codes.shape, 0)
    filled = jnp.zeros(codes.shape, f32)
    for head in range(decay_code.shape[0]):
        filled = jnp.where(line == head, decay_code[head].astype(f32), filled)
    codes[...] = filled.astype(bf16)
    for copy in copies[:2]:
        copy.wait()
    column = jnp.broadcast_to(keep[0:1, :].astype(f32), (HDIM, rows)).T
    wide = jnp.concatenate([column] * (width // HDIM), axis=1)
    raw[:, 3 * width :] = (raw_g[...].astype(f32) * wide).astype(bf16)
    for copy in copies[2:]:
        copy.wait()
    for head in range(local.shape[2]):
        rate = jnp.exp2(-0.5 * jnp.full((1, HDIM), decay_code[head], f32))
        found, spans = [], []
        for half, (low, high) in enumerate(((0, cut), (cut, rows))):
            where = lax.broadcasted_iota(jnp.int32, (high - low, HDIM), 0).astype(f32)
            to_end = jnp.exp(-rate * (high - low - 1.0 - where))
            from_start = jnp.exp(-rate * where)
            spans.append(jnp.exp(-rate * (high - low)))
            at = lambda part: raw[low:high, part * width + head * HDIM : part * width + (head + 1) * HDIM]
            kv = tn((at(1).astype(f32) * to_end).astype(bf16), at(2))
            qg = tn((at(0).astype(f32) * from_start).astype(bf16), at(3))
            found.append((kv, qg))
            local[half, 0, head] = kv
            local[half, 1, head] = qg
        message[0, head] = (spans[1] * found[0][0] + found[1][0]).astype(bf16)
        message[1, head] = (found[0][1] + spans[0] * found[1][1]).astype(bf16)


def begin(q, k, v, g, accepted, decay_code, weights, early):
    rows, width = q.shape
    out_rows = weights[0].shape[0]
    share = out_rows // (4 * SHARES)
    shaped = [w.reshape(4, SHARES, share, width) for w in weights]
    heads = decay_code.shape[0]
    far = pl.BlockSpec(memory_space=pl.ANY)
    return pl.pallas_call(
        functools.partial(begin_kernel, early),
        out_shape=[
            spec(rows, 4 * width),
            spec(16, HDIM),
            jax.ShapeDtypeStruct((2, 2, heads, HDIM, HDIM), f32),
            spec(2, heads, HDIM, HDIM),
            *[spec(share, 3 * width)] * 3,
        ],
        in_specs=[far] * 5 + [pl.BlockSpec(memory_space=pltpu.SMEM)] + [far] * 3,
        out_specs=whole(7),
        scratch_shapes=[
            pltpu.VMEM((rows, width), bf16),
            pltpu.VMEM((1, rows), jnp.int32),
            pltpu.SemaphoreType.DMA((14,)),
        ],
        compiler_params=pltpu.CompilerParams(vmem_limit_bytes=VMEM_ALL),
        cost_estimate=LIGHT,
        name="begin",
    )(q, k, v, g, accepted.reshape(1, rows), decay_code, *shaped)


def spot():
    seq = lax.axis_index("seq")
    return lax.div(seq, 8), lax.rem(lax.div(seq, 2), 4), lax.rem(seq, 2)


def fade(codes, head, span, count):
    rate = jnp.exp2(-0.5 * codes[head : head + 1, :].astype(f32))
    faded = jnp.exp(-rate * (span * jnp.maximum(count, 0).astype(f32)))
    return jnp.where(count >= 0, faded, 0.0)


def join_kernel(rows, codes_at, mine_at, other_at, out, codes, mine, other, sems):
    z, x, c = spot()
    late = c == 1
    chip = z * 4 + x
    for copy in fetch([(codes_at, codes), (mine_at, mine), (other_at, other)], sems):
        copy.wait()
    for head in range(mine.shape[1]):
        one = fade(codes, head, rows, jnp.int32(1))
        near, far = mine[:, head].astype(f32), other[:, head].astype(f32)
        before, after = jnp.where(late, far, near), jnp.where(late, near, far)
        kv = (one * before[0] + after[0]).astype(bf16)
        qg = (before[1] + one * after[1]).astype(bf16)
        for to in range(out.shape[0]):

            @pl.when(c == head)
            def _(to=to, kv=kv, qg=qg):
                out[to, 0] = jnp.where(to > chip, kv, qg)


def join(rows, codes, mine, other):
    return pl.pallas_call(
        functools.partial(join_kernel, rows),
        out_shape=spec(16, 1, *mine.shape[2:]),
        in_specs=[pl.BlockSpec(memory_space=pl.ANY)] * 3,
        out_specs=pl.BlockSpec(memory_space=pltpu.VMEM),
        scratch_shapes=[
            pltpu.VMEM(codes.shape, bf16),
            pltpu.VMEM(mine.shape, bf16),
            pltpu.VMEM(other.shape, bf16),
            pltpu.SemaphoreType.DMA((3,)),
        ],
        compiler_params=pltpu.CompilerParams(vmem_limit_bytes=VMEM_ALL),
        cost_estimate=LIGHT,
        name="join",
    )(codes, mine, other)


def gather_kernel(rows, decay_code, arrived, out):
    z, x, c = spot()
    chip = z * 4 + x
    kv = qg = jnp.zeros((HDIM, HDIM), f32)
    code = jnp.full((1, HDIM), jnp.where(c == 0, decay_code[0], decay_code[1]), jnp.int32)
    for there in range(arrived.shape[0]):
        it = arrived[there, 0].astype(f32)
        kv += it * fade(code, 0, 2 * rows, chip - 1 - there)
        qg += it * fade(code, 0, 2 * rows, there - chip - 1)
    out[0] = kv.astype(bf16)
    out[1] = qg.astype(bf16)


def enter_states(early, rows, codes, mine, theirs, other, local, state0, state1):
    z, x, c = spot()
    late = c == 1
    heads = other.shape[1]
    width = heads * HDIM
    for head in range(heads):
        kv = jnp.where(c == head, mine[0], theirs[0]).astype(f32)
        qg = jnp.where(c == head, mine[1], theirs[1]).astype(f32)
        one = fade(codes, head, rows, jnp.int32(1))
        start = fade(codes, head, early, jnp.int32(1))
        end = fade(codes, head, rows - early, jnp.int32(1))
        kv = jnp.where(late, one * kv + other[0, head].astype(f32), kv)
        qg = jnp.where(late, qg, one * qg + other[1, head].astype(f32))
        here = pl.ds(head * HDIM, HDIM)
        there = pl.ds(width + head * HDIM, HDIM)
        state0[here] = kv.astype(bf16)
        state0[there] = (end * qg + local[1, 1, head]).astype(bf16)
        state1[here] = (start * kv + local[0, 0, head]).astype(bf16)
        state1[there] = qg.astype(bf16)
    state0[2 * width :] = codes[...]
    state1[2 * width :] = codes[...]


def gather(rows, decay_code, arrived):
    return pl.pallas_call(
        functools.partial(gather_kernel, rows),
        out_shape=spec(2, HDIM, HDIM),
        in_specs=[pl.BlockSpec(memory_space=pltpu.SMEM), pl.BlockSpec(memory_space=pltpu.VMEM)],
        out_specs=pl.BlockSpec(memory_space=pltpu.VMEM),
        compiler_params=params(),
        cost_estimate=LIGHT,
        name="gather",
    )(decay_code, arrived)


def attend_rows(raws, state, out_rows, first_row, targets):
    heads = (state.shape[0] - 16) // (2 * HDIM)
    width = heads * HDIM
    rows = out_rows
    starts = list(range(0, rows, BLK))
    sizes = [min(BLK, rows - start) for start in starts]
    count = len(starts)
    edges = [0]
    for raw in raws:
        edges.append(edges[-1] + raw.shape[0])

    def take(block, part, head):
        low, high = starts[block], starts[block] + sizes[block]
        here = slice(part * width + head * HDIM, part * width + (head + 1) * HDIM)
        found = []
        for raw, start, end in zip(raws, edges, edges[1:]):
            if max(low, start) < min(high, end):
                found.append(raw[max(low, start) - start : min(high, end) - start, here])
        return found[0] if len(found) == 1 else jnp.concatenate(found, axis=0)

    def table(rate1, later, earlier, flip):
        shape = (sizes[earlier], sizes[later]) if flip else (sizes[later], sizes[earlier])
        row = lax.broadcasted_iota(jnp.int32, shape, 0)
        col = lax.broadcasted_iota(jnp.int32, shape, 1)
        rate = rate1 if shape[1] == HDIM else jnp.concatenate([rate1] * (shape[1] // HDIM), axis=1)
        gap = (col - row if flip else row - col).astype(f32)
        if later == earlier:
            return jnp.where(gap >= 0, jnp.exp(-rate * jnp.maximum(gap, 0.0)), 0.0)
        return jnp.exp(-rate * (starts[later] - starts[earlier] + gap))

    cut = lambda a, d: (a * d).astype(bf16)
    for head in range(heads):
        code = state[2 * width + head : 2 * width + head + 1, :].astype(f32)
        rate = jnp.exp2(-0.5 * code)
        made = {}

        def decay(later, earlier, flip):
            key = (starts[later] - starts[earlier], sizes[later], sizes[earlier], flip)
            if key not in made:
                made[key] = table(rate, later, earlier, flip)
            return made[key]

        q, k, v, g = ([take(block, part, head) for block in range(count)] for part in range(4))
        kv = state[head * HDIM : (head + 1) * HDIM, :]
        qg = state[width + head * HDIM : width + (head + 1) * HDIM, :]
        for block in range(count):
            start, size = starts[block], sizes[block]
            where = lax.broadcasted_iota(jnp.int32, (size, HDIM), 0).astype(f32) + start
            lag = jnp.exp(-rate * (rows - where))
            dq = jnp.exp(-rate * (where + 1.0)) * nt(g[block], kv)
            dk = lag * nt(v[block], qg)
            dv = lag * nn(k[block], qg)
            for other in range(block + 1):
                dq += nn(cut(nt(g[block], v[other]), decay(block, other, False)), k[other])
            for other in range(block, count):
                dk += nn(cut(nt(v[block], g[other]), decay(other, block, True)), q[other])
                dv += nn(cut(nt(k[block], q[other]), decay(other, block, True)), g[other])
            for part, value in enumerate((dq, dk, dv)):
                here = pl.ds(part * width + head * HDIM, HDIM)
                value = value.astype(bf16)
                low = first_row + start
                for ref, begins in targets:
                    from_row, to_row = max(low, begins), min(low + size, begins + ref.shape[0])
                    if from_row < to_row:
                        ref[from_row - begins : to_row - begins, here] = value[from_row - low : to_row - low]


def attend_kernel(early, rows, *refs):
    inputs, out, rest = refs[:6], refs[6], refs[7:]
    held, (state0, state1, made, sems, out_sems) = rest[:6], rest[6:]
    copies = fetch(list(zip(inputs, held)), sems)
    for copy in copies[:5]:
        copy.wait()
    count = made.shape[0]
    enter_states(float(early), rows, *held[:5], state0, state1)
    written = []

    def leave(low, high):
        written.append(pltpu.make_async_copy(made.at[low:high], out.at[low:high], out_sems.at[len(written)]))
        written[-1].start()

    copies[5].wait()
    attend_rows([held[5].at[0:early]], state0, early, 0, [(made, 0)])
    leave(0, early)
    attend_rows([held[5].at[early:]], state1, count - early, early, [(made, 0)])
    leave(early, count)
    for copy in written:
        copy.wait()


def attend(early, rows, codes, mine, theirs, other, local, raw):
    operands = (codes, mine, theirs, other, local, raw)
    count, depth = raw.shape[0], raw.shape[1] // 4 * 3
    state = pltpu.VMEM((2 * other.shape[1] * HDIM + codes.shape[0], HDIM), bf16)
    anywhere = pl.BlockSpec(memory_space=pl.ANY)
    return pl.pallas_call(
        functools.partial(attend_kernel, early, rows),
        out_shape=spec(count, depth),
        in_specs=[anywhere] * 6,
        out_specs=anywhere,
        scratch_shapes=[pltpu.VMEM(a.shape, a.dtype) for a in operands]
        + [state, state, pltpu.VMEM((count, depth), bf16)]
        + [pltpu.SemaphoreType.DMA((6,)), pltpu.SemaphoreType.DMA((2,))],
        compiler_params=pltpu.CompilerParams(vmem_limit_bytes=VMEM_ALL),
        cost_estimate=LIGHT,
        name="attend",
    )(*operands)


OWN_STEPS = 4


def own_kernel(done, wq, wk, wv, out, w, sems):
    y = lax.axis_index("head")
    cols, width = w.shape[1:]
    part = cols // OWN_STEPS
    pairs = []
    for step in range(OWN_STEPS):
        begins = pl.multiple_of(y * cols + step * part, part)
        pairs += [(ref.at[pl.ds(begins, part)], w.at[i, pl.ds(step * part, part)]) for i, ref in enumerate((wq, wk, wv))]
    copies = fetch(pairs, sems)
    for step in range(OWN_STEPS):
        for copy in copies[3 * step : 3 * step + 3]:
            copy.wait()
        here = slice(step * part, (step + 1) * part)
        total = None
        for i in range(3):
            term = nt(done[:, i * width : (i + 1) * width], w[i, here])
            total = term if total is None else total + term
        out[:, here] = total.astype(bf16)


def project_own(done, weights):
    rows = done.shape[0]
    cols, width = weights[0].shape[0] // 4, weights[0].shape[1]
    return pl.pallas_call(
        own_kernel,
        out_shape=spec(rows, cols),
        in_specs=whole(1) + [pl.BlockSpec(memory_space=pl.ANY)] * 3,
        out_specs=pl.BlockSpec(memory_space=pltpu.VMEM),
        scratch_shapes=[pltpu.VMEM((3, cols, width), bf16), pltpu.SemaphoreType.DMA((3 * OWN_STEPS,))],
        compiler_params=params(),
        cost_estimate=LIGHT,
        name="project_own",
    )(done, *weights)


def arrange_kernel(*refs):
    *blocks, out = refs
    z, x, c = spot()
    outer = jnp.where(c == 0, z, x)
    share = blocks[0].shape[1]
    for far, block in enumerate(blocks):
        at = pl.multiple_of(lax.rem(outer + 4 - far, 4) * share, share)
        for src in range(3):
            out[src, pl.ds(at, share)] = block[src]


def arrange(blocks):
    srcs, share, depth = blocks[0].shape
    return pl.pallas_call(
        arrange_kernel,
        out_shape=spec(srcs, 4 * share, depth),
        in_specs=whole(4),
        out_specs=pl.BlockSpec(memory_space=pltpu.VMEM),
        compiler_params=params(),
        cost_estimate=LIGHT,
        name="arrange",
    )(*blocks)


def column_tiles(tables, cores):
    z, x, c = spot()
    for table, mirrored in zip(tables, cores):
        core = 1 - c if mirrored else c
        half = table.shape[1]
        for start in range(0, half, BLK):
            yield table, slice(start, start + BLK), pl.ds(pl.multiple_of(core * half + start, BLK), BLK)


def others_kernel(spans, cores, *refs):
    parts, refs = refs[: len(spans)], refs[len(spans) :]
    tables, (partial, out) = refs[: len(cores)], refs[len(cores) :]
    for table, inside, at in column_tiles(tables, cores):
        total = partial[:, at].astype(f32)
        for (src, _), part in zip(spans, parts):
            total = total + nt(part[...], table[src - 1, inside])
        out[:, at] = total.astype(bf16)


def project_others(parts, tables, mirrored, partial):
    spans = tuple(part[:2] for part in parts)
    operands = [*[part[2] for part in parts], *tables, partial]
    return pl.pallas_call(
        functools.partial(others_kernel, spans, mirrored),
        out_shape=spec(*partial.shape),
        in_specs=whole(len(operands)),
        out_specs=pl.BlockSpec(memory_space=pltpu.VMEM),
        input_output_aliases={len(operands) - 1: 0},
        compiler_params=params(),
        cost_estimate=LIGHT,
        name="project_others",
    )(*operands)


def last_kernel(spans, cores, *refs):
    parts, refs = refs[: len(spans)], refs[len(spans) :]
    tables, refs = refs[: len(cores)], refs[len(cores) :]
    partial, refs = refs[0], refs[1:]
    out, tiles, sems = refs[-3:]
    made = []
    for i, ((src, start), part) in enumerate(zip(spans, parts)):
        rows = part.shape[0]
        for table, inside, at in column_tiles(tables, cores):
            total = partial[start : start + rows, at].astype(f32) + nt(part[...], table[src - 1, inside])
            slot = len(made)
            tiles[slot] = total.astype(bf16)
            made.append(pltpu.make_async_copy(tiles.at[slot], out.at[pl.ds(start, rows), at], sems.at[slot]))
            made[-1].start()
    for copy in made:
        copy.wait()


def project_last(parts, tables, mirrored, partial, held=None):
    rows = parts[0][2].shape[0]
    count = len(parts) * len(tables) * tables[0].shape[1] // BLK
    spans = tuple(part[:2] for part in parts)
    operands = [*[part[2] for part in parts], *tables, partial] + ([] if held is None else [held])
    anywhere = pl.BlockSpec(memory_space=pl.ANY)
    return pl.pallas_call(
        functools.partial(last_kernel, spans, mirrored),
        out_shape=spec(*partial.shape),
        in_specs=whole(len(parts) + len(tables) + 1) + ([] if held is None else [anywhere]),
        out_specs=anywhere,
        scratch_shapes=[pltpu.VMEM((count, rows, BLK), bf16), pltpu.SemaphoreType.DMA((count,))],
        input_output_aliases={} if held is None else {len(operands) - 1: 0},
        compiler_params=params(),
        cost_estimate=LIGHT,
        name="project_last",
    )(*operands)


def turn(a, by):
    return lax.ppermute(a, "head", [(i, (i + by) % 4) for i in range(4)])


def move(a, where):
    pairs = [(place(z, x, c), place(*where(z, x, c))) for z in range(4) for x in range(4) for c in range(2)]
    return lax.ppermute(a, "seq", pairs)


def across(a):
    return move(a, lambda z, x, c: (z, x, 1 - c))


CHIPS = [[place(z, x, c) for z in range(4) for x in range(4)] for c in range(2)]
def major(a, by):
    return move(a, lambda z, x, c: (z + by, x, c) if c == 0 else (z, x + by, c))


def tie(*groups):
    return lax.optimization_barrier(groups)


def shards(queries, key_rows, value_rows, grad_out, accepted, decay_code, w_query, w_key, w_value):
    heads = decay_code.shape[0]
    count = queries.shape[0]
    rows = float(count)
    weights = (w_query, w_key, w_value)
    raw, codes, local, message, *sent = begin(
        queries, key_rows, value_rows, grad_out, accepted, decay_code, weights, EARLY
    )
    other = across(message)
    leaving = join(rows, codes, message, other)
    share = [turn(sent[0], 1), turn(sent[1], -1), turn(sent[2], 2)]
    arrived = lax.all_to_all(leaving, "seq", 0, 0, axis_index_groups=CHIPS)
    chip_state = gather(rows, decay_code, arrived)
    theirs = across(chip_state)
    done = attend(EARLY, rows, codes, chip_state, theirs, other, local, raw)
    done, *share = tie(done, *share)
    left, right = turn(done, 1), turn(done, -1)
    total = project_own(done, weights)
    left, right, total = tie(left, right, total)
    share = jnp.stack(share)
    half = [share] + [major(share, by) for by in (1, 2, 3)]
    half, _, _ = tie(half, left, right)
    half = arrange(half)
    other_half = across(half)
    far = []
    for start in range(0, count // 2, CHUNK):
        far.append((3, start, turn(left[start : start + CHUNK], 1)))
        start += count // 2
        far.append((3, start, turn(right[start : start + CHUNK], -1)))
    sides = (1, 0, left), (2, 0, right)
    total = project_others(sides, (half,), (False,), total)
    total = project_others(sides, (other_half,), (True,), total)
    out = None
    for i in range(0, len(far), 2):
        out = project_last(far[i : i + 2], (half, other_half), (False, True), total, out)
    return out


def solution(mesh):
    in_specs = (P("seq", "head"),) * 4 + (P("seq"), P("head")) + (P(None, "head"),) * 3
    return jax.shard_map(shards, mesh=mesh, in_specs=in_specs, out_specs=P("seq", "head"), check_vma=False)
```

time: 111 us -> 102 us (0.919)
  waiting for transfers between devices: 45.8 us -> 33 us
  local copies, waits for them, and re-layouts: 1.9 us -> 8.46 us
  other arithmetic: 3.36 us -> 0.1 us
  starting transfers between devices: 29.4 us -> 27.9 us
  Pallas kernels: 30 us -> 31.3 us
    ppermute x5 -> x6, waiting for transfers between devices: 14.2 us -> 2.11 us  [move(): return lax.ppermute(a, 'seq', pairs)]
    ppermute x9, waiting for transfers between devices: 31.6 us -> 24.6 us  [turn(): return lax.ppermute(a, 'head', [(i, (i + by) % 4) for i in range(4)])]
    unnamed x18 -> x16, local copies, waits for them, and re-layouts: 1.9 us -> 8.35 us
    all_to_all x1, waiting for transfers between devices: 0.01 us -> 6.28 us  [shards(): arrived = lax.all_to_all(leaving, 'seq', 0, 0, axis_index_groups=CHIPS)]
    another operation x2 -> x1, other arithmetic: 3.36 us -> 0.1 us  [shards(): share = jnp.stack(share)]
    ppermute x5 -> x6, starting transfers between devices: 9.02 us -> 7.3 us  [move(): return lax.ppermute(a, 'seq', pairs)]
    pallas_call x8 -> x10, Pallas kernels: 30 us -> 31.3 us  [the longest x1 7.14 us: project_own(): pl.pallas_call(own_kernel, out_shape=spec(rows, cols), in_specs=whole(1)...]
  transfers between devices with their start and end apart: 15 -> 16, of which waited for: 8 -> 6; matrix products, arithmetic and copies ran while one was open for 1% -> 0% of each run, Pallas kernels for 17% -> 22%
where the time goes in v3:
time: 102 us; the launch traced here: 101 us
  waiting for transfers between devices  33 us (32%)
  Pallas kernels  31.3 us (31%)
  starting transfers between devices  27.9 us (27%)
  local copies, waits for them, and re-layouts  8.46 us (8%)
    ppermute x9, waiting for transfers between devices, turn(): return lax.ppermute(a, 'head', [(i, (i + by) % 4) for i in range(4)])  24.6 us
    ppermute x9, starting transfers between devices, turn(): return lax.ppermute(a, 'head', [(i, (i + by) % 4) for i in range(4)])  12.9 us
    unnamed x16, local copies, waits for them, and re-layouts  8.35 us
    all_to_all x1, starting transfers between devices, shards(): arrived = lax.all_to_all(leaving, 'seq', 0, 0, axis_index_groups=CHIPS)  7.69 us
    ppermute x6, starting transfers between devices, move(): return lax.ppermute(a, 'seq', pairs)  7.3 us
    pallas_call x1, Pallas kernels, project_own(): pl.pallas_call(own_kernel, out_shape=spec(rows, cols), in_specs=whole(1)...  7.14 us
    pallas_call x1, Pallas kernels, attend(): pl.pallas_call(functools.partial(attend_kernel, early, rows), out_shape=s...  6.82 us
    all_to_all x1, waiting for transfers between devices, shards(): arrived = lax.all_to_all(leaving, 'seq', 0, 0, axis_index_groups=CHIPS)  6.28 us
  transfers between devices with their start and end apart: 16, of which 6 were waited for; matrix products, arithmetic and copies ran while one was open for 0% of the time, Pallas kernels for 22%

profile of v3, /device:TPU:1, one launch (start us, length us, event | category | flops | bytes accessed | tf_op | source)
XLA Modules:
  0.0 101.1 jit_solution(5525550701011199790)
XLA Ops:
  0.0 4.5 %begin.1 = (bf16[1024,1024]{1,0:T(8,128)(2,1)}, bf16[16,128]{1,0:T(8,128)(2,1)}, f32[2,2,2,128,128]{4,3,2,1,0:T(8,128)}, bf16[2,2,128,128]{3,2,1,0:T(8,128)(2,1)...) custom-call(bf16[1024,256]{1,0:T(8,128)(2,1)} %q.1, bf16[1024,256]{1,0:T(8,128)(2,1)} %k.1, ...), custom_call_target="tpu_custom_call" | custom-call | flops 1 | bytes 1 | tf_op jit(solution)/shard_map/begin/pallas_call | solution.py:110
  4.5 1.5 %collective-permute-start = (bf16[2,2,128,128]{3,2,1,0:T(8,128)(2,1)}, bf16[2,2,128,128]{3,2,1,0:T(8,128)(2,1)S(1)}, u32[]{:S(2)}, u32[]{:S(2)}) collective-permute-start(bf16[2,2,128,128]{3,2,1,0:T(8,128)(2,1)} %get-tuple-element.24.mine_at), channel_id=1, source_target_pairs={{0,4},{4,0},{8,12},{12,8},{16,20},{20,16},{24,28},{28,24},{32,36},... | collective-permute-start | bytes 393224 | tf_op jit(solution)/shard_map/ppermute | solution.py:476
  6.0 1.2 %collective-permute-done.other_at.refs_3_ = bf16[2,2,128,128]{3,2,1,0:T(8,128)(2,1)S(1)} collective-permute-done((bf16[2,2,128,128]{3,2,1,0:T(8,128)(2,1)}, bf16[2,2,128,128]{3,2,1,0:T(8,128)(2,1)S(1)}, u32[]{:S(2)}, u32[]{:S(2)}) %collective-permute-start) | collective-permute-done | bytes 131104 | tf_op jit(solution)/shard_map/ppermute | solution.py:476
  7.9 1.9 %join.1 = bf16[16,1,128,128]{3,2,1,0:T(8,128)(2,1)} custom-call(bf16[16,128]{1,0:T(8,128)(2,1)} %get-tuple-element.23.codes_at.refs_0_, bf16[2,2,128,128]{3,2,1,0:T(8,128)(2,1)} %get-tuple-element.24.mine_at, bf16[2,2,128,128]{3,2,1,0:T(8,128)(2,1)} %copy-done.6), custom_call_target="tpu_custom_call" | custom-call | flops 1 | bytes 1 | tf_op jit(solution)/shard_map/join/pallas_call | solution.py:163
  9.8 7.7 %all-to-all-start = ((bf16[16,1,128,128]{3,2,1,0:T(8,128)(2,1)}), bf16[16,1,128,128]{3,2,1,0:T(8,128)(2,1)S(1)}, u32[]{:S(2)}, u32[]{:S(2)}) async-start(bf16[16,1,128,128]{3,2,1,0:T(8,128)(2,1)} %join.1), calls=%async_computation | async-start | bytes 1048576 | tf_op jit(solution)/shard_map/all_to_all | solution.py:503
  17.5 1.4 %collective-permute-start.2 = (bf16[192,768]{1,0:T(8,128)(2,1)}, bf16[192,768]{1,0:T(8,128)(2,1)S(1)}, u32[]{:S(2)}, u32[]{:S(2)}) collective-permute-start(bf16[192,768]{1,0:T(8,128)(2,1)} %get-tuple-element.27), channel_id=1, source_target_pairs={{0,1},{1,2},{2,3},{3,0},{4,5},{5,6},{6,7},{7,4},{8,9},{9,10},{10,1... | collective-permute-start | bytes 884744 | tf_op jit(solution)/shard_map/ppermute | solution.py:471
  18.9 1.5 %collective-permute-start.3 = (bf16[192,768]{1,0:T(8,128)(2,1)}, bf16[192,768]{1,0:T(8,128)(2,1)S(1)}, u32[]{:S(2)}, u32[]{:S(2)}) collective-permute-start(bf16[192,768]{1,0:T(8,128)(2,1)} %get-tuple-element.28), channel_id=1, source_target_pairs={{0,3},{1,0},{2,1},{3,2},{4,7},{5,4},{6,5},{7,6},{8,11},{9,8},{10,9... | collective-permute-start | bytes 884744 | tf_op jit(solution)/shard_map/ppermute | solution.py:471
  20.4 1.6 %collective-permute-start.4 = (bf16[192,768]{1,0:T(8,128)(2,1)}, bf16[192,768]{1,0:T(8,128)(2,1)S(1)}, u32[]{:S(2)}, u32[]{:S(2)}) collective-permute-start(bf16[192,768]{1,0:T(8,128)(2,1)} %get-tuple-element.29), channel_id=1, source_target_pairs={{0,2},{1,3},{2,0},{3,1},{4,6},{5,7},{6,4},{7,5},{8,10},{9,11},{10,... | collective-permute-start | bytes 884744 | tf_op jit(solution)/shard_map/ppermute | solution.py:471
  22.0 6.3 %all-to-all-done.arrived = bf16[16,1,128,128]{3,2,1,0:T(8,128)(2,1)S(1)} async-done(((bf16[16,1,128,128]{3,2,1,0:T(8,128)(2,1)}), bf16[16,1,128,128]{3,2,1,0:T(8,128)(2,1)S(1)}, u32[]{:S(2)}, u32[]{:S(2)}) %all-to-all-start) | async-done | bytes 524320 | tf_op jit(solution)/shard_map/all_to_all | solution.py:503
  28.3 0.8 gather.1.refs_1_
  29.1 1.8 %collective-permute-start.1 = (bf16[2,128,128]{2,1,0:T(8,128)(2,1)S(1)}, bf16[2,128,128]{2,1,0:T(8,128)(2,1)S(1)}, u32[]{:S(2)}, u32[]{:S(2)}) collective-permute-start(bf16[2,128,128]{2,1,0:T(8,128)(2,1)S(1)} %gather.1.refs_1_), channel_id=1, source_target_pairs={{0,4},{4,0},{8,12},{12,8},{16,20},{20,16},{24,28},{28,24},{32,36},... | collective-permute-start | bytes 196616 | tf_op jit(solution)/shard_map/ppermute | solution.py:476
  30.9 0.9 collective-permute-done.1.refs_2_
  32.4 6.8 %attend.1.done = bf16[1024,768]{1,0:T(8,128)(2,1)} custom-call(bf16[16,128]{1,0:T(8,128)(2,1)} %get-tuple-element.23.codes_at.refs_0_, bf16[2,128,128]{2,1,0:T(8,128)(2,1)} %copy-done.4, bf16[2,128,128]{2,1,0:T(8,128)(2,1)} %copy-done.7, bf16[2,2,128,128]{3,2,1,0:T(8,128)(2,1)} %copy-done.6, f32[2,2,2,128,128]{4,3,2,1,0:T(8,128)} %get-tuple-element.25.refs_4_, ...), custom_call_target="tpu_custom_call" | custom-call | flops 1 | bytes 1 | tf_op jit(solution)/shard_map/attend/pallas_call | solution.py:323
  39.3 1.4 %collective-permute-start.5 = (bf16[1024,768]{1,0:T(8,128)(2,1)}, bf16[1024,768]{1,0:T(8,128)(2,1)S(1)}, u32[]{:S(2)}, u32[]{:S(2)}) collective-permute-start(bf16[1024,768]{1,0:T(8,128)(2,1)} %attend.1.done), channel_id=1, source_target_pairs={{0,1},{1,2},{2,3},{3,0},{4,5},{5,6},{6,7},{7,4},{8,9},{9,10},{10,1... | collective-permute-start | bytes 4718600 | tf_op jit(solution)/shard_map/ppermute | solution.py:471
  40.7 1.5 %collective-permute-start.6 = (bf16[1024,768]{1,0:T(8,128)(2,1)}, bf16[1024,768]{1,0:T(8,128)(2,1)S(1)}, u32[]{:S(2)}, u32[]{:S(2)}) collective-permute-start(bf16[1024,768]{1,0:T(8,128)(2,1)} %attend.1.done), channel_id=1, source_target_pairs={{0,3},{1,0},{2,1},{3,2},{4,7},{5,4},{6,5},{7,6},{8,11},{9,8},{10,9... | collective-permute-start | bytes 4718600 | tf_op jit(solution)/shard_map/ppermute | solution.py:471
  42.9 2.1 %collective-permute-start.11 = (bf16[3,192,768]{2,1,0:T(8,128)(2,1)S(1)}, bf16[3,192,768]{2,1,0:T(8,128)(2,1)S(1)}, u32[]{:S(2)}, u32[]{:S(2)}) collective-permute-start(bf16[3,192,768]{2,1,0:T(8,128)(2,1)S(1)} %pad_maximum_fusion.refs_0_), channel_id=1, source_target_pairs={{0,96},{4,28},{8,104},{12,4},{16,112},{20,12},{24,120},{28,20},{32... | collective-permute-start | bytes 2654216 | tf_op jit(solution)/shard_map/ppermute | solution.py:476
  45.1 1.9 %copy-done = bf16[6144,256]{1,0:T(8,128)(2,1)S(1)} copy-done((bf16[6144,256]{1,0:T(8,128)(2,1)S(1)}, bf16[6144,256]{1,0:T(8,128)(2,1)}, u32[]{:S(2)}) %copy-start) | copy-done | bytes 3145752
  47.0 1.9 %copy-done.1 = bf16[6144,256]{1,0:T(8,128)(2,1)S(1)} copy-done((bf16[6144,256]{1,0:T(8,128)(2,1)S(1)}, bf16[6144,256]{1,0:T(8,128)(2,1)}, u32[]{:S(2)}) %copy-start.1) | copy-done | bytes 3145752
  48.8 1.9 %copy-done.2 = bf16[6144,256]{1,0:T(8,128)(2,1)S(1)} copy-done((bf16[6144,256]{1,0:T(8,128)(2,1)S(1)}, bf16[6144,256]{1,0:T(8,128)(2,1)}, u32[]{:S(2)}) %copy-start.2) | copy-done | bytes 3145752
  50.7 1.4 %copy-done.3 = bf16[1024,768]{1,0:T(8,128)(2,1)S(1)} copy-done((bf16[1024,768]{1,0:T(8,128)(2,1)S(1)}, bf16[1024,768]{1,0:T(8,128)(2,1)}, u32[]{:S(2)}) %copy-start.3) | copy-done | bytes 1572888
  52.1 7.1 %project_own.1.refs_3_ = bf16[1024,1536]{1,0:T(8,128)(2,1)S(1)} custom-call(bf16[1024,768]{1,0:T(8,128)(2,1)S(1)} %copy-done.3, bf16[6144,256]{1,0:T(8,128)(2,1)S(1)} %copy-done, bf16[6144,256]{1,0:T(8,128)(2,1)S(1)} %copy-done.1, bf16[6144,256]{1,0:T(8,128)(2,1)S(1)} %copy-done.2), custom_call_target="tpu_custom_call" | custom-call | flops 1 | bytes 1 | tf_op jit(solution)/shard_map/project_own/pallas_call | solution.py:363
  59.3 17.3 %collective-permute-done.5.refs_0_ = bf16[1024,768]{1,0:T(8,128)(2,1)S(1)} collective-permute-done((bf16[1024,768]{1,0:T(8,128)(2,1)}, bf16[1024,768]{1,0:T(8,128)(2,1)S(1)}, u32[]{:S(2)}, u32[]{:S(2)}) %collective-permute-start.5) | collective-permute-done | bytes 1572896 | tf_op jit(solution)/shard_map/ppermute | solution.py:471
  76.9 1.2 %collective-permute-start.12 = (bf16[3,768,768]{2,1,0:T(8,128)(2,1)S(1)}, bf16[3,768,768]{2,1,0:T(8,128)(2,1)S(1)}, u32[]{:S(2)}, u32[]{:S(2)}) collective-permute-start(bf16[3,768,768]{2,1,0:T(8,128)(2,1)S(1)} %arrange.1.refs_2_), channel_id=1, source_target_pairs={{0,4},{4,0},{8,12},{12,8},{16,20},{20,16},{24,28},{28,24},{32,36},... | collective-permute-start | bytes 10616840 | tf_op jit(solution)/shard_map/ppermute | solution.py:476
  78.1 1.4 %collective-permute-start.13 = (bf16[256,768]{1,0:T(8,128)(2,1)S(1)}, bf16[256,768]{1,0:T(8,128)(2,1)S(1)}, u32[]{:S(2)}, u32[]{:S(2)}) collective-permute-start(bf16[256,768]{1,0:T(8,128)(2,1)S(1)} %get-tuple-element.43), channel_id=1, source_target_pairs={{0,1},{1,2},{2,3},{3,0},{4,5},{5,6},{6,7},{7,4},{8,9},{9,10},{10,1... | collective-permute-start | bytes 1179656 | tf_op jit(solution)/shard_map/ppermute | solution.py:471
  79.5 1.5 %collective-permute-start.14 = (bf16[256,768]{1,0:T(8,128)(2,1)S(1)}, bf16[256,768]{1,0:T(8,128)(2,1)S(1)}, u32[]{:S(2)}, u32[]{:S(2)}) collective-permute-start(bf16[256,768]{1,0:T(8,128)(2,1)S(1)} %get-tuple-element.41), channel_id=1, source_target_pairs={{0,3},{1,0},{2,1},{3,2},{4,7},{5,4},{6,5},{7,6},{8,11},{9,8},{10,9... | collective-permute-start | bytes 1179656 | tf_op jit(solution)/shard_map/ppermute | solution.py:471
  81.1 2.7 %collective-permute-start.8 = (bf16[256,768]{1,0:T(8,128)(2,1)S(1)}, bf16[256,768]{1,0:T(8,128)(2,1)S(1)}, u32[]{:S(2)}, u32[]{:S(2)}) collective-permute-start(bf16[256,768]{1,0:T(8,128)(2,1)S(1)} %get-tuple-element.42), channel_id=1, source_target_pairs={{0,3},{1,0},{2,1},{3,2},{4,7},{5,4},{6,5},{7,6},{8,11},{9,8},{10,9... | collective-permute-start | bytes 1179656 | tf_op jit(solution)/shard_map/ppermute | solution.py:471
  83.7 2.7 %project_others.2.refs_3_ = bf16[1024,1536]{1,0:T(8,128)(2,1)S(1)} custom-call(bf16[1024,768]{1,0:T(8,128)(2,1)S(1)} %collective-permute-done.5.refs_0_, bf16[1024,768]{1,0:T(8,128)(2,1)S(1)} %collective-permute-done.6.refs_1_, bf16[3,768,768]{2,1,0:T(8,128)(2,1)S(1)} %arrange.1.refs_2_, ...), custom_call_target="tpu_custom_call", output_to_operand_aliasing={{}: (3, {})} | custom-call | flops 1 | bytes 1 | tf_op jit(solution)/shard_map/project_others/pallas_call | solution.py:421
  86.4 2.7 %project_others.3.refs_4_ = bf16[1024,1536]{1,0:T(8,128)(2,1)S(1)} custom-call(bf16[1024,768]{1,0:T(8,128)(2,1)S(1)} %collective-permute-done.5.refs_0_, bf16[1024,768]{1,0:T(8,128)(2,1)S(1)} %collective-permute-done.6.refs_1_, bf16[3,768,768]{2,1,0:T(8,128)(2,1)S(1)} %collective-permute-done.12.refs_2_.refs_3_, ...), custom_call_target="tpu_custom_call", output_to_operand_aliasing={{}: (3, {})} | custom-call | flops 1 | bytes 1 | tf_op jit(solution)/shard_map/project_others/pallas_call | solution.py:421
  89.1 1.2 %collective-permute-done.13.refs_0_ = bf16[256,768]{1,0:T(8,128)(2,1)S(1)} collective-permute-done((bf16[256,768]{1,0:T(8,128)(2,1)S(1)}, bf16[256,768]{1,0:T(8,128)(2,1)S(1)}, u32[]{:S(2)}, u32[]{:S(2)}) %collective-permute-start.13) | collective-permute-done | bytes 393248 | tf_op jit(solution)/shard_map/ppermute | solution.py:471
  90.3 2.3 %project_last.2.refs_5_ = bf16[1024,1536]{1,0:T(8,128)(2,1)} custom-call(bf16[256,768]{1,0:T(8,128)(2,1)S(1)} %collective-permute-done.13.refs_0_, bf16[256,768]{1,0:T(8,128)(2,1)S(1)} %collective-permute-done.14.refs_1_, bf16[3,768,768]{2,1,0:T(8,128)(2,1)S(1)} %arrange.1.refs_2_, bf16[3,768,768]{2,1,0:T(8,128)(2,1)S(1)} %collective-permute-done.12.refs_2_.refs_3_, ...), custom_call_target="tpu_custom_call" | custom-call | flops 1 | bytes 1 | tf_op jit(solution)/shard_map/project_last/pallas_call | solution.py:457
  92.5 6.2 %collective-permute-done.7.refs_0_ = bf16[256,768]{1,0:T(8,128)(2,1)S(1)} collective-permute-done((bf16[256,768]{1,0:T(8,128)(2,1)S(1)}, bf16[256,768]{1,0:T(8,128)(2,1)S(1)}, u32[]{:S(2)}, u32[]{:S(2)}) %collective-permute-start.7) | collective-permute-done | bytes 393248 | tf_op jit(solution)/shard_map/ppermute | solution.py:471
  98.7 2.3 %project_last.3 = bf16[1024,1536]{1,0:T(8,128)(2,1)} custom-call(bf16[256,768]{1,0:T(8,128)(2,1)S(1)} %collective-permute-done.7.refs_0_, bf16[256,768]{1,0:T(8,128)(2,1)S(1)} %collective-permute-done.8.refs_1_, bf16[3,768,768]{2,1,0:T(8,128)(2,1)S(1)} %arrange.1.refs_2_, ...), custom_call_target="tpu_custom_call", output_to_operand_aliasing={{}: (5, {})} | custom-call | flops 1 | bytes 1 | tf_op jit(solution)/shard_map/project_last/pallas_call | solution.py:457
  (29 shorter events, 2.4 us)
Async XLA Ops:
  0.0 28.3 %copy-start.5 = (s32[2]{0:T(128)S(1)}, s32[2]{0:T(128)}, u32[]{:S(2)}) copy-start(s32[2]{0:T(128)} %decay_code.3) | copy-start | bytes 28
  4.5 2.7 %collective-permute-start = (bf16[2,2,128,128]{3,2,1,0:T(8,128)(2,1)}, bf16[2,2,128,128]{3,2,1,0:T(8,128)(2,1)S(1)}, u32[]{:S(2)}, u32[]{:S(2)}) collective-permute-start(bf16[2,2,128,128]{3,2,1,0:T(8,128)(2,1)} %get-tuple-element.24.mine_at), channel_id=1, source_target_pairs={{0,4},{4,0},{8,12},{12,8},{16,20},{20,16},{24,28},{28,24},{32,36},... | collective-permute-start | bytes 393224 | tf_op jit(solution)/shard_map/ppermute | solution.py:476
  7.2 0.7 copy-start.6
  9.8 18.4 %all-to-all-start = ((bf16[16,1,128,128]{3,2,1,0:T(8,128)(2,1)}), bf16[16,1,128,128]{3,2,1,0:T(8,128)(2,1)S(1)}, u32[]{:S(2)}, u32[]{:S(2)}) async-start(bf16[16,1,128,128]{3,2,1,0:T(8,128)(2,1)} %join.1), calls=%async_computation | async-start | bytes 1048576 | tf_op jit(solution)/shard_map/all_to_all | solution.py:503
  17.5 21.7 %collective-permute-start.2 = (bf16[192,768]{1,0:T(8,128)(2,1)}, bf16[192,768]{1,0:T(8,128)(2,1)S(1)}, u32[]{:S(2)}, u32[]{:S(2)}) collective-permute-start(bf16[192,768]{1,0:T(8,128)(2,1)} %get-tuple-element.27), channel_id=1, source_target_pairs={{0,1},{1,2},{2,3},{3,0},{4,5},{5,6},{6,7},{7,4},{8,9},{9,10},{10,1... | collective-permute-start | bytes 884744 | tf_op jit(solution)/shard_map/ppermute | solution.py:471
  18.9 20.4 %collective-permute-start.3 = (bf16[192,768]{1,0:T(8,128)(2,1)}, bf16[192,768]{1,0:T(8,128)(2,1)S(1)}, u32[]{:S(2)}, u32[]{:S(2)}) collective-permute-start(bf16[192,768]{1,0:T(8,128)(2,1)} %get-tuple-element.28), channel_id=1, source_target_pairs={{0,3},{1,0},{2,1},{3,2},{4,7},{5,4},{6,5},{7,6},{8,11},{9,8},{10,9... | collective-permute-start | bytes 884744 | tf_op jit(solution)/shard_map/ppermute | solution.py:471
  20.4 18.9 %collective-permute-start.4 = (bf16[192,768]{1,0:T(8,128)(2,1)}, bf16[192,768]{1,0:T(8,128)(2,1)S(1)}, u32[]{:S(2)}, u32[]{:S(2)}) collective-permute-start(bf16[192,768]{1,0:T(8,128)(2,1)} %get-tuple-element.29), channel_id=1, source_target_pairs={{0,2},{1,3},{2,0},{3,1},{4,6},{5,7},{6,4},{7,5},{8,10},{9,11},{10,... | collective-permute-start | bytes 884744 | tf_op jit(solution)/shard_map/ppermute | solution.py:471
  29.1 2.8 %copy-start.4 = (bf16[2,128,128]{2,1,0:T(8,128)(2,1)}, bf16[2,128,128]{2,1,0:T(8,128)(2,1)S(1)}, u32[]{:S(2)}) copy-start(bf16[2,128,128]{2,1,0:T(8,128)(2,1)S(1)} %gather.1.refs_1_) | copy-start | bytes 196612
  29.1 2.7 %collective-permute-start.1 = (bf16[2,128,128]{2,1,0:T(8,128)(2,1)S(1)}, bf16[2,128,128]{2,1,0:T(8,128)(2,1)S(1)}, u32[]{:S(2)}, u32[]{:S(2)}) collective-permute-start(bf16[2,128,128]{2,1,0:T(8,128)(2,1)S(1)} %gather.1.refs_1_), channel_id=1, source_target_pairs={{0,4},{4,0},{8,12},{12,8},{16,20},{20,16},{24,28},{28,24},{32,36},... | collective-permute-start | bytes 196616 | tf_op jit(solution)/shard_map/ppermute | solution.py:476
  31.8 0.6 copy-start.7
  39.3 37.3 %collective-permute-start.5 = (bf16[1024,768]{1,0:T(8,128)(2,1)}, bf16[1024,768]{1,0:T(8,128)(2,1)S(1)}, u32[]{:S(2)}, u32[]{:S(2)}) collective-permute-start(bf16[1024,768]{1,0:T(8,128)(2,1)} %attend.1.done), channel_id=1, source_target_pairs={{0,1},{1,2},{2,3},{3,0},{4,5},{5,6},{6,7},{7,4},{8,9},{9,10},{10,1... | collective-permute-start | bytes 4718600 | tf_op jit(solution)/shard_map/ppermute | solution.py:471
  40.7 35.9 %collective-permute-start.6 = (bf16[1024,768]{1,0:T(8,128)(2,1)}, bf16[1024,768]{1,0:T(8,128)(2,1)S(1)}, u32[]{:S(2)}, u32[]{:S(2)}) collective-permute-start(bf16[1024,768]{1,0:T(8,128)(2,1)} %attend.1.done), channel_id=1, source_target_pairs={{0,3},{1,0},{2,1},{3,2},{4,7},{5,4},{6,5},{7,6},{8,11},{9,8},{10,9... | collective-permute-start | bytes 4718600 | tf_op jit(solution)/shard_map/ppermute | solution.py:471
  42.3 34.3 %collective-permute-start.10 = (bf16[3,192,768]{2,1,0:T(8,128)(2,1)S(1)}, bf16[3,192,768]{2,1,0:T(8,128)(2,1)S(1)}, u32[]{:S(2)}, u32[]{:S(2)}) collective-permute-start(bf16[3,192,768]{2,1,0:T(8,128)(2,1)S(1)} %pad_maximum_fusion.refs_0_), channel_id=1, source_target_pairs={{0,64},{4,20},{8,72},{12,28},{16,80},{20,4},{24,88},{28,12},{32,96... | collective-permute-start | bytes 2654216 | tf_op jit(solution)/shard_map/ppermute | solution.py:476
  42.9 33.7 %collective-permute-start.11 = (bf16[3,192,768]{2,1,0:T(8,128)(2,1)S(1)}, bf16[3,192,768]{2,1,0:T(8,128)(2,1)S(1)}, u32[]{:S(2)}, u32[]{:S(2)}) collective-permute-start(bf16[3,192,768]{2,1,0:T(8,128)(2,1)S(1)} %pad_maximum_fusion.refs_0_), channel_id=1, source_target_pairs={{0,96},{4,28},{8,104},{12,4},{16,112},{20,12},{24,120},{28,20},{32... | collective-permute-start | bytes 2654216 | tf_op jit(solution)/shard_map/ppermute | solution.py:476
  45.1 31.5 %collective-permute-start.9 = (bf16[3,192,768]{2,1,0:T(8,128)(2,1)S(1)}, bf16[3,192,768]{2,1,0:T(8,128)(2,1)S(1)}, u32[]{:S(2)}, u32[]{:S(2)}) collective-permute-start(bf16[3,192,768]{2,1,0:T(8,128)(2,1)S(1)} %pad_maximum_fusion.refs_0_), channel_id=1, source_target_pairs={{0,32},{4,12},{8,40},{12,20},{16,48},{20,28},{24,56},{28,4},{32,64... | collective-permute-start | bytes 2654216 | tf_op jit(solution)/shard_map/ppermute | solution.py:476
  45.1 1.9 %copy-start = (bf16[6144,256]{1,0:T(8,128)(2,1)S(1)}, bf16[6144,256]{1,0:T(8,128)(2,1)}, u32[]{:S(2)}) copy-start(bf16[6144,256]{1,0:T(8,128)(2,1)} %wq.1) | copy-start | bytes 9437188
  47.0 1.9 %copy-start.1 = (bf16[6144,256]{1,0:T(8,128)(2,1)S(1)}, bf16[6144,256]{1,0:T(8,128)(2,1)}, u32[]{:S(2)}) copy-start(bf16[6144,256]{1,0:T(8,128)(2,1)} %wk.1) | copy-start | bytes 9437188
  48.8 1.9 %copy-start.2 = (bf16[6144,256]{1,0:T(8,128)(2,1)S(1)}, bf16[6144,256]{1,0:T(8,128)(2,1)}, u32[]{:S(2)}) copy-start(bf16[6144,256]{1,0:T(8,128)(2,1)} %wv.1) | copy-start | bytes 9437188
  50.7 1.4 %copy-start.3 = (bf16[1024,768]{1,0:T(8,128)(2,1)S(1)}, bf16[1024,768]{1,0:T(8,128)(2,1)}, u32[]{:S(2)}) copy-start(bf16[1024,768]{1,0:T(8,128)(2,1)} %attend.1.done) | copy-start | bytes 4718596
  76.9 9.5 %collective-permute-start.12 = (bf16[3,768,768]{2,1,0:T(8,128)(2,1)S(1)}, bf16[3,768,768]{2,1,0:T(8,128)(2,1)S(1)}, u32[]{:S(2)}, u32[]{:S(2)}) collective-permute-start(bf16[3,768,768]{2,1,0:T(8,128)(2,1)S(1)} %arrange.1.refs_2_), channel_id=1, source_target_pairs={{0,4},{4,0},{8,12},{12,8},{16,20},{20,16},{24,28},{28,24},{32,36},... | collective-permute-start | bytes 10616840 | tf_op jit(solution)/shard_map/ppermute | solution.py:476
  78.1 12.1 %collective-permute-start.13 = (bf16[256,768]{1,0:T(8,128)(2,1)S(1)}, bf16[256,768]{1,0:T(8,128)(2,1)S(1)}, u32[]{:S(2)}, u32[]{:S(2)}) collective-permute-start(bf16[256,768]{1,0:T(8,128)(2,1)S(1)} %get-tuple-element.43), channel_id=1, source_target_pairs={{0,1},{1,2},{2,3},{3,0},{4,5},{5,6},{6,7},{7,4},{8,9},{9,10},{10,1... | collective-permute-start | bytes 1179656 | tf_op jit(solution)/shard_map/ppermute | solution.py:471
  79.5 10.7 %collective-permute-start.14 = (bf16[256,768]{1,0:T(8,128)(2,1)S(1)}, bf16[256,768]{1,0:T(8,128)(2,1)S(1)}, u32[]{:S(2)}, u32[]{:S(2)}) collective-permute-start(bf16[256,768]{1,0:T(8,128)(2,1)S(1)} %get-tuple-element.41), channel_id=1, source_target_pairs={{0,3},{1,0},{2,1},{3,2},{4,7},{5,4},{6,5},{7,6},{8,11},{9,8},{10,9... | collective-permute-start | bytes 1179656 | tf_op jit(solution)/shard_map/ppermute | solution.py:471
  81.1 17.6 %collective-permute-start.7 = (bf16[256,768]{1,0:T(8,128)(2,1)S(1)}, bf16[256,768]{1,0:T(8,128)(2,1)S(1)}, u32[]{:S(2)}, u32[]{:S(2)}) collective-permute-start(bf16[256,768]{1,0:T(8,128)(2,1)S(1)} %get-tuple-element.44), channel_id=1, source_target_pairs={{0,1},{1,2},{2,3},{3,0},{4,5},{5,6},{6,7},{7,4},{8,9},{9,10},{10,1... | collective-permute-start | bytes 1179656 | tf_op jit(solution)/shard_map/ppermute | solution.py:471
  81.1 17.6 %collective-permute-start.8 = (bf16[256,768]{1,0:T(8,128)(2,1)S(1)}, bf16[256,768]{1,0:T(8,128)(2,1)S(1)}, u32[]{:S(2)}, u32[]{:S(2)}) collective-permute-start(bf16[256,768]{1,0:T(8,128)(2,1)S(1)} %get-tuple-element.42), channel_id=1, source_target_pairs={{0,3},{1,0},{2,1},{3,2},{4,7},{5,4},{6,5},{7,6},{8,11},{9,8},{10,9... | collective-permute-start | bytes 1179656 | tf_op jit(solution)/shard_map/ppermute | solution.py:471

commit v4 on v3

--- a/solution.py
+++ b/solution.py
@@ -225,9 +225,9 @@
     )(decay_code, arrived)
 
 
-def attend_rows(raws, state, out_rows, first_row, targets):
-    heads = (state.shape[0] - 16) // (2 * HDIM)
-    width = heads * HDIM
+def attend_rows(raws, codes, out_rows, first_row, targets):
+    width = raws[0].shape[1] // 4
+    heads = width // HDIM
     rows = out_rows
     starts = list(range(0, rows, BLK))
     sizes = [min(BLK, rows - start) for start in starts]
@@ -257,8 +257,7 @@
 
     cut = lambda a, d: (a * d).astype(bf16)
     for head in range(heads):
-        code = state[2 * width + head : 2 * width + head + 1, :].astype(f32)
-        rate = jnp.exp2(-0.5 * code)
+        rate = jnp.exp2(-0.5 * codes[head : head + 1, :].astype(f32))
         made = {}
 
         def decay(later, earlier, flip):
@@ -268,15 +267,9 @@
             return made[key]
 
         q, k, v, g = ([take(block, part, head) for block in range(count)] for part in range(4))
-        kv = state[head * HDIM : (head + 1) * HDIM, :]
-        qg = state[width + head * HDIM : width + (head + 1) * HDIM, :]
         for block in range(count):
             start, size = starts[block], sizes[block]
-            where = lax.broadcasted_iota(jnp.int32, (size, HDIM), 0).astype(f32) + start
-            lag = jnp.exp(-rate * (rows - where))
-            dq = jnp.exp(-rate * (where + 1.0)) * nt(g[block], kv)
-            dk = lag * nt(v[block], qg)
-            dv = lag * nn(k[block], qg)
+            dq = dk = dv = jnp.zeros((size, HDIM), f32)
             for other in range(block + 1):
                 dq += nn(cut(nt(g[block], v[other]), decay(block, other, False)), k[other])
             for other in range(block, count):
@@ -292,42 +285,81 @@
                         ref[from_row - begins : to_row - begins, here] = value[from_row - low : to_row - low]
 
 
+def inside_kernel(early, codes_at, raw_at, out, codes, raw, made, sems, out_sems):
+    copies = fetch([(codes_at, codes), (raw_at, raw)], sems)
+    for copy in copies:
+        copy.wait()
+    count = made.shape[0]
+    written = []
+    for i, (low, high) in enumerate(((0, early), (early, count))):
+        attend_rows([raw.at[low:high]], codes, high - low, low, [(made, 0)])
+        written.append(pltpu.make_async_copy(made.at[low:high], out.at[low:high], out_sems.at[i]))
+        written[-1].start()
+    for copy in written:
+        copy.wait()
+
+
+def inside(early, codes, raw):
+    count, depth = raw.shape[0], raw.shape[1] // 4 * 3
+    anywhere = pl.BlockSpec(memory_space=pl.ANY)
+    return pl.pallas_call(
+        functools.partial(inside_kernel, early),
+        out_shape=spec(count, depth),
+        in_specs=[anywhere] * 2,
+        out_specs=anywhere,
+        scratch_shapes=[
+            pltpu.VMEM(codes.shape, bf16),
+            pltpu.VMEM(raw.shape, bf16),
+            pltpu.VMEM((count, depth), bf16),
+            pltpu.SemaphoreType.DMA((2,)),
+            pltpu.SemaphoreType.DMA((2,)),
+        ],
+        compiler_params=pltpu.CompilerParams(vmem_limit_bytes=VMEM_ALL),
+        cost_estimate=LIGHT,
+        name="inside",
+    )(codes, raw)
+
+
 def attend_kernel(early, rows, *refs):
-    inputs, out, rest = refs[:6], refs[6], refs[7:]
-    held, (state0, state1, made, sems, out_sems) = rest[:6], rest[6:]
+    inputs, out, rest = refs[:7], refs[7], refs[8:]
+    held, (state0, state1, sems, out_sems) = rest[:7], rest[7:]
     copies = fetch(list(zip(inputs, held)), sems)
     for copy in copies[:5]:
         copy.wait()
-    count = made.shape[0]
+    codes, raw, made = held[0], held[5], held[6]
+    count, width = made.shape[0], made.shape[1] // 3
     enter_states(float(early), rows, *held[:5], state0, state1)
+    for copy in copies[5:]:
+        copy.wait()
     written = []
-
-    def leave(low, high):
-        written.append(pltpu.make_async_copy(made.at[low:high], out.at[low:high], out_sems.at[len(written)]))
+    for i, (low, high, state) in enumerate(((0, early, state0), (early, count, state1))):
+        where = lax.broadcasted_iota(jnp.int32, (high - low, HDIM), 0).astype(f32)
+        for head in range(width // HDIM):
+            rate = jnp.exp2(-0.5 * codes[head : head + 1, :].astype(f32))
+            lead, lag = jnp.exp(-rate * (where + 1.0)), jnp.exp(-rate * (high - low - where))
+            k, v, g = (raw[low:high, part * width + head * HDIM : part * width + (head + 1) * HDIM] for part in (1, 2, 3))
+            kv = state[head * HDIM : (head + 1) * HDIM, :]
+            qg = state[width + head * HDIM : width + (head + 1) * HDIM, :]
+            for part, value in enumerate((lead * nt(g, kv), lag * nt(v, qg), lag * nn(k, qg))):
+                here = pl.ds(part * width + head * HDIM, HDIM)
+                made[low:high, here] = (made[low:high, here].astype(f32) + value).astype(bf16)
+        written.append(pltpu.make_async_copy(made.at[low:high], out.at[low:high], out_sems.at[i]))
         written[-1].start()
-
-    copies[5].wait()
-    attend_rows([held[5].at[0:early]], state0, early, 0, [(made, 0)])
-    leave(0, early)
-    attend_rows([held[5].at[early:]], state1, count - early, early, [(made, 0)])
-    leave(early, count)
     for copy in written:
         copy.wait()
 
 
-def attend(early, rows, codes, mine, theirs, other, local, raw):
-    operands = (codes, mine, theirs, other, local, raw)
-    count, depth = raw.shape[0], raw.shape[1] // 4 * 3
+def attend(early, rows, codes, mine, theirs, other, local, raw, made):
+    operands = (codes, mine, theirs, other, local, raw, made)
     state = pltpu.VMEM((2 * other.shape[1] * HDIM + codes.shape[0], HDIM), bf16)
     anywhere = pl.BlockSpec(memory_space=pl.ANY)
     return pl.pallas_call(
         functools.partial(attend_kernel, early, rows),
-        out_shape=spec(count, depth),
-        in_specs=[anywhere] * 6,
+        out_shape=spec(*made.shape),
+        in_specs=[anywhere] * 7,
         out_specs=anywhere,
         scratch_shapes=[pltpu.VMEM(a.shape, a.dtype) for a in operands]
-        + [state, state, pltpu.VMEM((count, depth), bf16)]
-        + [pltpu.SemaphoreType.DMA((6,)), pltpu.SemaphoreType.DMA((2,))],
+        + [state, state, pltpu.SemaphoreType.DMA((7,)), pltpu.SemaphoreType.DMA((2,))],
         compiler_params=pltpu.CompilerParams(vmem_limit_bytes=VMEM_ALL),
         cost_estimate=LIGHT,
         name="attend",
@@ -501,9 +533,11 @@
     leaving = join(rows, codes, message, other)
     share = [turn(sent[0], 1), turn(sent[1], -1), turn(sent[2], 2)]
     arrived = lax.all_to_all(leaving, "seq", 0, 0, axis_index_groups=CHIPS)
+    held, leaving = tie((codes, raw), leaving)
+    arrived, made = tie(arrived, inside(EARLY, *held))
     chip_state = gather(rows, decay_code, arrived)
     theirs = across(chip_state)
-    done = attend(EARLY, rows, codes, chip_state, theirs, other, local, raw)
+    done = attend(EARLY, rows, codes, chip_state, theirs, other, local, raw, made)
     done, *share = tie(done, *share)
     left, right = turn(done, 1), turn(done, -1)
     total = project_own(done, weights)

time: 102 us -> 98.8 us (0.969)
  waiting for transfers between devices: 33 us -> 25.6 us
  Pallas kernels: 31.3 us -> 34.7 us
  starting transfers between devices: 27.9 us -> 29.2 us
    all_to_all x1, waiting for transfers between devices: 6.28 us -> 0.16 us  [shards(): arrived = lax.all_to_all(leaving, 'seq', 0, 0, axis_index_groups=CHIPS)]
    pallas_call x0 -> x1, Pallas kernels: none -> 6.11 us  [inside(): pl.pallas_call(functools.partial(inside_kernel, early), out_shape=spec(co...]
    pallas_call x1, Pallas kernels: 6.82 us -> 4.24 us  [attend(): pl.pallas_call(functools.partial(attend_kernel, early, rows), out_shape=s...]
    ppermute x9, waiting for transfers between devices: 24.6 us -> 23.3 us  [turn(): return lax.ppermute(a, 'head', [(i, (i + by) % 4) for i in range(4)])]
    ppermute x6, starting transfers between devices: 7.3 us -> 8.6 us  [move(): return lax.ppermute(a, 'seq', pairs)]
  transfers between devices with their start and end apart: 16 -> 16, of which waited for: 6 -> 6; matrix products, arithmetic and copies ran while one was open for 0% -> 0% of each run, Pallas kernels for 22% -> 26%
where the time goes in v4:
time: 98.8 us; the launch traced here: 98.4 us
  Pallas kernels  34.7 us (35%)
  starting transfers between devices  29.2 us (30%)
  waiting for transfers between devices  25.6 us (26%)
  local copies, waits for them, and re-layouts  8.45 us (9%)
    ppermute x9, waiting for transfers between devices, turn(): return lax.ppermute(a, 'head', [(i, (i + by) % 4) for i in range(4)])  23.3 us
    ppermute x9, starting transfers between devices, turn(): return lax.ppermute(a, 'head', [(i, (i + by) % 4) for i in range(4)])  12.9 us
    ppermute x6, starting transfers between devices, move(): return lax.ppermute(a, 'seq', pairs)  8.6 us
    unnamed x16, local copies, waits for them, and re-layouts  8.34 us
    all_to_all x1, starting transfers between devices, shards(): arrived = lax.all_to_all(leaving, 'seq', 0, 0, axis_index_groups=CHIPS)  7.69 us
    pallas_call x1, Pallas kernels, project_own(): pl.pallas_call(own_kernel, out_shape=spec(rows, cols), in_specs=whole(1)...  7.14 us
    pallas_call x1, Pallas kernels, inside(): pl.pallas_call(functools.partial(inside_kernel, early), out_shape=spec(co...  6.11 us
    pallas_call x2, Pallas kernels, project_others(): pl.pallas_call(functools.partial(others_kernel, spans, mirrored), out_sha...  5.33 us
  transfers between devices with their start and end apart: 16, of which 6 were waited for; matrix products, arithmetic and copies ran while one was open for 0% of the time, Pallas kernels for 26%

profile of v4, /device:TPU:1, one launch (start us, length us, event | category | flops | bytes accessed | tf_op | source)
XLA Modules:
  0.0 98.4 jit_solution(18300152414575540922)
XLA Ops:
  0.0 4.4 %begin.1 = (bf16[1024,1024]{1,0:T(8,128)(2,1)}, bf16[16,128]{1,0:T(8,128)(2,1)}, f32[2,2,2,128,128]{4,3,2,1,0:T(8,128)}, bf16[2,2,128,128]{3,2,1,0:T(8,128)(2,1)...) custom-call(bf16[1024,256]{1,0:T(8,128)(2,1)} %q.1, bf16[1024,256]{1,0:T(8,128)(2,1)} %k.1, ...), custom_call_target="tpu_custom_call" | custom-call | flops 1 | bytes 1 | tf_op jit(solution)/shard_map/begin/pallas_call | solution.py:110
  4.4 1.5 %collective-permute-start = (bf16[2,2,128,128]{3,2,1,0:T(8,128)(2,1)}, bf16[2,2,128,128]{3,2,1,0:T(8,128)(2,1)S(1)}, u32[]{:S(2)}, u32[]{:S(2)}) collective-permute-start(bf16[2,2,128,128]{3,2,1,0:T(8,128)(2,1)} %get-tuple-element.28.mine_at), channel_id=1, source_target_pairs={{0,4},{4,0},{8,12},{12,8},{16,20},{20,16},{24,28},{28,24},{32,36},... | collective-permute-start | bytes 393224 | tf_op jit(solution)/shard_map/ppermute | solution.py:508
  5.9 1.2 %collective-permute-done.other_at.refs_3_ = bf16[2,2,128,128]{3,2,1,0:T(8,128)(2,1)S(1)} collective-permute-done((bf16[2,2,128,128]{3,2,1,0:T(8,128)(2,1)}, bf16[2,2,128,128]{3,2,1,0:T(8,128)(2,1)S(1)}, u32[]{:S(2)}, u32[]{:S(2)}) %collective-permute-start) | collective-permute-done | bytes 131104 | tf_op jit(solution)/shard_map/ppermute | solution.py:508
  7.7 1.9 %join.1 = bf16[16,1,128,128]{3,2,1,0:T(8,128)(2,1)} custom-call(bf16[16,128]{1,0:T(8,128)(2,1)} %get-tuple-element.30.codes_at.refs_0_, bf16[2,2,128,128]{3,2,1,0:T(8,128)(2,1)} %get-tuple-element.28.mine_at, bf16[2,2,128,128]{3,2,1,0:T(8,128)(2,1)} %copy-done.6), custom_call_target="tpu_custom_call" | custom-call | flops 1 | bytes 1 | tf_op jit(solution)/shard_map/join/pallas_call | solution.py:163
  9.7 7.7 %all-to-all-start = ((bf16[16,1,128,128]{3,2,1,0:T(8,128)(2,1)}), bf16[16,1,128,128]{3,2,1,0:T(8,128)(2,1)S(1)}, u32[]{:S(2)}, u32[]{:S(2)}) async-start(bf16[16,1,128,128]{3,2,1,0:T(8,128)(2,1)} %join.1), calls=%async_computation | async-start | bytes 1048576 | tf_op jit(solution)/shard_map/all_to_all | solution.py:535
  17.4 1.4 %collective-permute-start.2 = (bf16[192,768]{1,0:T(8,128)(2,1)}, bf16[192,768]{1,0:T(8,128)(2,1)S(1)}, u32[]{:S(2)}, u32[]{:S(2)}) collective-permute-start(bf16[192,768]{1,0:T(8,128)(2,1)} %get-tuple-element.35), channel_id=1, source_target_pairs={{0,1},{1,2},{2,3},{3,0},{4,5},{5,6},{6,7},{7,4},{8,9},{9,10},{10,1... | collective-permute-start | bytes 884744 | tf_op jit(solution)/shard_map/ppermute | solution.py:503
  18.8 1.5 %collective-permute-start.3 = (bf16[192,768]{1,0:T(8,128)(2,1)}, bf16[192,768]{1,0:T(8,128)(2,1)S(1)}, u32[]{:S(2)}, u32[]{:S(2)}) collective-permute-start(bf16[192,768]{1,0:T(8,128)(2,1)} %get-tuple-element.36), channel_id=1, source_target_pairs={{0,3},{1,0},{2,1},{3,2},{4,7},{5,4},{6,5},{7,6},{8,11},{9,8},{10,9... | collective-permute-start | bytes 884744 | tf_op jit(solution)/shard_map/ppermute | solution.py:503
  20.3 1.6 %collective-permute-start.4 = (bf16[192,768]{1,0:T(8,128)(2,1)}, bf16[192,768]{1,0:T(8,128)(2,1)S(1)}, u32[]{:S(2)}, u32[]{:S(2)}) collective-permute-start(bf16[192,768]{1,0:T(8,128)(2,1)} %get-tuple-element.37), channel_id=1, source_target_pairs={{0,2},{1,3},{2,0},{3,1},{4,6},{5,7},{6,4},{7,5},{8,10},{9,11},{10,... | collective-permute-start | bytes 884744 | tf_op jit(solution)/shard_map/ppermute | solution.py:503
  21.8 6.1 %inside.1.refs_6_ = bf16[1024,768]{1,0:T(8,128)(2,1)} custom-call(bf16[16,128]{1,0:T(8,128)(2,1)} %get-tuple-element.30.codes_at.refs_0_, bf16[1024,1024]{1,0:T(8,128)(2,1)} %get-tuple-element.31.raw_at.refs_5_), custom_call_target="tpu_custom_call" | custom-call | flops 1 | bytes 1 | tf_op jit(solution)/shard_map/inside/pallas_call | solution.py:305
  28.9 1.8 %collective-permute-start.1 = (bf16[2,128,128]{2,1,0:T(8,128)(2,1)S(1)}, bf16[2,128,128]{2,1,0:T(8,128)(2,1)S(1)}, u32[]{:S(2)}, u32[]{:S(2)}) collective-permute-start(bf16[2,128,128]{2,1,0:T(8,128)(2,1)S(1)} %gather.1.refs_1_), channel_id=1, source_target_pairs={{0,4},{4,0},{8,12},{12,8},{16,20},{20,16},{24,28},{28,24},{32,36},... | collective-permute-start | bytes 196616 | tf_op jit(solution)/shard_map/ppermute | solution.py:508
  30.8 0.9 collective-permute-done.1.refs_2_
  32.3 4.2 %attend.1.done = bf16[1024,768]{1,0:T(8,128)(2,1)} custom-call(bf16[16,128]{1,0:T(8,128)(2,1)} %get-tuple-element.30.codes_at.refs_0_, bf16[2,128,128]{2,1,0:T(8,128)(2,1)} %copy-done.4, bf16[2,128,128]{2,1,0:T(8,128)(2,1)} %copy-done.7, bf16[2,2,128,128]{3,2,1,0:T(8,128)(2,1)} %copy-done.6, f32[2,2,2,128,128]{4,3,2,1,0:T(8,128)} %get-tuple-element.33.refs_4_, ...), custom_call_target="tpu_custom_call" | custom-call | flops 1 | bytes 1 | tf_op jit(solution)/shard_map/attend/pallas_call | solution.py:356
  36.6 1.4 %collective-permute-start.5 = (bf16[1024,768]{1,0:T(8,128)(2,1)}, bf16[1024,768]{1,0:T(8,128)(2,1)S(1)}, u32[]{:S(2)}, u32[]{:S(2)}) collective-permute-start(bf16[1024,768]{1,0:T(8,128)(2,1)} %attend.1.done), channel_id=1, source_target_pairs={{0,1},{1,2},{2,3},{3,0},{4,5},{5,6},{6,7},{7,4},{8,9},{9,10},{10,1... | collective-permute-start | bytes 4718600 | tf_op jit(solution)/shard_map/ppermute | solution.py:503
  38.0 1.5 %collective-permute-start.6 = (bf16[1024,768]{1,0:T(8,128)(2,1)}, bf16[1024,768]{1,0:T(8,128)(2,1)S(1)}, u32[]{:S(2)}, u32[]{:S(2)}) collective-permute-start(bf16[1024,768]{1,0:T(8,128)(2,1)} %attend.1.done), channel_id=1, source_target_pairs={{0,3},{1,0},{2,1},{3,2},{4,7},{5,4},{6,5},{7,6},{8,11},{9,8},{10,9... | collective-permute-start | bytes 4718600 | tf_op jit(solution)/shard_map/ppermute | solution.py:503
  39.6 2.6 %collective-permute-start.10 = (bf16[3,192,768]{2,1,0:T(8,128)(2,1)S(1)}, bf16[3,192,768]{2,1,0:T(8,128)(2,1)S(1)}, u32[]{:S(2)}, u32[]{:S(2)}) collective-permute-start(bf16[3,192,768]{2,1,0:T(8,128)(2,1)S(1)} %pad_maximum_fusion.refs_0_), channel_id=1, source_target_pairs={{0,64},{4,20},{8,72},{12,28},{16,80},{20,4},{24,88},{28,12},{32,96... | collective-permute-start | bytes 2654216 | tf_op jit(solution)/shard_map/ppermute | solution.py:508
  42.2 0.9 collective-permute-start.11
  43.6 1.9 %copy-done = bf16[6144,256]{1,0:T(8,128)(2,1)S(1)} copy-done((bf16[6144,256]{1,0:T(8,128)(2,1)S(1)}, bf16[6144,256]{1,0:T(8,128)(2,1)}, u32[]{:S(2)}) %copy-start) | copy-done | bytes 3145752
  45.5 1.9 %copy-done.1 = bf16[6144,256]{1,0:T(8,128)(2,1)S(1)} copy-done((bf16[6144,256]{1,0:T(8,128)(2,1)S(1)}, bf16[6144,256]{1,0:T(8,128)(2,1)}, u32[]{:S(2)}) %copy-start.1) | copy-done | bytes 3145752
  47.4 1.9 %copy-done.2 = bf16[6144,256]{1,0:T(8,128)(2,1)S(1)} copy-done((bf16[6144,256]{1,0:T(8,128)(2,1)S(1)}, bf16[6144,256]{1,0:T(8,128)(2,1)}, u32[]{:S(2)}) %copy-start.2) | copy-done | bytes 3145752
  49.3 1.4 %copy-done.3 = bf16[1024,768]{1,0:T(8,128)(2,1)S(1)} copy-done((bf16[1024,768]{1,0:T(8,128)(2,1)S(1)}, bf16[1024,768]{1,0:T(8,128)(2,1)}, u32[]{:S(2)}) %copy-start.3) | copy-done | bytes 1572888
  50.7 7.1 %project_own.1.refs_3_ = bf16[1024,1536]{1,0:T(8,128)(2,1)S(1)} custom-call(bf16[1024,768]{1,0:T(8,128)(2,1)S(1)} %copy-done.3, bf16[6144,256]{1,0:T(8,128)(2,1)S(1)} %copy-done, bf16[6144,256]{1,0:T(8,128)(2,1)S(1)} %copy-done.1, bf16[6144,256]{1,0:T(8,128)(2,1)S(1)} %copy-done.2), custom_call_target="tpu_custom_call" | custom-call | flops 1 | bytes 1 | tf_op jit(solution)/shard_map/project_own/pallas_call | solution.py:395
  57.9 16.0 %collective-permute-done.5.refs_0_ = bf16[1024,768]{1,0:T(8,128)(2,1)S(1)} collective-permute-done((bf16[1024,768]{1,0:T(8,128)(2,1)}, bf16[1024,768]{1,0:T(8,128)(2,1)S(1)}, u32[]{:S(2)}, u32[]{:S(2)}) %collective-permute-start.5) | collective-permute-done | bytes 1572896 | tf_op jit(solution)/shard_map/ppermute | solution.py:503
  74.1 1.2 %collective-permute-start.12 = (bf16[3,768,768]{2,1,0:T(8,128)(2,1)S(1)}, bf16[3,768,768]{2,1,0:T(8,128)(2,1)S(1)}, u32[]{:S(2)}, u32[]{:S(2)}) collective-permute-start(bf16[3,768,768]{2,1,0:T(8,128)(2,1)S(1)} %arrange.1.refs_2_), channel_id=1, source_target_pairs={{0,4},{4,0},{8,12},{12,8},{16,20},{20,16},{24,28},{28,24},{32,36},... | collective-permute-start | bytes 10616840 | tf_op jit(solution)/shard_map/ppermute | solution.py:508
  75.4 1.4 %collective-permute-start.13 = (bf16[256,768]{1,0:T(8,128)(2,1)S(1)}, bf16[256,768]{1,0:T(8,128)(2,1)S(1)}, u32[]{:S(2)}, u32[]{:S(2)}) collective-permute-start(bf16[256,768]{1,0:T(8,128)(2,1)S(1)} %get-tuple-element.51), channel_id=1, source_target_pairs={{0,1},{1,2},{2,3},{3,0},{4,5},{5,6},{6,7},{7,4},{8,9},{9,10},{10,1... | collective-permute-start | bytes 1179656 | tf_op jit(solution)/shard_map/ppermute | solution.py:503
  76.8 1.5 %collective-permute-start.14 = (bf16[256,768]{1,0:T(8,128)(2,1)S(1)}, bf16[256,768]{1,0:T(8,128)(2,1)S(1)}, u32[]{:S(2)}, u32[]{:S(2)}) collective-permute-start(bf16[256,768]{1,0:T(8,128)(2,1)S(1)} %get-tuple-element.49), channel_id=1, source_target_pairs={{0,3},{1,0},{2,1},{3,2},{4,7},{5,4},{6,5},{7,6},{8,11},{9,8},{10,9... | collective-permute-start | bytes 1179656 | tf_op jit(solution)/shard_map/ppermute | solution.py:503
  78.3 2.7 %collective-permute-start.8 = (bf16[256,768]{1,0:T(8,128)(2,1)S(1)}, bf16[256,768]{1,0:T(8,128)(2,1)S(1)}, u32[]{:S(2)}, u32[]{:S(2)}) collective-permute-start(bf16[256,768]{1,0:T(8,128)(2,1)S(1)} %get-tuple-element.50), channel_id=1, source_target_pairs={{0,3},{1,0},{2,1},{3,2},{4,7},{5,4},{6,5},{7,6},{8,11},{9,8},{10,9... | collective-permute-start | bytes 1179656 | tf_op jit(solution)/shard_map/ppermute | solution.py:503
  81.0 2.7 %project_others.2.refs_3_ = bf16[1024,1536]{1,0:T(8,128)(2,1)S(1)} custom-call(bf16[1024,768]{1,0:T(8,128)(2,1)S(1)} %collective-permute-done.5.refs_0_, bf16[1024,768]{1,0:T(8,128)(2,1)S(1)} %collective-permute-done.6.refs_1_, bf16[3,768,768]{2,1,0:T(8,128)(2,1)S(1)} %arrange.1.refs_2_, ...), custom_call_target="tpu_custom_call", output_to_operand_aliasing={{}: (3, {})} | custom-call | flops 1 | bytes 1 | tf_op jit(solution)/shard_map/project_others/pallas_call | solution.py:453
  83.7 2.7 %project_others.3.refs_4_ = bf16[1024,1536]{1,0:T(8,128)(2,1)S(1)} custom-call(bf16[1024,768]{1,0:T(8,128)(2,1)S(1)} %collective-permute-done.5.refs_0_, bf16[1024,768]{1,0:T(8,128)(2,1)S(1)} %collective-permute-done.6.refs_1_, bf16[3,768,768]{2,1,0:T(8,128)(2,1)S(1)} %collective-permute-done.12.refs_2_.refs_3_, ...), custom_call_target="tpu_custom_call", output_to_operand_aliasing={{}: (3, {})} | custom-call | flops 1 | bytes 1 | tf_op jit(solution)/shard_map/project_others/pallas_call | solution.py:453
  86.4 1.2 %collective-permute-done.13.refs_0_ = bf16[256,768]{1,0:T(8,128)(2,1)S(1)} collective-permute-done((bf16[256,768]{1,0:T(8,128)(2,1)S(1)}, bf16[256,768]{1,0:T(8,128)(2,1)S(1)}, u32[]{:S(2)}, u32[]{:S(2)}) %collective-permute-start.13) | collective-permute-done | bytes 393248 | tf_op jit(solution)/shard_map/ppermute | solution.py:503
  87.5 2.3 %project_last.2.refs_5_ = bf16[1024,1536]{1,0:T(8,128)(2,1)} custom-call(bf16[256,768]{1,0:T(8,128)(2,1)S(1)} %collective-permute-done.13.refs_0_, bf16[256,768]{1,0:T(8,128)(2,1)S(1)} %collective-permute-done.14.refs_1_, bf16[3,768,768]{2,1,0:T(8,128)(2,1)S(1)} %arrange.1.refs_2_, bf16[3,768,768]{2,1,0:T(8,128)(2,1)S(1)} %collective-permute-done.12.refs_2_.refs_3_, ...), custom_call_target="tpu_custom_call" | custom-call | flops 1 | bytes 1 | tf_op jit(solution)/shard_map/project_last/pallas_call | solution.py:489
  89.8 6.2 %collective-permute-done.7.refs_0_ = bf16[256,768]{1,0:T(8,128)(2,1)S(1)} collective-permute-done((bf16[256,768]{1,0:T(8,128)(2,1)S(1)}, bf16[256,768]{1,0:T(8,128)(2,1)S(1)}, u32[]{:S(2)}, u32[]{:S(2)}) %collective-permute-start.7) | collective-permute-done | bytes 393248 | tf_op jit(solution)/shard_map/ppermute | solution.py:503
  96.0 2.3 %project_last.3 = bf16[1024,1536]{1,0:T(8,128)(2,1)} custom-call(bf16[256,768]{1,0:T(8,128)(2,1)S(1)} %collective-permute-done.7.refs_0_, bf16[256,768]{1,0:T(8,128)(2,1)S(1)} %collective-permute-done.8.refs_1_, bf16[3,768,768]{2,1,0:T(8,128)(2,1)S(1)} %arrange.1.refs_2_, ...), custom_call_target="tpu_custom_call", output_to_operand_aliasing={{}: (5, {})} | custom-call | flops 1 | bytes 1 | tf_op jit(solution)/shard_map/project_last/pallas_call | solution.py:489
  (30 shorter events, 3.3 us)
Async XLA Ops:
  4.4 23.7 %copy-start.5 = (s32[2]{0:T(128)S(1)}, s32[2]{0:T(128)}, u32[]{:S(2)}) copy-start(s32[2]{0:T(128)} %decay_code.3) | copy-start | bytes 28
  4.4 2.7 %collective-permute-start = (bf16[2,2,128,128]{3,2,1,0:T(8,128)(2,1)}, bf16[2,2,128,128]{3,2,1,0:T(8,128)(2,1)S(1)}, u32[]{:S(2)}, u32[]{:S(2)}) collective-permute-start(bf16[2,2,128,128]{3,2,1,0:T(8,128)(2,1)} %get-tuple-element.28.mine_at), channel_id=1, source_target_pairs={{0,4},{4,0},{8,12},{12,8},{16,20},{20,16},{24,28},{28,24},{32,36},... | collective-permute-start | bytes 393224 | tf_op jit(solution)/shard_map/ppermute | solution.py:508
  7.1 0.6 copy-start.6
  9.7 18.4 %all-to-all-start = ((bf16[16,1,128,128]{3,2,1,0:T(8,128)(2,1)}), bf16[16,1,128,128]{3,2,1,0:T(8,128)(2,1)S(1)}, u32[]{:S(2)}, u32[]{:S(2)}) async-start(bf16[16,1,128,128]{3,2,1,0:T(8,128)(2,1)} %join.1), calls=%async_computation | async-start | bytes 1048576 | tf_op jit(solution)/shard_map/all_to_all | solution.py:535
  17.4 19.2 %collective-permute-start.2 = (bf16[192,768]{1,0:T(8,128)(2,1)}, bf16[192,768]{1,0:T(8,128)(2,1)S(1)}, u32[]{:S(2)}, u32[]{:S(2)}) collective-permute-start(bf16[192,768]{1,0:T(8,128)(2,1)} %get-tuple-element.35), channel_id=1, source_target_pairs={{0,1},{1,2},{2,3},{3,0},{4,5},{5,6},{6,7},{7,4},{8,9},{9,10},{10,1... | collective-permute-start | bytes 884744 | tf_op jit(solution)/shard_map/ppermute | solution.py:503
  18.8 17.8 %collective-permute-start.3 = (bf16[192,768]{1,0:T(8,128)(2,1)}, bf16[192,768]{1,0:T(8,128)(2,1)S(1)}, u32[]{:S(2)}, u32[]{:S(2)}) collective-permute-start(bf16[192,768]{1,0:T(8,128)(2,1)} %get-tuple-element.36), channel_id=1, source_target_pairs={{0,3},{1,0},{2,1},{3,2},{4,7},{5,4},{6,5},{7,6},{8,11},{9,8},{10,9... | collective-permute-start | bytes 884744 | tf_op jit(solution)/shard_map/ppermute | solution.py:503
  20.3 16.3 %collective-permute-start.4 = (bf16[192,768]{1,0:T(8,128)(2,1)}, bf16[192,768]{1,0:T(8,128)(2,1)S(1)}, u32[]{:S(2)}, u32[]{:S(2)}) collective-permute-start(bf16[192,768]{1,0:T(8,128)(2,1)} %get-tuple-element.37), channel_id=1, source_target_pairs={{0,2},{1,3},{2,0},{3,1},{4,6},{5,7},{6,4},{7,5},{8,10},{9,11},{10,... | collective-permute-start | bytes 884744 | tf_op jit(solution)/shard_map/ppermute | solution.py:503
  28.9 2.8 %copy-start.4 = (bf16[2,128,128]{2,1,0:T(8,128)(2,1)}, bf16[2,128,128]{2,1,0:T(8,128)(2,1)S(1)}, u32[]{:S(2)}) copy-start(bf16[2,128,128]{2,1,0:T(8,128)(2,1)S(1)} %gather.1.refs_1_) | copy-start | bytes 196612
  28.9 2.7 %collective-permute-start.1 = (bf16[2,128,128]{2,1,0:T(8,128)(2,1)S(1)}, bf16[2,128,128]{2,1,0:T(8,128)(2,1)S(1)}, u32[]{:S(2)}, u32[]{:S(2)}) collective-permute-start(bf16[2,128,128]{2,1,0:T(8,128)(2,1)S(1)} %gather.1.refs_1_), channel_id=1, source_target_pairs={{0,4},{4,0},{8,12},{12,8},{16,20},{20,16},{24,28},{28,24},{32,36},... | collective-permute-start | bytes 196616 | tf_op jit(solution)/shard_map/ppermute | solution.py:508
  31.7 0.6 copy-start.7
  36.6 37.3 %collective-permute-start.5 = (bf16[1024,768]{1,0:T(8,128)(2,1)}, bf16[1024,768]{1,0:T(8,128)(2,1)S(1)}, u32[]{:S(2)}, u32[]{:S(2)}) collective-permute-start(bf16[1024,768]{1,0:T(8,128)(2,1)} %attend.1.done), channel_id=1, source_target_pairs={{0,1},{1,2},{2,3},{3,0},{4,5},{5,6},{6,7},{7,4},{8,9},{9,10},{10,1... | collective-permute-start | bytes 4718600 | tf_op jit(solution)/shard_map/ppermute | solution.py:503
  38.0 35.9 %collective-permute-start.6 = (bf16[1024,768]{1,0:T(8,128)(2,1)}, bf16[1024,768]{1,0:T(8,128)(2,1)S(1)}, u32[]{:S(2)}, u32[]{:S(2)}) collective-permute-start(bf16[1024,768]{1,0:T(8,128)(2,1)} %attend.1.done), channel_id=1, source_target_pairs={{0,3},{1,0},{2,1},{3,2},{4,7},{5,4},{6,5},{7,6},{8,11},{9,8},{10,9... | collective-permute-start | bytes 4718600 | tf_op jit(solution)/shard_map/ppermute | solution.py:503
  39.6 34.3 %collective-permute-start.10 = (bf16[3,192,768]{2,1,0:T(8,128)(2,1)S(1)}, bf16[3,192,768]{2,1,0:T(8,128)(2,1)S(1)}, u32[]{:S(2)}, u32[]{:S(2)}) collective-permute-start(bf16[3,192,768]{2,1,0:T(8,128)(2,1)S(1)} %pad_maximum_fusion.refs_0_), channel_id=1, source_target_pairs={{0,64},{4,20},{8,72},{12,28},{16,80},{20,4},{24,88},{28,12},{32,96... | collective-permute-start | bytes 2654216 | tf_op jit(solution)/shard_map/ppermute | solution.py:508
  42.2 31.7 %collective-permute-start.11 = (bf16[3,192,768]{2,1,0:T(8,128)(2,1)S(1)}, bf16[3,192,768]{2,1,0:T(8,128)(2,1)S(1)}, u32[]{:S(2)}, u32[]{:S(2)}) collective-permute-start(bf16[3,192,768]{2,1,0:T(8,128)(2,1)S(1)} %pad_maximum_fusion.refs_0_), channel_id=1, source_target_pairs={{0,96},{4,28},{8,104},{12,4},{16,112},{20,12},{24,120},{28,20},{32... | collective-permute-start | bytes 2654216 | tf_op jit(solution)/shard_map/ppermute | solution.py:508
  43.1 30.8 %collective-permute-start.9 = (bf16[3,192,768]{2,1,0:T(8,128)(2,1)S(1)}, bf16[3,192,768]{2,1,0:T(8,128)(2,1)S(1)}, u32[]{:S(2)}, u32[]{:S(2)}) collective-permute-start(bf16[3,192,768]{2,1,0:T(8,128)(2,1)S(1)} %pad_maximum_fusion.refs_0_), channel_id=1, source_target_pairs={{0,32},{4,12},{8,40},{12,20},{16,48},{20,28},{24,56},{28,4},{32,64... | collective-permute-start | bytes 2654216 | tf_op jit(solution)/shard_map/ppermute | solution.py:508
  43.6 1.9 %copy-start = (bf16[6144,256]{1,0:T(8,128)(2,1)S(1)}, bf16[6144,256]{1,0:T(8,128)(2,1)}, u32[]{:S(2)}) copy-start(bf16[6144,256]{1,0:T(8,128)(2,1)} %wq.1) | copy-start | bytes 9437188
  45.5 1.9 %copy-start.1 = (bf16[6144,256]{1,0:T(8,128)(2,1)S(1)}, bf16[6144,256]{1,0:T(8,128)(2,1)}, u32[]{:S(2)}) copy-start(bf16[6144,256]{1,0:T(8,128)(2,1)} %wk.1) | copy-start | bytes 9437188
  47.4 1.9 %copy-start.2 = (bf16[6144,256]{1,0:T(8,128)(2,1)S(1)}, bf16[6144,256]{1,0:T(8,128)(2,1)}, u32[]{:S(2)}) copy-start(bf16[6144,256]{1,0:T(8,128)(2,1)} %wv.1) | copy-start | bytes 9437188
  49.3 1.4 %copy-start.3 = (bf16[1024,768]{1,0:T(8,128)(2,1)S(1)}, bf16[1024,768]{1,0:T(8,128)(2,1)}, u32[]{:S(2)}) copy-start(bf16[1024,768]{1,0:T(8,128)(2,1)} %attend.1.done) | copy-start | bytes 4718596
  74.1 9.6 %collective-permute-start.12 = (bf16[3,768,768]{2,1,0:T(8,128)(2,1)S(1)}, bf16[3,768,768]{2,1,0:T(8,128)(2,1)S(1)}, u32[]{:S(2)}, u32[]{:S(2)}) collective-permute-start(bf16[3,768,768]{2,1,0:T(8,128)(2,1)S(1)} %arrange.1.refs_2_), channel_id=1, source_target_pairs={{0,4},{4,0},{8,12},{12,8},{16,20},{20,16},{24,28},{28,24},{32,36},... | collective-permute-start | bytes 10616840 | tf_op jit(solution)/shard_map/ppermute | solution.py:508
  75.4 12.1 %collective-permute-start.13 = (bf16[256,768]{1,0:T(8,128)(2,1)S(1)}, bf16[256,768]{1,0:T(8,128)(2,1)S(1)}, u32[]{:S(2)}, u32[]{:S(2)}) collective-permute-start(bf16[256,768]{1,0:T(8,128)(2,1)S(1)} %get-tuple-element.51), channel_id=1, source_target_pairs={{0,1},{1,2},{2,3},{3,0},{4,5},{5,6},{6,7},{7,4},{8,9},{9,10},{10,1... | collective-permute-start | bytes 1179656 | tf_op jit(solution)/shard_map/ppermute | solution.py:503
  76.8 10.7 %collective-permute-start.14 = (bf16[256,768]{1,0:T(8,128)(2,1)S(1)}, bf16[256,768]{1,0:T(8,128)(2,1)S(1)}, u32[]{:S(2)}, u32[]{:S(2)}) collective-permute-start(bf16[256,768]{1,0:T(8,128)(2,1)S(1)} %get-tuple-element.49), channel_id=1, source_target_pairs={{0,3},{1,0},{2,1},{3,2},{4,7},{5,4},{6,5},{7,6},{8,11},{9,8},{10,9... | collective-permute-start | bytes 1179656 | tf_op jit(solution)/shard_map/ppermute | solution.py:503
  78.3 17.6 %collective-permute-start.7 = (bf16[256,768]{1,0:T(8,128)(2,1)S(1)}, bf16[256,768]{1,0:T(8,128)(2,1)S(1)}, u32[]{:S(2)}, u32[]{:S(2)}) collective-permute-start(bf16[256,768]{1,0:T(8,128)(2,1)S(1)} %get-tuple-element.52), channel_id=1, source_target_pairs={{0,1},{1,2},{2,3},{3,0},{4,5},{5,6},{6,7},{7,4},{8,9},{9,10},{10,1... | collective-permute-start | bytes 1179656 | tf_op jit(solution)/shard_map/ppermute | solution.py:503
  78.3 17.6 %collective-permute-start.8 = (bf16[256,768]{1,0:T(8,128)(2,1)S(1)}, bf16[256,768]{1,0:T(8,128)(2,1)S(1)}, u32[]{:S(2)}, u32[]{:S(2)}) collective-permute-start(bf16[256,768]{1,0:T(8,128)(2,1)S(1)} %get-tuple-element.50), channel_id=1, source_target_pairs={{0,3},{1,0},{2,1},{3,2},{4,7},{5,4},{6,5},{7,6},{8,11},{9,8},{10,9... | collective-permute-start | bytes 1179656 | tf_op jit(solution)/shard_map/ppermute | solution.py:503

commit v5 on v4

--- a/solution.py
+++ b/solution.py
@@ -323,16 +323,19 @@
 def attend_kernel(early, rows, *refs):
     inputs, out, rest = refs[:7], refs[7], refs[8:]
     held, (state0, state1, sems, out_sems) = rest[:7], rest[7:]
-    copies = fetch(list(zip(inputs, held)), sems)
+    pairs = list(zip(inputs[:5], held[:5]))
+    for part in (slice(0, early), slice(early, None)):
+        pairs += [(source.at[part], target.at[part]) for source, target in zip(inputs[5:], held[5:])]
+    copies = fetch(pairs, sems)
     for copy in copies[:5]:
         copy.wait()
     codes, raw, made = held[0], held[5], held[6]
     count, width = made.shape[0], made.shape[1] // 3
     enter_states(float(early), rows, *held[:5], state0, state1)
-    for copy in copies[5:]:
-        copy.wait()
     written = []
     for i, (low, high, state) in enumerate(((0, early, state0), (early, count, state1))):
+        for copy in copies[5 + 2 * i : 7 + 2 * i]:
+            copy.wait()
         where = lax.broadcasted_iota(jnp.int32, (high - low, HDIM), 0).astype(f32)
         for head in range(width // HDIM):
             rate = jnp.exp2(-0.5 * codes[head : head + 1, :].astype(f32))
@@ -359,7 +362,7 @@
         in_specs=[anywhere] * 7,
         out_specs=anywhere,
         scratch_shapes=[pltpu.VMEM(a.shape, a.dtype) for a in operands]
-        + [state, state, pltpu.SemaphoreType.DMA((7,)), pltpu.SemaphoreType.DMA((2,))],
+        + [state, state, pltpu.SemaphoreType.DMA((9,)), pltpu.SemaphoreType.DMA((2,))],
         compiler_params=pltpu.CompilerParams(vmem_limit_bytes=VMEM_ALL),
         cost_estimate=LIGHT,
         name="attend",
@@ -438,12 +441,13 @@
 
 
 def others_kernel(spans, cores, *refs):
+    z, x, c = spot()
     parts, refs = refs[: len(spans)], refs[len(spans) :]
     tables, (partial, out) = refs[: len(cores)], refs[len(cores) :]
     for table, inside, at in column_tiles(tables, cores):
         total = partial[:, at].astype(f32)
         for (src, _), part in zip(spans, parts):
-            total = total + nt(part[...], table[src - 1, inside])
+            total = total + nt(part[...], table[jnp.where(c == 1, src - 1, 2 - src), inside])
         out[:, at] = total.astype(bf16)
 
 
@@ -501,6 +505,15 @@
 
 def turn(a, by):
     return lax.ppermute(a, "head", [(i, (i + by) % 4) for i in range(4)])
+
+
+def swing(a, by):
+    pairs = []
+    for seq in range(32):
+        for y in range(4):
+            to = (y + (by if seq % 2 == 1 else -by)) % 4
+            pairs.append((seq * 4 + y, seq * 4 + to))
+    return lax.ppermute(a, ("seq", "head"), pairs)
 
 
 def move(a, where):
@@ -539,20 +552,20 @@
     theirs = across(chip_state)
     done = attend(EARLY, rows, codes, chip_state, theirs, other, local, raw, made)
     done, *share = tie(done, *share)
-    left, right = turn(done, 1), turn(done, -1)
+    former, latter = swing(done, 1), swing(done, -1)
     total = project_own(done, weights)
-    left, right, total = tie(left, right, total)
+    former, latter, total = tie(former, latter, total)
     share = jnp.stack(share)
     half = [share] + [major(share, by) for by in (1, 2, 3)]
-    half, _, _ = tie(half, left, right)
+    half, _, _ = tie(half, former, latter)
     half = arrange(half)
     other_half = across(half)
     far = []
     for start in range(0, count // 2, CHUNK):
-        far.append((3, start, turn(left[start : start + CHUNK], 1)))
+        far.append((3, start, swing(former[start : start + CHUNK], 1)))
         start += count // 2
-        far.append((3, start, turn(right[start : start + CHUNK], -1)))
-    sides = (1, 0, left), (2, 0, right)
+        far.append((3, start, swing(latter[start : start + CHUNK], -1)))
+    sides = (1, 0, former), (2, 0, latter)
     total = project_others(sides, (half,), (False,), total)
     total = project_others(sides, (other_half,), (True,), total)
     out = None

time: 98.8 us -> 97.9 us (level)
    ppermute x9 -> x3, waiting for transfers between devices: 23.3 us -> 0.01 us  [turn(): return lax.ppermute(a, 'head', [(i, (i + by) % 4) for i in range(4)])]
    ppermute x0 -> x6, waiting for transfers between devices: none -> 23 us  [swing(): return lax.ppermute(a, ('seq', 'head'), pairs)]
    ppermute x0 -> x6, starting transfers between devices: none -> 8.48 us  [swing(): return lax.ppermute(a, ('seq', 'head'), pairs)]
    ppermute x9 -> x3, starting transfers between devices: 12.9 us -> 4.45 us  [turn(): return lax.ppermute(a, 'head', [(i, (i + by) % 4) for i in range(4)])]
  transfers between devices with their start and end apart: 16 -> 16, of which waited for: 6 -> 8; matrix products, arithmetic and copies ran while one was open for 0% -> 0% of each run, Pallas kernels for 26% -> 26%
where the time goes in v5:
time: 97.9 us; the launch traced here: 97.5 us
  Pallas kernels  34.3 us (35%)
  starting transfers between devices  29 us (30%)
  waiting for transfers between devices  25.3 us (26%)
  local copies, waits for them, and re-layouts  8.45 us (9%)
    ppermute x6, waiting for transfers between devices, swing(): return lax.ppermute(a, ('seq', 'head'), pairs)  23 us
    ppermute x6, starting transfers between devices, swing(): return lax.ppermute(a, ('seq', 'head'), pairs)  8.48 us
    unnamed x16, local copies, waits for them, and re-layouts  8.34 us
    ppermute x6, starting transfers between devices, move(): return lax.ppermute(a, 'seq', pairs)  8.34 us
    all_to_all x1, starting transfers between devices, shards(): arrived = lax.all_to_all(leaving, 'seq', 0, 0, axis_index_groups=CHIPS)  7.69 us
    pallas_call x1, Pallas kernels, project_own(): pl.pallas_call(own_kernel, out_shape=spec(rows, cols), in_specs=whole(1)...  7.14 us
    pallas_call x1, Pallas kernels, inside(): pl.pallas_call(functools.partial(inside_kernel, early), out_shape=spec(co...  6.11 us
    pallas_call x2, Pallas kernels, project_others(): pl.pallas_call(functools.partial(others_kernel, spans, mirrored), out_sha...  5.35 us
  transfers between devices with their start and end apart: 16, of which 8 were waited for; matrix products, arithmetic and copies ran while one was open for 0% of the time, Pallas kernels for 26%

profile of v5, /device:TPU:1, one launch (start us, length us, event | category | flops | bytes accessed | tf_op | source)
XLA Modules:
  0.0 97.5 jit_solution(14473265552728079020)
XLA Ops:
  0.0 4.4 %begin.1 = (bf16[1024,1024]{1,0:T(8,128)(2,1)}, bf16[16,128]{1,0:T(8,128)(2,1)}, f32[2,2,2,128,128]{4,3,2,1,0:T(8,128)}, bf16[2,2,128,128]{3,2,1,0:T(8,128)(2,1)...) custom-call(bf16[1024,256]{1,0:T(8,128)(2,1)} %q.1, bf16[1024,256]{1,0:T(8,128)(2,1)} %k.1, ...), custom_call_target="tpu_custom_call" | custom-call | flops 1 | bytes 1 | tf_op jit(solution)/shard_map/begin/pallas_call | solution.py:110
  4.4 1.5 %collective-permute-start = (bf16[2,2,128,128]{3,2,1,0:T(8,128)(2,1)}, bf16[2,2,128,128]{3,2,1,0:T(8,128)(2,1)S(1)}, u32[]{:S(2)}, u32[]{:S(2)}) collective-permute-start(bf16[2,2,128,128]{3,2,1,0:T(8,128)(2,1)} %get-tuple-element.28.mine_at), channel_id=1, source_target_pairs={{0,4},{4,0},{8,12},{12,8},{16,20},{20,16},{24,28},{28,24},{32,36},... | collective-permute-start | bytes 393224 | tf_op jit(solution)/shard_map/ppermute | solution.py:521
  5.9 1.2 %collective-permute-done.other_at.refs_3_ = bf16[2,2,128,128]{3,2,1,0:T(8,128)(2,1)S(1)} collective-permute-done((bf16[2,2,128,128]{3,2,1,0:T(8,128)(2,1)}, bf16[2,2,128,128]{3,2,1,0:T(8,128)(2,1)S(1)}, u32[]{:S(2)}, u32[]{:S(2)}) %collective-permute-start) | collective-permute-done | bytes 131104 | tf_op jit(solution)/shard_map/ppermute | solution.py:521
  7.7 1.9 %join.1 = bf16[16,1,128,128]{3,2,1,0:T(8,128)(2,1)} custom-call(bf16[16,128]{1,0:T(8,128)(2,1)} %get-tuple-element.30.codes_at.refs_0_, bf16[2,2,128,128]{3,2,1,0:T(8,128)(2,1)} %get-tuple-element.28.mine_at, bf16[2,2,128,128]{3,2,1,0:T(8,128)(2,1)} %copy-done.6), custom_call_target="tpu_custom_call" | custom-call | flops 1 | bytes 1 | tf_op jit(solution)/shard_map/join/pallas_call | solution.py:163
  9.7 7.7 %all-to-all-start = ((bf16[16,1,128,128]{3,2,1,0:T(8,128)(2,1)}), bf16[16,1,128,128]{3,2,1,0:T(8,128)(2,1)S(1)}, u32[]{:S(2)}, u32[]{:S(2)}) async-start(bf16[16,1,128,128]{3,2,1,0:T(8,128)(2,1)} %join.1), calls=%async_computation | async-start | bytes 1048576 | tf_op jit(solution)/shard_map/all_to_all | solution.py:548
  17.4 1.4 %collective-permute-start.2 = (bf16[192,768]{1,0:T(8,128)(2,1)}, bf16[192,768]{1,0:T(8,128)(2,1)S(1)}, u32[]{:S(2)}, u32[]{:S(2)}) collective-permute-start(bf16[192,768]{1,0:T(8,128)(2,1)} %get-tuple-element.35), channel_id=1, source_target_pairs={{0,1},{1,2},{2,3},{3,0},{4,5},{5,6},{6,7},{7,4},{8,9},{9,10},{10,1... | collective-permute-start | bytes 884744 | tf_op jit(solution)/shard_map/ppermute | solution.py:507
  18.8 1.5 %collective-permute-start.3 = (bf16[192,768]{1,0:T(8,128)(2,1)}, bf16[192,768]{1,0:T(8,128)(2,1)S(1)}, u32[]{:S(2)}, u32[]{:S(2)}) collective-permute-start(bf16[192,768]{1,0:T(8,128)(2,1)} %get-tuple-element.36), channel_id=1, source_target_pairs={{0,3},{1,0},{2,1},{3,2},{4,7},{5,4},{6,5},{7,6},{8,11},{9,8},{10,9... | collective-permute-start | bytes 884744 | tf_op jit(solution)/shard_map/ppermute | solution.py:507
  20.3 1.6 %collective-permute-start.4 = (bf16[192,768]{1,0:T(8,128)(2,1)}, bf16[192,768]{1,0:T(8,128)(2,1)S(1)}, u32[]{:S(2)}, u32[]{:S(2)}) collective-permute-start(bf16[192,768]{1,0:T(8,128)(2,1)} %get-tuple-element.37), channel_id=1, source_target_pairs={{0,2},{1,3},{2,0},{3,1},{4,6},{5,7},{6,4},{7,5},{8,10},{9,11},{10,... | collective-permute-start | bytes 884744 | tf_op jit(solution)/shard_map/ppermute | solution.py:507
  21.8 6.1 %inside.1.refs_6_ = bf16[1024,768]{1,0:T(8,128)(2,1)} custom-call(bf16[16,128]{1,0:T(8,128)(2,1)} %get-tuple-element.30.codes_at.refs_0_, bf16[1024,1024]{1,0:T(8,128)(2,1)} %get-tuple-element.31.raw_at.refs_5_), custom_call_target="tpu_custom_call" | custom-call | flops 1 | bytes 1 | tf_op jit(solution)/shard_map/inside/pallas_call | solution.py:305
  28.9 1.8 %collective-permute-start.1 = (bf16[2,128,128]{2,1,0:T(8,128)(2,1)S(1)}, bf16[2,128,128]{2,1,0:T(8,128)(2,1)S(1)}, u32[]{:S(2)}, u32[]{:S(2)}) collective-permute-start(bf16[2,128,128]{2,1,0:T(8,128)(2,1)S(1)} %gather.1.refs_1_), channel_id=1, source_target_pairs={{0,4},{4,0},{8,12},{12,8},{16,20},{20,16},{24,28},{28,24},{32,36},... | collective-permute-start | bytes 196616 | tf_op jit(solution)/shard_map/ppermute | solution.py:521
  30.8 0.9 collective-permute-done.1.refs_2_
  32.3 3.8 %attend.1.done = bf16[1024,768]{1,0:T(8,128)(2,1)} custom-call(bf16[16,128]{1,0:T(8,128)(2,1)} %get-tuple-element.30.codes_at.refs_0_, bf16[2,128,128]{2,1,0:T(8,128)(2,1)} %copy-done.4, bf16[2,128,128]{2,1,0:T(8,128)(2,1)} %copy-done.7, bf16[2,2,128,128]{3,2,1,0:T(8,128)(2,1)} %copy-done.6, f32[2,2,2,128,128]{4,3,2,1,0:T(8,128)} %get-tuple-element.33.refs_4_, ...), custom_call_target="tpu_custom_call" | custom-call | flops 1 | bytes 1 | tf_op jit(solution)/shard_map/attend/pallas_call | solution.py:359
  36.2 1.4 %collective-permute-start.5 = (bf16[1024,768]{1,0:T(8,128)(2,1)}, bf16[1024,768]{1,0:T(8,128)(2,1)S(1)}, u32[]{:S(2)}, u32[]{:S(2)}) collective-permute-start(bf16[1024,768]{1,0:T(8,128)(2,1)} %attend.1.done), channel_id=1, source_target_pairs={{0,3},{1,0},{2,1},{3,2},{4,5},{5,6},{6,7},{7,4},{8,11},{9,8},{10,9... | collective-permute-start | bytes 4718600 | tf_op jit(solution)/shard_map/ppermute | solution.py:516
  37.5 1.5 %collective-permute-start.6 = (bf16[1024,768]{1,0:T(8,128)(2,1)}, bf16[1024,768]{1,0:T(8,128)(2,1)S(1)}, u32[]{:S(2)}, u32[]{:S(2)}) collective-permute-start(bf16[1024,768]{1,0:T(8,128)(2,1)} %attend.1.done), channel_id=1, source_target_pairs={{0,1},{1,2},{2,3},{3,0},{4,7},{5,4},{6,5},{7,6},{8,9},{9,10},{10,1... | collective-permute-start | bytes 4718600 | tf_op jit(solution)/shard_map/ppermute | solution.py:516
  39.1 2.6 %collective-permute-start.10 = (bf16[3,192,768]{2,1,0:T(8,128)(2,1)S(1)}, bf16[3,192,768]{2,1,0:T(8,128)(2,1)S(1)}, u32[]{:S(2)}, u32[]{:S(2)}) collective-permute-start(bf16[3,192,768]{2,1,0:T(8,128)(2,1)S(1)} %pad_maximum_fusion.refs_0_), channel_id=1, source_target_pairs={{0,64},{4,20},{8,72},{12,28},{16,80},{20,4},{24,88},{28,12},{32,96... | collective-permute-start | bytes 2654216 | tf_op jit(solution)/shard_map/ppermute | solution.py:521
  41.7 0.9 collective-permute-start.11
  43.2 1.9 %copy-done = bf16[6144,256]{1,0:T(8,128)(2,1)S(1)} copy-done((bf16[6144,256]{1,0:T(8,128)(2,1)S(1)}, bf16[6144,256]{1,0:T(8,128)(2,1)}, u32[]{:S(2)}) %copy-start) | copy-done | bytes 3145752
  45.1 1.9 %copy-done.1 = bf16[6144,256]{1,0:T(8,128)(2,1)S(1)} copy-done((bf16[6144,256]{1,0:T(8,128)(2,1)S(1)}, bf16[6144,256]{1,0:T(8,128)(2,1)}, u32[]{:S(2)}) %copy-start.1) | copy-done | bytes 3145752
  47.0 1.9 %copy-done.2 = bf16[6144,256]{1,0:T(8,128)(2,1)S(1)} copy-done((bf16[6144,256]{1,0:T(8,128)(2,1)S(1)}, bf16[6144,256]{1,0:T(8,128)(2,1)}, u32[]{:S(2)}) %copy-start.2) | copy-done | bytes 3145752
  48.9 1.4 %copy-done.3 = bf16[1024,768]{1,0:T(8,128)(2,1)S(1)} copy-done((bf16[1024,768]{1,0:T(8,128)(2,1)S(1)}, bf16[1024,768]{1,0:T(8,128)(2,1)}, u32[]{:S(2)}) %copy-start.3) | copy-done | bytes 1572888
  50.3 7.1 %project_own.1.refs_3_ = bf16[1024,1536]{1,0:T(8,128)(2,1)S(1)} custom-call(bf16[1024,768]{1,0:T(8,128)(2,1)S(1)} %copy-done.3, bf16[6144,256]{1,0:T(8,128)(2,1)S(1)} %copy-done, bf16[6144,256]{1,0:T(8,128)(2,1)S(1)} %copy-done.1, bf16[6144,256]{1,0:T(8,128)(2,1)S(1)} %copy-done.2), custom_call_target="tpu_custom_call" | custom-call | flops 1 | bytes 1 | tf_op jit(solution)/shard_map/project_own/pallas_call | solution.py:398
  57.4 12.8 %collective-permute-done.5.refs_0_ = bf16[1024,768]{1,0:T(8,128)(2,1)S(1)} collective-permute-done((bf16[1024,768]{1,0:T(8,128)(2,1)}, bf16[1024,768]{1,0:T(8,128)(2,1)S(1)}, u32[]{:S(2)}, u32[]{:S(2)}) %collective-permute-start.5) | collective-permute-done | bytes 1572896 | tf_op jit(solution)/shard_map/ppermute | solution.py:516
  70.3 3.4 %collective-permute-done.6.refs_1_ = bf16[1024,768]{1,0:T(8,128)(2,1)S(1)} collective-permute-done((bf16[1024,768]{1,0:T(8,128)(2,1)}, bf16[1024,768]{1,0:T(8,128)(2,1)S(1)}, u32[]{:S(2)}, u32[]{:S(2)}) %collective-permute-start.6) | collective-permute-done | bytes 1572896 | tf_op jit(solution)/shard_map/ppermute | solution.py:516
  73.9 0.9 collective-permute-start.12
  75.5 2.4 %collective-permute-start.14 = (bf16[256,768]{1,0:T(8,128)(2,1)S(1)}, bf16[256,768]{1,0:T(8,128)(2,1)S(1)}, u32[]{:S(2)}, u32[]{:S(2)}) collective-permute-start(bf16[256,768]{1,0:T(8,128)(2,1)S(1)} %get-tuple-element.49), channel_id=1, source_target_pairs={{0,1},{1,2},{2,3},{3,0},{4,7},{5,4},{6,5},{7,6},{8,9},{9,10},{10,1... | collective-permute-start | bytes 1179656 | tf_op jit(solution)/shard_map/ppermute | solution.py:516
  77.9 2.7 %collective-permute-start.8 = (bf16[256,768]{1,0:T(8,128)(2,1)S(1)}, bf16[256,768]{1,0:T(8,128)(2,1)S(1)}, u32[]{:S(2)}, u32[]{:S(2)}) collective-permute-start(bf16[256,768]{1,0:T(8,128)(2,1)S(1)} %get-tuple-element.50), channel_id=1, source_target_pairs={{0,1},{1,2},{2,3},{3,0},{4,7},{5,4},{6,5},{7,6},{8,9},{9,10},{10,1... | collective-permute-start | bytes 1179656 | tf_op jit(solution)/shard_map/ppermute | solution.py:516
  80.6 2.7 %project_others.2.refs_3_ = bf16[1024,1536]{1,0:T(8,128)(2,1)S(1)} custom-call(bf16[1024,768]{1,0:T(8,128)(2,1)S(1)} %collective-permute-done.5.refs_0_, bf16[1024,768]{1,0:T(8,128)(2,1)S(1)} %collective-permute-done.6.refs_1_, bf16[3,768,768]{2,1,0:T(8,128)(2,1)S(1)} %arrange.1.refs_2_, ...), custom_call_target="tpu_custom_call", output_to_operand_aliasing={{}: (3, {})} | custom-call | flops 1 | bytes 1 | tf_op jit(solution)/shard_map/project_others/pallas_call | solution.py:457
  83.3 2.7 %project_others.3.refs_4_ = bf16[1024,1536]{1,0:T(8,128)(2,1)S(1)} custom-call(bf16[1024,768]{1,0:T(8,128)(2,1)S(1)} %collective-permute-done.5.refs_0_, bf16[1024,768]{1,0:T(8,128)(2,1)S(1)} %collective-permute-done.6.refs_1_, bf16[3,768,768]{2,1,0:T(8,128)(2,1)S(1)} %collective-permute-done.12.refs_2_.refs_3_, ...), custom_call_target="tpu_custom_call", output_to_operand_aliasing={{}: (3, {})} | custom-call | flops 1 | bytes 1 | tf_op jit(solution)/shard_map/project_others/pallas_call | solution.py:457
  86.7 2.3 %project_last.2.refs_5_ = bf16[1024,1536]{1,0:T(8,128)(2,1)} custom-call(bf16[256,768]{1,0:T(8,128)(2,1)S(1)} %collective-permute-done.13.refs_0_, bf16[256,768]{1,0:T(8,128)(2,1)S(1)} %collective-permute-done.14.refs_1_, bf16[3,768,768]{2,1,0:T(8,128)(2,1)S(1)} %arrange.1.refs_2_, bf16[3,768,768]{2,1,0:T(8,128)(2,1)S(1)} %collective-permute-done.12.refs_2_.refs_3_, ...), custom_call_target="tpu_custom_call" | custom-call | flops 1 | bytes 1 | tf_op jit(solution)/shard_map/project_last/pallas_call | solution.py:493
  89.0 3.2 %collective-permute-done.7.refs_0_ = bf16[256,768]{1,0:T(8,128)(2,1)S(1)} collective-permute-done((bf16[256,768]{1,0:T(8,128)(2,1)S(1)}, bf16[256,768]{1,0:T(8,128)(2,1)S(1)}, u32[]{:S(2)}, u32[]{:S(2)}) %collective-permute-start.7) | collective-permute-done | bytes 393248 | tf_op jit(solution)/shard_map/ppermute | solution.py:516
  92.2 2.8 %collective-permute-done.8.refs_1_ = bf16[256,768]{1,0:T(8,128)(2,1)S(1)} collective-permute-done((bf16[256,768]{1,0:T(8,128)(2,1)S(1)}, bf16[256,768]{1,0:T(8,128)(2,1)S(1)}, u32[]{:S(2)}, u32[]{:S(2)}) %collective-permute-start.8) | collective-permute-done | bytes 393248 | tf_op jit(solution)/shard_map/ppermute | solution.py:516
  95.0 2.3 %project_last.3 = bf16[1024,1536]{1,0:T(8,128)(2,1)} custom-call(bf16[256,768]{1,0:T(8,128)(2,1)S(1)} %collective-permute-done.7.refs_0_, bf16[256,768]{1,0:T(8,128)(2,1)S(1)} %collective-permute-done.8.refs_1_, bf16[3,768,768]{2,1,0:T(8,128)(2,1)S(1)} %arrange.1.refs_2_, ...), custom_call_target="tpu_custom_call", output_to_operand_aliasing={{}: (5, {})} | custom-call | flops 1 | bytes 1 | tf_op jit(solution)/shard_map/project_last/pallas_call | solution.py:493
  (30 shorter events, 4.6 us)
Async XLA Ops:
  4.4 23.7 %copy-start.5 = (s32[2]{0:T(128)S(1)}, s32[2]{0:T(128)}, u32[]{:S(2)}) copy-start(s32[2]{0:T(128)} %decay_code.3) | copy-start | bytes 28
  4.4 2.7 %collective-permute-start = (bf16[2,2,128,128]{3,2,1,0:T(8,128)(2,1)}, bf16[2,2,128,128]{3,2,1,0:T(8,128)(2,1)S(1)}, u32[]{:S(2)}, u32[]{:S(2)}) collective-permute-start(bf16[2,2,128,128]{3,2,1,0:T(8,128)(2,1)} %get-tuple-element.28.mine_at), channel_id=1, source_target_pairs={{0,4},{4,0},{8,12},{12,8},{16,20},{20,16},{24,28},{28,24},{32,36},... | collective-permute-start | bytes 393224 | tf_op jit(solution)/shard_map/ppermute | solution.py:521
  7.1 0.6 copy-start.6
  9.7 18.4 %all-to-all-start = ((bf16[16,1,128,128]{3,2,1,0:T(8,128)(2,1)}), bf16[16,1,128,128]{3,2,1,0:T(8,128)(2,1)S(1)}, u32[]{:S(2)}, u32[]{:S(2)}) async-start(bf16[16,1,128,128]{3,2,1,0:T(8,128)(2,1)} %join.1), calls=%async_computation | async-start | bytes 1048576 | tf_op jit(solution)/shard_map/all_to_all | solution.py:548
  17.4 18.7 %collective-permute-start.2 = (bf16[192,768]{1,0:T(8,128)(2,1)}, bf16[192,768]{1,0:T(8,128)(2,1)S(1)}, u32[]{:S(2)}, u32[]{:S(2)}) collective-permute-start(bf16[192,768]{1,0:T(8,128)(2,1)} %get-tuple-element.35), channel_id=1, source_target_pairs={{0,1},{1,2},{2,3},{3,0},{4,5},{5,6},{6,7},{7,4},{8,9},{9,10},{10,1... | collective-permute-start | bytes 884744 | tf_op jit(solution)/shard_map/ppermute | solution.py:507
  18.8 17.4 %collective-permute-start.3 = (bf16[192,768]{1,0:T(8,128)(2,1)}, bf16[192,768]{1,0:T(8,128)(2,1)S(1)}, u32[]{:S(2)}, u32[]{:S(2)}) collective-permute-start(bf16[192,768]{1,0:T(8,128)(2,1)} %get-tuple-element.36), channel_id=1, source_target_pairs={{0,3},{1,0},{2,1},{3,2},{4,7},{5,4},{6,5},{7,6},{8,11},{9,8},{10,9... | collective-permute-start | bytes 884744 | tf_op jit(solution)/shard_map/ppermute | solution.py:507
  20.3 15.9 %collective-permute-start.4 = (bf16[192,768]{1,0:T(8,128)(2,1)}, bf16[192,768]{1,0:T(8,128)(2,1)S(1)}, u32[]{:S(2)}, u32[]{:S(2)}) collective-permute-start(bf16[192,768]{1,0:T(8,128)(2,1)} %get-tuple-element.37), channel_id=1, source_target_pairs={{0,2},{1,3},{2,0},{3,1},{4,6},{5,7},{6,4},{7,5},{8,10},{9,11},{10,... | collective-permute-start | bytes 884744 | tf_op jit(solution)/shard_map/ppermute | solution.py:507
  28.9 2.8 %copy-start.4 = (bf16[2,128,128]{2,1,0:T(8,128)(2,1)}, bf16[2,128,128]{2,1,0:T(8,128)(2,1)S(1)}, u32[]{:S(2)}) copy-start(bf16[2,128,128]{2,1,0:T(8,128)(2,1)S(1)} %gather.1.refs_1_) | copy-start | bytes 196612
  28.9 2.7 %collective-permute-start.1 = (bf16[2,128,128]{2,1,0:T(8,128)(2,1)S(1)}, bf16[2,128,128]{2,1,0:T(8,128)(2,1)S(1)}, u32[]{:S(2)}, u32[]{:S(2)}) collective-permute-start(bf16[2,128,128]{2,1,0:T(8,128)(2,1)S(1)} %gather.1.refs_1_), channel_id=1, source_target_pairs={{0,4},{4,0},{8,12},{12,8},{16,20},{20,16},{24,28},{28,24},{32,36},... | collective-permute-start | bytes 196616 | tf_op jit(solution)/shard_map/ppermute | solution.py:521
  31.7 0.6 copy-start.7
  36.2 34.1 %collective-permute-start.5 = (bf16[1024,768]{1,0:T(8,128)(2,1)}, bf16[1024,768]{1,0:T(8,128)(2,1)S(1)}, u32[]{:S(2)}, u32[]{:S(2)}) collective-permute-start(bf16[1024,768]{1,0:T(8,128)(2,1)} %attend.1.done), channel_id=1, source_target_pairs={{0,3},{1,0},{2,1},{3,2},{4,5},{5,6},{6,7},{7,4},{8,11},{9,8},{10,9... | collective-permute-start | bytes 4718600 | tf_op jit(solution)/shard_map/ppermute | solution.py:516
  37.5 36.1 %collective-permute-start.6 = (bf16[1024,768]{1,0:T(8,128)(2,1)}, bf16[1024,768]{1,0:T(8,128)(2,1)S(1)}, u32[]{:S(2)}, u32[]{:S(2)}) collective-permute-start(bf16[1024,768]{1,0:T(8,128)(2,1)} %attend.1.done), channel_id=1, source_target_pairs={{0,1},{1,2},{2,3},{3,0},{4,7},{5,4},{6,5},{7,6},{8,9},{9,10},{10,1... | collective-permute-start | bytes 4718600 | tf_op jit(solution)/shard_map/ppermute | solution.py:516
  39.1 34.5 %collective-permute-start.10 = (bf16[3,192,768]{2,1,0:T(8,128)(2,1)S(1)}, bf16[3,192,768]{2,1,0:T(8,128)(2,1)S(1)}, u32[]{:S(2)}, u32[]{:S(2)}) collective-permute-start(bf16[3,192,768]{2,1,0:T(8,128)(2,1)S(1)} %pad_maximum_fusion.refs_0_), channel_id=1, source_target_pairs={{0,64},{4,20},{8,72},{12,28},{16,80},{20,4},{24,88},{28,12},{32,96... | collective-permute-start | bytes 2654216 | tf_op jit(solution)/shard_map/ppermute | solution.py:521
  41.7 31.9 %collective-permute-start.11 = (bf16[3,192,768]{2,1,0:T(8,128)(2,1)S(1)}, bf16[3,192,768]{2,1,0:T(8,128)(2,1)S(1)}, u32[]{:S(2)}, u32[]{:S(2)}) collective-permute-start(bf16[3,192,768]{2,1,0:T(8,128)(2,1)S(1)} %pad_maximum_fusion.refs_0_), channel_id=1, source_target_pairs={{0,96},{4,28},{8,104},{12,4},{16,112},{20,12},{24,120},{28,20},{32... | collective-permute-start | bytes 2654216 | tf_op jit(solution)/shard_map/ppermute | solution.py:521
  42.6 31.0 %collective-permute-start.9 = (bf16[3,192,768]{2,1,0:T(8,128)(2,1)S(1)}, bf16[3,192,768]{2,1,0:T(8,128)(2,1)S(1)}, u32[]{:S(2)}, u32[]{:S(2)}) collective-permute-start(bf16[3,192,768]{2,1,0:T(8,128)(2,1)S(1)} %pad_maximum_fusion.refs_0_), channel_id=1, source_target_pairs={{0,32},{4,12},{8,40},{12,20},{16,48},{20,28},{24,56},{28,4},{32,64... | collective-permute-start | bytes 2654216 | tf_op jit(solution)/shard_map/ppermute | solution.py:521
  43.2 1.9 %copy-start = (bf16[6144,256]{1,0:T(8,128)(2,1)S(1)}, bf16[6144,256]{1,0:T(8,128)(2,1)}, u32[]{:S(2)}) copy-start(bf16[6144,256]{1,0:T(8,128)(2,1)} %wq.1) | copy-start | bytes 9437188
  45.1 1.9 %copy-start.1 = (bf16[6144,256]{1,0:T(8,128)(2,1)S(1)}, bf16[6144,256]{1,0:T(8,128)(2,1)}, u32[]{:S(2)}) copy-start(bf16[6144,256]{1,0:T(8,128)(2,1)} %wk.1) | copy-start | bytes 9437188
  47.0 1.9 %copy-start.2 = (bf16[6144,256]{1,0:T(8,128)(2,1)S(1)}, bf16[6144,256]{1,0:T(8,128)(2,1)}, u32[]{:S(2)}) copy-start(bf16[6144,256]{1,0:T(8,128)(2,1)} %wv.1) | copy-start | bytes 9437188
  48.9 1.4 %copy-start.3 = (bf16[1024,768]{1,0:T(8,128)(2,1)S(1)}, bf16[1024,768]{1,0:T(8,128)(2,1)}, u32[]{:S(2)}) copy-start(bf16[1024,768]{1,0:T(8,128)(2,1)} %attend.1.done) | copy-start | bytes 4718596
  73.9 9.3 %collective-permute-start.12 = (bf16[3,768,768]{2,1,0:T(8,128)(2,1)S(1)}, bf16[3,768,768]{2,1,0:T(8,128)(2,1)S(1)}, u32[]{:S(2)}, u32[]{:S(2)}) collective-permute-start(bf16[3,768,768]{2,1,0:T(8,128)(2,1)S(1)} %arrange.1.refs_2_), channel_id=1, source_target_pairs={{0,4},{4,0},{8,12},{12,8},{16,20},{20,16},{24,28},{28,24},{32,36},... | collective-permute-start | bytes 10616840 | tf_op jit(solution)/shard_map/ppermute | solution.py:521
  74.9 11.0 %collective-permute-start.13 = (bf16[256,768]{1,0:T(8,128)(2,1)S(1)}, bf16[256,768]{1,0:T(8,128)(2,1)S(1)}, u32[]{:S(2)}, u32[]{:S(2)}) collective-permute-start(bf16[256,768]{1,0:T(8,128)(2,1)S(1)} %get-tuple-element.51), channel_id=1, source_target_pairs={{0,3},{1,0},{2,1},{3,2},{4,5},{5,6},{6,7},{7,4},{8,11},{9,8},{10,9... | collective-permute-start | bytes 1179656 | tf_op jit(solution)/shard_map/ppermute | solution.py:516
  75.5 11.3 %collective-permute-start.14 = (bf16[256,768]{1,0:T(8,128)(2,1)S(1)}, bf16[256,768]{1,0:T(8,128)(2,1)S(1)}, u32[]{:S(2)}, u32[]{:S(2)}) collective-permute-start(bf16[256,768]{1,0:T(8,128)(2,1)S(1)} %get-tuple-element.49), channel_id=1, source_target_pairs={{0,1},{1,2},{2,3},{3,0},{4,7},{5,4},{6,5},{7,6},{8,9},{9,10},{10,1... | collective-permute-start | bytes 1179656 | tf_op jit(solution)/shard_map/ppermute | solution.py:516
  77.9 14.3 %collective-permute-start.7 = (bf16[256,768]{1,0:T(8,128)(2,1)S(1)}, bf16[256,768]{1,0:T(8,128)(2,1)S(1)}, u32[]{:S(2)}, u32[]{:S(2)}) collective-permute-start(bf16[256,768]{1,0:T(8,128)(2,1)S(1)} %get-tuple-element.52), channel_id=1, source_target_pairs={{0,3},{1,0},{2,1},{3,2},{4,5},{5,6},{6,7},{7,4},{8,11},{9,8},{10,9... | collective-permute-start | bytes 1179656 | tf_op jit(solution)/shard_map/ppermute | solution.py:516
  77.9 17.1 %collective-permute-start.8 = (bf16[256,768]{1,0:T(8,128)(2,1)S(1)}, bf16[256,768]{1,0:T(8,128)(2,1)S(1)}, u32[]{:S(2)}, u32[]{:S(2)}) collective-permute-start(bf16[256,768]{1,0:T(8,128)(2,1)S(1)} %get-tuple-element.50), channel_id=1, source_target_pairs={{0,1},{1,2},{2,3},{3,0},{4,7},{5,4},{6,5},{7,6},{8,9},{9,10},{10,1... | collective-permute-start | bytes 1179656 | tf_op jit(solution)/shard_map/ppermute | solution.py:516

commit v6 on v5

--- a/solution.py
+++ b/solution.py
@@ -324,22 +324,26 @@
     inputs, out, rest = refs[:7], refs[7], refs[8:]
     held, (state0, state1, sems, out_sems) = rest[:7], rest[7:]
     pairs = list(zip(inputs[:5], held[:5]))
-    for part in (slice(0, early), slice(early, None)):
+    count = held[6].shape[0]
+    for low in range(0, count, BLK):
+        part = slice(low, low + BLK)
         pairs += [(source.at[part], target.at[part]) for source, target in zip(inputs[5:], held[5:])]
     copies = fetch(pairs, sems)
     for copy in copies[:5]:
         copy.wait()
     codes, raw, made = held[0], held[5], held[6]
-    count, width = made.shape[0], made.shape[1] // 3
+    width = made.shape[1] // 3
     enter_states(float(early), rows, *held[:5], state0, state1)
     written = []
-    for i, (low, high, state) in enumerate(((0, early, state0), (early, count, state1))):
+    for i, low in enumerate(range(0, count, BLK)):
+        high = low + BLK
+        begins, ends, state = (0, early, state0) if high <= early else (early, count, state1)
         for copy in copies[5 + 2 * i : 7 + 2 * i]:
             copy.wait()
-        where = lax.broadcasted_iota(jnp.int32, (high - low, HDIM), 0).astype(f32)
+        where = lax.broadcasted_iota(jnp.int32, (BLK, HDIM), 0).astype(f32) + (low - begins)
         for head in range(width // HDIM):
             rate = jnp.exp2(-0.5 * codes[head : head + 1, :].astype(f32))
-            lead, lag = jnp.exp(-rate * (where + 1.0)), jnp.exp(-rate * (high - low - where))
+            lead, lag = jnp.exp(-rate * (where + 1.0)), jnp.exp(-rate * (ends - begins - where))
             k, v, g = (raw[low:high, part * width + head * HDIM : part * width + (head + 1) * HDIM] for part in (1, 2, 3))
             kv = state[head * HDIM : (head + 1) * HDIM, :]
             qg = state[width + head * HDIM : width + (head + 1) * HDIM, :]
@@ -362,7 +366,7 @@
         in_specs=[anywhere] * 7,
         out_specs=anywhere,
         scratch_shapes=[pltpu.VMEM(a.shape, a.dtype) for a in operands]
-        + [state, state, pltpu.SemaphoreType.DMA((9,)), pltpu.SemaphoreType.DMA((2,))],
+        + [state, state, pltpu.SemaphoreType.DMA((5 + 2 * (made.shape[0] // BLK),)), pltpu.SemaphoreType.DMA((made.shape[0] // BLK,))],
         compiler_params=pltpu.CompilerParams(vmem_limit_bytes=VMEM_ALL),
         cost_estimate=LIGHT,
         name="attend",

time: 97.9 us -> 97.6 us (level)
  no operation moved by 1% of the time
where the time goes in v6:
time: 97.6 us; the launch traced here: 97.2 us
  Pallas kernels  34 us (35%)
  starting transfers between devices  29 us (30%)
  waiting for transfers between devices  25.3 us (26%)
  local copies, waits for them, and re-layouts  8.45 us (9%)
    ppermute x6, waiting for transfers between devices, swing(): return lax.ppermute(a, ('seq', 'head'), pairs)  23 us
    ppermute x6, starting transfers between devices, swing(): return lax.ppermute(a, ('seq', 'head'), pairs)  8.49 us
    ppermute x6, starting transfers between devices, move(): return lax.ppermute(a, 'seq', pairs)  8.34 us
    unnamed x16, local copies, waits for them, and re-layouts  8.34 us
    all_to_all x1, starting transfers between devices, shards(): arrived = lax.all_to_all(leaving, 'seq', 0, 0, axis_index_groups=CHIPS)  7.69 us
    pallas_call x1, Pallas kernels, project_own(): pl.pallas_call(own_kernel, out_shape=spec(rows, cols), in_specs=whole(1)...  7.14 us
    pallas_call x1, Pallas kernels, inside(): pl.pallas_call(functools.partial(inside_kernel, early), out_shape=spec(co...  6.11 us
    pallas_call x2, Pallas kernels, project_others(): pl.pallas_call(functools.partial(others_kernel, spans, mirrored), out_sha...  5.35 us
  transfers between devices with their start and end apart: 16, of which 8 were waited for; matrix products, arithmetic and copies ran while one was open for 0% of the time, Pallas kernels for 26%

profile of v6, /device:TPU:1, one launch (start us, length us, event | category | flops | bytes accessed | tf_op | source)
XLA Modules:
  0.0 97.2 jit_solution(14049489393148912386)
XLA Ops:
  0.0 4.4 %begin.1 = (bf16[1024,1024]{1,0:T(8,128)(2,1)}, bf16[16,128]{1,0:T(8,128)(2,1)}, f32[2,2,2,128,128]{4,3,2,1,0:T(8,128)}, bf16[2,2,128,128]{3,2,1,0:T(8,128)(2,1)...) custom-call(bf16[1024,256]{1,0:T(8,128)(2,1)} %q.1, bf16[1024,256]{1,0:T(8,128)(2,1)} %k.1, ...), custom_call_target="tpu_custom_call" | custom-call | flops 1 | bytes 1 | tf_op jit(solution)/shard_map/begin/pallas_call | solution.py:110
  4.4 1.5 %collective-permute-start = (bf16[2,2,128,128]{3,2,1,0:T(8,128)(2,1)}, bf16[2,2,128,128]{3,2,1,0:T(8,128)(2,1)S(1)}, u32[]{:S(2)}, u32[]{:S(2)}) collective-permute-start(bf16[2,2,128,128]{3,2,1,0:T(8,128)(2,1)} %get-tuple-element.28.mine_at), channel_id=1, source_target_pairs={{0,4},{4,0},{8,12},{12,8},{16,20},{20,16},{24,28},{28,24},{32,36},... | collective-permute-start | bytes 393224 | tf_op jit(solution)/shard_map/ppermute | solution.py:525
  5.9 1.2 %collective-permute-done.other_at.refs_3_ = bf16[2,2,128,128]{3,2,1,0:T(8,128)(2,1)S(1)} collective-permute-done((bf16[2,2,128,128]{3,2,1,0:T(8,128)(2,1)}, bf16[2,2,128,128]{3,2,1,0:T(8,128)(2,1)S(1)}, u32[]{:S(2)}, u32[]{:S(2)}) %collective-permute-start) | collective-permute-done | bytes 131104 | tf_op jit(solution)/shard_map/ppermute | solution.py:525
  7.7 1.9 %join.1 = bf16[16,1,128,128]{3,2,1,0:T(8,128)(2,1)} custom-call(bf16[16,128]{1,0:T(8,128)(2,1)} %get-tuple-element.30.codes_at.refs_0_, bf16[2,2,128,128]{3,2,1,0:T(8,128)(2,1)} %get-tuple-element.28.mine_at, bf16[2,2,128,128]{3,2,1,0:T(8,128)(2,1)} %copy-done.6), custom_call_target="tpu_custom_call" | custom-call | flops 1 | bytes 1 | tf_op jit(solution)/shard_map/join/pallas_call | solution.py:163
  9.7 7.7 %all-to-all-start = ((bf16[16,1,128,128]{3,2,1,0:T(8,128)(2,1)}), bf16[16,1,128,128]{3,2,1,0:T(8,128)(2,1)S(1)}, u32[]{:S(2)}, u32[]{:S(2)}) async-start(bf16[16,1,128,128]{3,2,1,0:T(8,128)(2,1)} %join.1), calls=%async_computation | async-start | bytes 1048576 | tf_op jit(solution)/shard_map/all_to_all | solution.py:552
  17.4 1.4 %collective-permute-start.2 = (bf16[192,768]{1,0:T(8,128)(2,1)}, bf16[192,768]{1,0:T(8,128)(2,1)S(1)}, u32[]{:S(2)}, u32[]{:S(2)}) collective-permute-start(bf16[192,768]{1,0:T(8,128)(2,1)} %get-tuple-element.35), channel_id=1, source_target_pairs={{0,1},{1,2},{2,3},{3,0},{4,5},{5,6},{6,7},{7,4},{8,9},{9,10},{10,1... | collective-permute-start | bytes 884744 | tf_op jit(solution)/shard_map/ppermute | solution.py:511
  18.8 1.5 %collective-permute-start.3 = (bf16[192,768]{1,0:T(8,128)(2,1)}, bf16[192,768]{1,0:T(8,128)(2,1)S(1)}, u32[]{:S(2)}, u32[]{:S(2)}) collective-permute-start(bf16[192,768]{1,0:T(8,128)(2,1)} %get-tuple-element.36), channel_id=1, source_target_pairs={{0,3},{1,0},{2,1},{3,2},{4,7},{5,4},{6,5},{7,6},{8,11},{9,8},{10,9... | collective-permute-start | bytes 884744 | tf_op jit(solution)/shard_map/ppermute | solution.py:511
  20.3 1.6 %collective-permute-start.4 = (bf16[192,768]{1,0:T(8,128)(2,1)}, bf16[192,768]{1,0:T(8,128)(2,1)S(1)}, u32[]{:S(2)}, u32[]{:S(2)}) collective-permute-start(bf16[192,768]{1,0:T(8,128)(2,1)} %get-tuple-element.37), channel_id=1, source_target_pairs={{0,2},{1,3},{2,0},{3,1},{4,6},{5,7},{6,4},{7,5},{8,10},{9,11},{10,... | collective-permute-start | bytes 884744 | tf_op jit(solution)/shard_map/ppermute | solution.py:511
  21.8 6.1 %inside.1.refs_6_ = bf16[1024,768]{1,0:T(8,128)(2,1)} custom-call(bf16[16,128]{1,0:T(8,128)(2,1)} %get-tuple-element.30.codes_at.refs_0_, bf16[1024,1024]{1,0:T(8,128)(2,1)} %get-tuple-element.31.raw_at.refs_5_), custom_call_target="tpu_custom_call" | custom-call | flops 1 | bytes 1 | tf_op jit(solution)/shard_map/inside/pallas_call | solution.py:305
  28.9 1.8 %collective-permute-start.1 = (bf16[2,128,128]{2,1,0:T(8,128)(2,1)S(1)}, bf16[2,128,128]{2,1,0:T(8,128)(2,1)S(1)}, u32[]{:S(2)}, u32[]{:S(2)}) collective-permute-start(bf16[2,128,128]{2,1,0:T(8,128)(2,1)S(1)} %gather.1.refs_1_), channel_id=1, source_target_pairs={{0,4},{4,0},{8,12},{12,8},{16,20},{20,16},{24,28},{28,24},{32,36},... | collective-permute-start | bytes 196616 | tf_op jit(solution)/shard_map/ppermute | solution.py:525
  30.8 0.9 collective-permute-done.1.refs_2_
  32.3 3.5 %attend.1.done = bf16[1024,768]{1,0:T(8,128)(2,1)} custom-call(bf16[16,128]{1,0:T(8,128)(2,1)} %get-tuple-element.30.codes_at.refs_0_, bf16[2,128,128]{2,1,0:T(8,128)(2,1)} %copy-done.4, bf16[2,128,128]{2,1,0:T(8,128)(2,1)} %copy-done.7, bf16[2,2,128,128]{3,2,1,0:T(8,128)(2,1)} %copy-done.6, f32[2,2,2,128,128]{4,3,2,1,0:T(8,128)} %get-tuple-element.33.refs_4_, ...), custom_call_target="tpu_custom_call" | custom-call | flops 1 | bytes 1 | tf_op jit(solution)/shard_map/attend/pallas_call | solution.py:363
  35.8 1.4 %collective-permute-start.5 = (bf16[1024,768]{1,0:T(8,128)(2,1)}, bf16[1024,768]{1,0:T(8,128)(2,1)S(1)}, u32[]{:S(2)}, u32[]{:S(2)}) collective-permute-start(bf16[1024,768]{1,0:T(8,128)(2,1)} %attend.1.done), channel_id=1, source_target_pairs={{0,3},{1,0},{2,1},{3,2},{4,5},{5,6},{6,7},{7,4},{8,11},{9,8},{10,9... | collective-permute-start | bytes 4718600 | tf_op jit(solution)/shard_map/ppermute | solution.py:520
  37.2 1.5 %collective-permute-start.6 = (bf16[1024,768]{1,0:T(8,128)(2,1)}, bf16[1024,768]{1,0:T(8,128)(2,1)S(1)}, u32[]{:S(2)}, u32[]{:S(2)}) collective-permute-start(bf16[1024,768]{1,0:T(8,128)(2,1)} %attend.1.done), channel_id=1, source_target_pairs={{0,1},{1,2},{2,3},{3,0},{4,7},{5,4},{6,5},{7,6},{8,9},{9,10},{10,1... | collective-permute-start | bytes 4718600 | tf_op jit(solution)/shard_map/ppermute | solution.py:520
  38.8 2.6 %collective-permute-start.10 = (bf16[3,192,768]{2,1,0:T(8,128)(2,1)S(1)}, bf16[3,192,768]{2,1,0:T(8,128)(2,1)S(1)}, u32[]{:S(2)}, u32[]{:S(2)}) collective-permute-start(bf16[3,192,768]{2,1,0:T(8,128)(2,1)S(1)} %pad_maximum_fusion.refs_0_), channel_id=1, source_target_pairs={{0,64},{4,20},{8,72},{12,28},{16,80},{20,4},{24,88},{28,12},{32,96... | collective-permute-start | bytes 2654216 | tf_op jit(solution)/shard_map/ppermute | solution.py:525
  41.4 0.9 collective-permute-start.11
  42.9 1.9 %copy-done = bf16[6144,256]{1,0:T(8,128)(2,1)S(1)} copy-done((bf16[6144,256]{1,0:T(8,128)(2,1)S(1)}, bf16[6144,256]{1,0:T(8,128)(2,1)}, u32[]{:S(2)}) %copy-start) | copy-done | bytes 3145752
  44.8 1.9 %copy-done.1 = bf16[6144,256]{1,0:T(8,128)(2,1)S(1)} copy-done((bf16[6144,256]{1,0:T(8,128)(2,1)S(1)}, bf16[6144,256]{1,0:T(8,128)(2,1)}, u32[]{:S(2)}) %copy-start.1) | copy-done | bytes 3145752
  46.7 1.9 %copy-done.2 = bf16[6144,256]{1,0:T(8,128)(2,1)S(1)} copy-done((bf16[6144,256]{1,0:T(8,128)(2,1)S(1)}, bf16[6144,256]{1,0:T(8,128)(2,1)}, u32[]{:S(2)}) %copy-start.2) | copy-done | bytes 3145752
  48.6 1.4 %copy-done.3 = bf16[1024,768]{1,0:T(8,128)(2,1)S(1)} copy-done((bf16[1024,768]{1,0:T(8,128)(2,1)S(1)}, bf16[1024,768]{1,0:T(8,128)(2,1)}, u32[]{:S(2)}) %copy-start.3) | copy-done | bytes 1572888
  50.0 7.1 %project_own.1.refs_3_ = bf16[1024,1536]{1,0:T(8,128)(2,1)S(1)} custom-call(bf16[1024,768]{1,0:T(8,128)(2,1)S(1)} %copy-done.3, bf16[6144,256]{1,0:T(8,128)(2,1)S(1)} %copy-done, bf16[6144,256]{1,0:T(8,128)(2,1)S(1)} %copy-done.1, bf16[6144,256]{1,0:T(8,128)(2,1)S(1)} %copy-done.2), custom_call_target="tpu_custom_call" | custom-call | flops 1 | bytes 1 | tf_op jit(solution)/shard_map/project_own/pallas_call | solution.py:402
  57.1 12.9 %collective-permute-done.5.refs_0_ = bf16[1024,768]{1,0:T(8,128)(2,1)S(1)} collective-permute-done((bf16[1024,768]{1,0:T(8,128)(2,1)}, bf16[1024,768]{1,0:T(8,128)(2,1)S(1)}, u32[]{:S(2)}, u32[]{:S(2)}) %collective-permute-start.5) | collective-permute-done | bytes 1572896 | tf_op jit(solution)/shard_map/ppermute | solution.py:520
  70.0 3.4 %collective-permute-done.6.refs_1_ = bf16[1024,768]{1,0:T(8,128)(2,1)S(1)} collective-permute-done((bf16[1024,768]{1,0:T(8,128)(2,1)}, bf16[1024,768]{1,0:T(8,128)(2,1)S(1)}, u32[]{:S(2)}, u32[]{:S(2)}) %collective-permute-start.6) | collective-permute-done | bytes 1572896 | tf_op jit(solution)/shard_map/ppermute | solution.py:520
  73.6 0.9 collective-permute-start.12
  75.2 2.4 %collective-permute-start.14 = (bf16[256,768]{1,0:T(8,128)(2,1)S(1)}, bf16[256,768]{1,0:T(8,128)(2,1)S(1)}, u32[]{:S(2)}, u32[]{:S(2)}) collective-permute-start(bf16[256,768]{1,0:T(8,128)(2,1)S(1)} %get-tuple-element.49), channel_id=1, source_target_pairs={{0,1},{1,2},{2,3},{3,0},{4,7},{5,4},{6,5},{7,6},{8,9},{9,10},{10,1... | collective-permute-start | bytes 1179656 | tf_op jit(solution)/shard_map/ppermute | solution.py:520
  77.6 2.7 %collective-permute-start.8 = (bf16[256,768]{1,0:T(8,128)(2,1)S(1)}, bf16[256,768]{1,0:T(8,128)(2,1)S(1)}, u32[]{:S(2)}, u32[]{:S(2)}) collective-permute-start(bf16[256,768]{1,0:T(8,128)(2,1)S(1)} %get-tuple-element.50), channel_id=1, source_target_pairs={{0,1},{1,2},{2,3},{3,0},{4,7},{5,4},{6,5},{7,6},{8,9},{9,10},{10,1... | collective-permute-start | bytes 1179656 | tf_op jit(solution)/shard_map/ppermute | solution.py:520
  80.3 2.7 %project_others.2.refs_3_ = bf16[1024,1536]{1,0:T(8,128)(2,1)S(1)} custom-call(bf16[1024,768]{1,0:T(8,128)(2,1)S(1)} %collective-permute-done.5.refs_0_, bf16[1024,768]{1,0:T(8,128)(2,1)S(1)} %collective-permute-done.6.refs_1_, bf16[3,768,768]{2,1,0:T(8,128)(2,1)S(1)} %arrange.1.refs_2_, ...), custom_call_target="tpu_custom_call", output_to_operand_aliasing={{}: (3, {})} | custom-call | flops 1 | bytes 1 | tf_op jit(solution)/shard_map/project_others/pallas_call | solution.py:461
  83.0 2.7 %project_others.3.refs_4_ = bf16[1024,1536]{1,0:T(8,128)(2,1)S(1)} custom-call(bf16[1024,768]{1,0:T(8,128)(2,1)S(1)} %collective-permute-done.5.refs_0_, bf16[1024,768]{1,0:T(8,128)(2,1)S(1)} %collective-permute-done.6.refs_1_, bf16[3,768,768]{2,1,0:T(8,128)(2,1)S(1)} %collective-permute-done.12.refs_2_.refs_3_, ...), custom_call_target="tpu_custom_call", output_to_operand_aliasing={{}: (3, {})} | custom-call | flops 1 | bytes 1 | tf_op jit(solution)/shard_map/project_others/pallas_call | solution.py:461
  86.4 2.3 %project_last.2.refs_5_ = bf16[1024,1536]{1,0:T(8,128)(2,1)} custom-call(bf16[256,768]{1,0:T(8,128)(2,1)S(1)} %collective-permute-done.13.refs_0_, bf16[256,768]{1,0:T(8,128)(2,1)S(1)} %collective-permute-done.14.refs_1_, bf16[3,768,768]{2,1,0:T(8,128)(2,1)S(1)} %arrange.1.refs_2_, bf16[3,768,768]{2,1,0:T(8,128)(2,1)S(1)} %collective-permute-done.12.refs_2_.refs_3_, ...), custom_call_target="tpu_custom_call" | custom-call | flops 1 | bytes 1 | tf_op jit(solution)/shard_map/project_last/pallas_call | solution.py:497
  88.7 3.2 %collective-permute-done.7.refs_0_ = bf16[256,768]{1,0:T(8,128)(2,1)S(1)} collective-permute-done((bf16[256,768]{1,0:T(8,128)(2,1)S(1)}, bf16[256,768]{1,0:T(8,128)(2,1)S(1)}, u32[]{:S(2)}, u32[]{:S(2)}) %collective-permute-start.7) | collective-permute-done | bytes 393248 | tf_op jit(solution)/shard_map/ppermute | solution.py:520
  91.9 2.8 %collective-permute-done.8.refs_1_ = bf16[256,768]{1,0:T(8,128)(2,1)S(1)} collective-permute-done((bf16[256,768]{1,0:T(8,128)(2,1)S(1)}, bf16[256,768]{1,0:T(8,128)(2,1)S(1)}, u32[]{:S(2)}, u32[]{:S(2)}) %collective-permute-start.8) | collective-permute-done | bytes 393248 | tf_op jit(solution)/shard_map/ppermute | solution.py:520
  94.7 2.3 %project_last.3 = bf16[1024,1536]{1,0:T(8,128)(2,1)} custom-call(bf16[256,768]{1,0:T(8,128)(2,1)S(1)} %collective-permute-done.7.refs_0_, bf16[256,768]{1,0:T(8,128)(2,1)S(1)} %collective-permute-done.8.refs_1_, bf16[3,768,768]{2,1,0:T(8,128)(2,1)S(1)} %arrange.1.refs_2_, ...), custom_call_target="tpu_custom_call", output_to_operand_aliasing={{}: (5, {})} | custom-call | flops 1 | bytes 1 | tf_op jit(solution)/shard_map/project_last/pallas_call | solution.py:497
  (30 shorter events, 4.6 us)
Async XLA Ops:
  4.4 23.7 %copy-start.5 = (s32[2]{0:T(128)S(1)}, s32[2]{0:T(128)}, u32[]{:S(2)}) copy-start(s32[2]{0:T(128)} %decay_code.3) | copy-start | bytes 28
  4.4 2.7 %collective-permute-start = (bf16[2,2,128,128]{3,2,1,0:T(8,128)(2,1)}, bf16[2,2,128,128]{3,2,1,0:T(8,128)(2,1)S(1)}, u32[]{:S(2)}, u32[]{:S(2)}) collective-permute-start(bf16[2,2,128,128]{3,2,1,0:T(8,128)(2,1)} %get-tuple-element.28.mine_at), channel_id=1, source_target_pairs={{0,4},{4,0},{8,12},{12,8},{16,20},{20,16},{24,28},{28,24},{32,36},... | collective-permute-start | bytes 393224 | tf_op jit(solution)/shard_map/ppermute | solution.py:525
  7.1 0.6 copy-start.6
  9.7 18.4 %all-to-all-start = ((bf16[16,1,128,128]{3,2,1,0:T(8,128)(2,1)}), bf16[16,1,128,128]{3,2,1,0:T(8,128)(2,1)S(1)}, u32[]{:S(2)}, u32[]{:S(2)}) async-start(bf16[16,1,128,128]{3,2,1,0:T(8,128)(2,1)} %join.1), calls=%async_computation | async-start | bytes 1048576 | tf_op jit(solution)/shard_map/all_to_all | solution.py:552
  17.4 18.4 %collective-permute-start.2 = (bf16[192,768]{1,0:T(8,128)(2,1)}, bf16[192,768]{1,0:T(8,128)(2,1)S(1)}, u32[]{:S(2)}, u32[]{:S(2)}) collective-permute-start(bf16[192,768]{1,0:T(8,128)(2,1)} %get-tuple-element.35), channel_id=1, source_target_pairs={{0,1},{1,2},{2,3},{3,0},{4,5},{5,6},{6,7},{7,4},{8,9},{9,10},{10,1... | collective-permute-start | bytes 884744 | tf_op jit(solution)/shard_map/ppermute | solution.py:511
  18.8 17.1 %collective-permute-start.3 = (bf16[192,768]{1,0:T(8,128)(2,1)}, bf16[192,768]{1,0:T(8,128)(2,1)S(1)}, u32[]{:S(2)}, u32[]{:S(2)}) collective-permute-start(bf16[192,768]{1,0:T(8,128)(2,1)} %get-tuple-element.36), channel_id=1, source_target_pairs={{0,3},{1,0},{2,1},{3,2},{4,7},{5,4},{6,5},{7,6},{8,11},{9,8},{10,9... | collective-permute-start | bytes 884744 | tf_op jit(solution)/shard_map/ppermute | solution.py:511
  20.3 15.6 %collective-permute-start.4 = (bf16[192,768]{1,0:T(8,128)(2,1)}, bf16[192,768]{1,0:T(8,128)(2,1)S(1)}, u32[]{:S(2)}, u32[]{:S(2)}) collective-permute-start(bf16[192,768]{1,0:T(8,128)(2,1)} %get-tuple-element.37), channel_id=1, source_target_pairs={{0,2},{1,3},{2,0},{3,1},{4,6},{5,7},{6,4},{7,5},{8,10},{9,11},{10,... | collective-permute-start | bytes 884744 | tf_op jit(solution)/shard_map/ppermute | solution.py:511
  28.9 2.8 %copy-start.4 = (bf16[2,128,128]{2,1,0:T(8,128)(2,1)}, bf16[2,128,128]{2,1,0:T(8,128)(2,1)S(1)}, u32[]{:S(2)}) copy-start(bf16[2,128,128]{2,1,0:T(8,128)(2,1)S(1)} %gather.1.refs_1_) | copy-start | bytes 196612
  28.9 2.7 %collective-permute-start.1 = (bf16[2,128,128]{2,1,0:T(8,128)(2,1)S(1)}, bf16[2,128,128]{2,1,0:T(8,128)(2,1)S(1)}, u32[]{:S(2)}, u32[]{:S(2)}) collective-permute-start(bf16[2,128,128]{2,1,0:T(8,128)(2,1)S(1)} %gather.1.refs_1_), channel_id=1, source_target_pairs={{0,4},{4,0},{8,12},{12,8},{16,20},{20,16},{24,28},{28,24},{32,36},... | collective-permute-start | bytes 196616 | tf_op jit(solution)/shard_map/ppermute | solution.py:525
  31.7 0.6 copy-start.7
  35.8 34.1 %collective-permute-start.5 = (bf16[1024,768]{1,0:T(8,128)(2,1)}, bf16[1024,768]{1,0:T(8,128)(2,1)S(1)}, u32[]{:S(2)}, u32[]{:S(2)}) collective-permute-start(bf16[1024,768]{1,0:T(8,128)(2,1)} %attend.1.done), channel_id=1, source_target_pairs={{0,3},{1,0},{2,1},{3,2},{4,5},{5,6},{6,7},{7,4},{8,11},{9,8},{10,9... | collective-permute-start | bytes 4718600 | tf_op jit(solution)/shard_map/ppermute | solution.py:520
  37.2 36.1 %collective-permute-start.6 = (bf16[1024,768]{1,0:T(8,128)(2,1)}, bf16[1024,768]{1,0:T(8,128)(2,1)S(1)}, u32[]{:S(2)}, u32[]{:S(2)}) collective-permute-start(bf16[1024,768]{1,0:T(8,128)(2,1)} %attend.1.done), channel_id=1, source_target_pairs={{0,1},{1,2},{2,3},{3,0},{4,7},{5,4},{6,5},{7,6},{8,9},{9,10},{10,1... | collective-permute-start | bytes 4718600 | tf_op jit(solution)/shard_map/ppermute | solution.py:520
  38.8 34.5 %collective-permute-start.10 = (bf16[3,192,768]{2,1,0:T(8,128)(2,1)S(1)}, bf16[3,192,768]{2,1,0:T(8,128)(2,1)S(1)}, u32[]{:S(2)}, u32[]{:S(2)}) collective-permute-start(bf16[3,192,768]{2,1,0:T(8,128)(2,1)S(1)} %pad_maximum_fusion.refs_0_), channel_id=1, source_target_pairs={{0,64},{4,20},{8,72},{12,28},{16,80},{20,4},{24,88},{28,12},{32,96... | collective-permute-start | bytes 2654216 | tf_op jit(solution)/shard_map/ppermute | solution.py:525
  41.4 31.9 %collective-permute-start.11 = (bf16[3,192,768]{2,1,0:T(8,128)(2,1)S(1)}, bf16[3,192,768]{2,1,0:T(8,128)(2,1)S(1)}, u32[]{:S(2)}, u32[]{:S(2)}) collective-permute-start(bf16[3,192,768]{2,1,0:T(8,128)(2,1)S(1)} %pad_maximum_fusion.refs_0_), channel_id=1, source_target_pairs={{0,96},{4,28},{8,104},{12,4},{16,112},{20,12},{24,120},{28,20},{32... | collective-permute-start | bytes 2654216 | tf_op jit(solution)/shard_map/ppermute | solution.py:525
  42.3 31.0 %collective-permute-start.9 = (bf16[3,192,768]{2,1,0:T(8,128)(2,1)S(1)}, bf16[3,192,768]{2,1,0:T(8,128)(2,1)S(1)}, u32[]{:S(2)}, u32[]{:S(2)}) collective-permute-start(bf16[3,192,768]{2,1,0:T(8,128)(2,1)S(1)} %pad_maximum_fusion.refs_0_), channel_id=1, source_target_pairs={{0,32},{4,12},{8,40},{12,20},{16,48},{20,28},{24,56},{28,4},{32,64... | collective-permute-start | bytes 2654216 | tf_op jit(solution)/shard_map/ppermute | solution.py:525
  42.9 1.9 %copy-start = (bf16[6144,256]{1,0:T(8,128)(2,1)S(1)}, bf16[6144,256]{1,0:T(8,128)(2,1)}, u32[]{:S(2)}) copy-start(bf16[6144,256]{1,0:T(8,128)(2,1)} %wq.1) | copy-start | bytes 9437188
  44.8 1.9 %copy-start.1 = (bf16[6144,256]{1,0:T(8,128)(2,1)S(1)}, bf16[6144,256]{1,0:T(8,128)(2,1)}, u32[]{:S(2)}) copy-start(bf16[6144,256]{1,0:T(8,128)(2,1)} %wk.1) | copy-start | bytes 9437188
  46.7 1.9 %copy-start.2 = (bf16[6144,256]{1,0:T(8,128)(2,1)S(1)}, bf16[6144,256]{1,0:T(8,128)(2,1)}, u32[]{:S(2)}) copy-start(bf16[6144,256]{1,0:T(8,128)(2,1)} %wv.1) | copy-start | bytes 9437188
  48.6 1.4 %copy-start.3 = (bf16[1024,768]{1,0:T(8,128)(2,1)S(1)}, bf16[1024,768]{1,0:T(8,128)(2,1)}, u32[]{:S(2)}) copy-start(bf16[1024,768]{1,0:T(8,128)(2,1)} %attend.1.done) | copy-start | bytes 4718596
  73.6 9.3 %collective-permute-start.12 = (bf16[3,768,768]{2,1,0:T(8,128)(2,1)S(1)}, bf16[3,768,768]{2,1,0:T(8,128)(2,1)S(1)}, u32[]{:S(2)}, u32[]{:S(2)}) collective-permute-start(bf16[3,768,768]{2,1,0:T(8,128)(2,1)S(1)} %arrange.1.refs_2_), channel_id=1, source_target_pairs={{0,4},{4,0},{8,12},{12,8},{16,20},{20,16},{24,28},{28,24},{32,36},... | collective-permute-start | bytes 10616840 | tf_op jit(solution)/shard_map/ppermute | solution.py:525
  74.6 11.0 %collective-permute-start.13 = (bf16[256,768]{1,0:T(8,128)(2,1)S(1)}, bf16[256,768]{1,0:T(8,128)(2,1)S(1)}, u32[]{:S(2)}, u32[]{:S(2)}) collective-permute-start(bf16[256,768]{1,0:T(8,128)(2,1)S(1)} %get-tuple-element.51), channel_id=1, source_target_pairs={{0,3},{1,0},{2,1},{3,2},{4,5},{5,6},{6,7},{7,4},{8,11},{9,8},{10,9... | collective-permute-start | bytes 1179656 | tf_op jit(solution)/shard_map/ppermute | solution.py:520
  75.2 11.3 %collective-permute-start.14 = (bf16[256,768]{1,0:T(8,128)(2,1)S(1)}, bf16[256,768]{1,0:T(8,128)(2,1)S(1)}, u32[]{:S(2)}, u32[]{:S(2)}) collective-permute-start(bf16[256,768]{1,0:T(8,128)(2,1)S(1)} %get-tuple-element.49), channel_id=1, source_target_pairs={{0,1},{1,2},{2,3},{3,0},{4,7},{5,4},{6,5},{7,6},{8,9},{9,10},{10,1... | collective-permute-start | bytes 1179656 | tf_op jit(solution)/shard_map/ppermute | solution.py:520
  77.6 14.3 %collective-permute-start.7 = (bf16[256,768]{1,0:T(8,128)(2,1)S(1)}, bf16[256,768]{1,0:T(8,128)(2,1)S(1)}, u32[]{:S(2)}, u32[]{:S(2)}) collective-permute-start(bf16[256,768]{1,0:T(8,128)(2,1)S(1)} %get-tuple-element.52), channel_id=1, source_target_pairs={{0,3},{1,0},{2,1},{3,2},{4,5},{5,6},{6,7},{7,4},{8,11},{9,8},{10,9... | collective-permute-start | bytes 1179656 | tf_op jit(solution)/shard_map/ppermute | solution.py:520
  77.6 17.1 %collective-permute-start.8 = (bf16[256,768]{1,0:T(8,128)(2,1)S(1)}, bf16[256,768]{1,0:T(8,128)(2,1)S(1)}, u32[]{:S(2)}, u32[]{:S(2)}) collective-permute-start(bf16[256,768]{1,0:T(8,128)(2,1)S(1)} %get-tuple-element.50), channel_id=1, source_target_pairs={{0,1},{1,2},{2,3},{3,0},{4,7},{5,4},{6,5},{7,6},{8,9},{9,10},{10,1... | collective-permute-start | bytes 1179656 | tf_op jit(solution)/shard_map/ppermute | solution.py:520

commit v7 on v6

--- a/solution.py
+++ b/solution.py
@@ -476,10 +476,12 @@
     partial, refs = refs[0], refs[1:]
     out, tiles, sems = refs[-3:]
     made = []
-    for i, ((src, start), part) in enumerate(zip(spans, parts)):
-        rows = part.shape[0]
-        for table, inside, at in column_tiles(tables, cores):
-            total = partial[start : start + rows, at].astype(f32) + nt(part[...], table[src - 1, inside])
+    src, rows = spans[0][0], parts[0].shape[0]
+    together = jnp.concatenate([part[...] for part in parts], axis=0)
+    for table, inside, at in column_tiles(tables, cores):
+        product = nt(together, table[src - 1, inside])
+        for i, (_, start) in enumerate(spans):
+            total = partial[start : start + rows, at].astype(f32) + product[i * rows : (i + 1) * rows]
             slot = len(made)
             tiles[slot] = total.astype(bf16)
             made.append(pltpu.make_async_copy(tiles.at[slot], out.at[pl.ds(start, rows), at], sems.at[slot]))

time: 97.6 us -> 97.7 us (level)
  no operation moved by 1% of the time
where the time goes in v7:
time: 97.7 us; the launch traced here: 97.2 us
  Pallas kernels  34.1 us (35%)
  starting transfers between devices  29 us (30%)
  waiting for transfers between devices  25.3 us (26%)
  local copies, waits for them, and re-layouts  8.45 us (9%)
    ppermute x6, waiting for transfers between devices, swing(): return lax.ppermute(a, ('seq', 'head'), pairs)  23 us
    ppermute x6, starting transfers between devices, swing(): return lax.ppermute(a, ('seq', 'head'), pairs)  8.49 us
    ppermute x6, starting transfers between devices, move(): return lax.ppermute(a, 'seq', pairs)  8.34 us
    unnamed x16, local copies, waits for them, and re-layouts  8.34 us
    all_to_all x1, starting transfers between devices, shards(): arrived = lax.all_to_all(leaving, 'seq', 0, 0, axis_index_groups=CHIPS)  7.69 us
    pallas_call x1, Pallas kernels, project_own(): pl.pallas_call(own_kernel, out_shape=spec(rows, cols), in_specs=whole(1)...  7.14 us
    pallas_call x1, Pallas kernels, inside(): pl.pallas_call(functools.partial(inside_kernel, early), out_shape=spec(co...  6.11 us
    pallas_call x2, Pallas kernels, project_others(): pl.pallas_call(functools.partial(others_kernel, spans, mirrored), out_sha...  5.35 us
  transfers between devices with their start and end apart: 16, of which 8 were waited for; matrix products, arithmetic and copies ran while one was open for 0% of the time, Pallas kernels for 26%

profile of v7, /device:TPU:1, one launch (start us, length us, event | category | flops | bytes accessed | tf_op | source)
XLA Modules:
  0.0 97.2 jit_solution(3466403793429591)
XLA Ops:
  0.0 4.4 %begin.1 = (bf16[1024,1024]{1,0:T(8,128)(2,1)}, bf16[16,128]{1,0:T(8,128)(2,1)}, f32[2,2,2,128,128]{4,3,2,1,0:T(8,128)}, bf16[2,2,128,128]{3,2,1,0:T(8,128)(2,1)...) custom-call(bf16[1024,256]{1,0:T(8,128)(2,1)} %q.1, bf16[1024,256]{1,0:T(8,128)(2,1)} %k.1, ...), custom_call_target="tpu_custom_call" | custom-call | flops 1 | bytes 1 | tf_op jit(solution)/shard_map/begin/pallas_call | solution.py:110
  4.4 1.5 %collective-permute-start = (bf16[2,2,128,128]{3,2,1,0:T(8,128)(2,1)}, bf16[2,2,128,128]{3,2,1,0:T(8,128)(2,1)S(1)}, u32[]{:S(2)}, u32[]{:S(2)}) collective-permute-start(bf16[2,2,128,128]{3,2,1,0:T(8,128)(2,1)} %get-tuple-element.28.mine_at), channel_id=1, source_target_pairs={{0,4},{4,0},{8,12},{12,8},{16,20},{20,16},{24,28},{28,24},{32,36},... | collective-permute-start | bytes 393224 | tf_op jit(solution)/shard_map/ppermute | solution.py:527
  5.9 1.2 %collective-permute-done.other_at.refs_3_ = bf16[2,2,128,128]{3,2,1,0:T(8,128)(2,1)S(1)} collective-permute-done((bf16[2,2,128,128]{3,2,1,0:T(8,128)(2,1)}, bf16[2,2,128,128]{3,2,1,0:T(8,128)(2,1)S(1)}, u32[]{:S(2)}, u32[]{:S(2)}) %collective-permute-start) | collective-permute-done | bytes 131104 | tf_op jit(solution)/shard_map/ppermute | solution.py:527
  7.7 1.9 %join.1 = bf16[16,1,128,128]{3,2,1,0:T(8,128)(2,1)} custom-call(bf16[16,128]{1,0:T(8,128)(2,1)} %get-tuple-element.30.codes_at.refs_0_, bf16[2,2,128,128]{3,2,1,0:T(8,128)(2,1)} %get-tuple-element.28.mine_at, bf16[2,2,128,128]{3,2,1,0:T(8,128)(2,1)} %copy-done.6), custom_call_target="tpu_custom_call" | custom-call | flops 1 | bytes 1 | tf_op jit(solution)/shard_map/join/pallas_call | solution.py:163
  9.7 7.7 %all-to-all-start = ((bf16[16,1,128,128]{3,2,1,0:T(8,128)(2,1)}), bf16[16,1,128,128]{3,2,1,0:T(8,128)(2,1)S(1)}, u32[]{:S(2)}, u32[]{:S(2)}) async-start(bf16[16,1,128,128]{3,2,1,0:T(8,128)(2,1)} %join.1), calls=%async_computation | async-start | bytes 1048576 | tf_op jit(solution)/shard_map/all_to_all | solution.py:554
  17.4 1.4 %collective-permute-start.2 = (bf16[192,768]{1,0:T(8,128)(2,1)}, bf16[192,768]{1,0:T(8,128)(2,1)S(1)}, u32[]{:S(2)}, u32[]{:S(2)}) collective-permute-start(bf16[192,768]{1,0:T(8,128)(2,1)} %get-tuple-element.35), channel_id=1, source_target_pairs={{0,1},{1,2},{2,3},{3,0},{4,5},{5,6},{6,7},{7,4},{8,9},{9,10},{10,1... | collective-permute-start | bytes 884744 | tf_op jit(solution)/shard_map/ppermute | solution.py:513
  18.8 1.5 %collective-permute-start.3 = (bf16[192,768]{1,0:T(8,128)(2,1)}, bf16[192,768]{1,0:T(8,128)(2,1)S(1)}, u32[]{:S(2)}, u32[]{:S(2)}) collective-permute-start(bf16[192,768]{1,0:T(8,128)(2,1)} %get-tuple-element.36), channel_id=1, source_target_pairs={{0,3},{1,0},{2,1},{3,2},{4,7},{5,4},{6,5},{7,6},{8,11},{9,8},{10,9... | collective-permute-start | bytes 884744 | tf_op jit(solution)/shard_map/ppermute | solution.py:513
  20.3 1.6 %collective-permute-start.4 = (bf16[192,768]{1,0:T(8,128)(2,1)}, bf16[192,768]{1,0:T(8,128)(2,1)S(1)}, u32[]{:S(2)}, u32[]{:S(2)}) collective-permute-start(bf16[192,768]{1,0:T(8,128)(2,1)} %get-tuple-element.37), channel_id=1, source_target_pairs={{0,2},{1,3},{2,0},{3,1},{4,6},{5,7},{6,4},{7,5},{8,10},{9,11},{10,... | collective-permute-start | bytes 884744 | tf_op jit(solution)/shard_map/ppermute | solution.py:513
  21.8 6.1 %inside.1.refs_6_ = bf16[1024,768]{1,0:T(8,128)(2,1)} custom-call(bf16[16,128]{1,0:T(8,128)(2,1)} %get-tuple-element.30.codes_at.refs_0_, bf16[1024,1024]{1,0:T(8,128)(2,1)} %get-tuple-element.31.raw_at.refs_5_), custom_call_target="tpu_custom_call" | custom-call | flops 1 | bytes 1 | tf_op jit(solution)/shard_map/inside/pallas_call | solution.py:305
  28.9 1.8 %collective-permute-start.1 = (bf16[2,128,128]{2,1,0:T(8,128)(2,1)S(1)}, bf16[2,128,128]{2,1,0:T(8,128)(2,1)S(1)}, u32[]{:S(2)}, u32[]{:S(2)}) collective-permute-start(bf16[2,128,128]{2,1,0:T(8,128)(2,1)S(1)} %gather.1.refs_1_), channel_id=1, source_target_pairs={{0,4},{4,0},{8,12},{12,8},{16,20},{20,16},{24,28},{28,24},{32,36},... | collective-permute-start | bytes 196616 | tf_op jit(solution)/shard_map/ppermute | solution.py:527
  30.8 0.9 collective-permute-done.1.refs_2_
  32.3 3.5 %attend.1.done = bf16[1024,768]{1,0:T(8,128)(2,1)} custom-call(bf16[16,128]{1,0:T(8,128)(2,1)} %get-tuple-element.30.codes_at.refs_0_, bf16[2,128,128]{2,1,0:T(8,128)(2,1)} %copy-done.4, bf16[2,128,128]{2,1,0:T(8,128)(2,1)} %copy-done.7, bf16[2,2,128,128]{3,2,1,0:T(8,128)(2,1)} %copy-done.6, f32[2,2,2,128,128]{4,3,2,1,0:T(8,128)} %get-tuple-element.33.refs_4_, ...), custom_call_target="tpu_custom_call" | custom-call | flops 1 | bytes 1 | tf_op jit(solution)/shard_map/attend/pallas_call | solution.py:363
  35.8 1.4 %collective-permute-start.5 = (bf16[1024,768]{1,0:T(8,128)(2,1)}, bf16[1024,768]{1,0:T(8,128)(2,1)S(1)}, u32[]{:S(2)}, u32[]{:S(2)}) collective-permute-start(bf16[1024,768]{1,0:T(8,128)(2,1)} %attend.1.done), channel_id=1, source_target_pairs={{0,3},{1,0},{2,1},{3,2},{4,5},{5,6},{6,7},{7,4},{8,11},{9,8},{10,9... | collective-permute-start | bytes 4718600 | tf_op jit(solution)/shard_map/ppermute | solution.py:522
  37.2 1.5 %collective-permute-start.6 = (bf16[1024,768]{1,0:T(8,128)(2,1)}, bf16[1024,768]{1,0:T(8,128)(2,1)S(1)}, u32[]{:S(2)}, u32[]{:S(2)}) collective-permute-start(bf16[1024,768]{1,0:T(8,128)(2,1)} %attend.1.done), channel_id=1, source_target_pairs={{0,1},{1,2},{2,3},{3,0},{4,7},{5,4},{6,5},{7,6},{8,9},{9,10},{10,1... | collective-permute-start | bytes 4718600 | tf_op jit(solution)/shard_map/ppermute | solution.py:522
  38.8 2.6 %collective-permute-start.10 = (bf16[3,192,768]{2,1,0:T(8,128)(2,1)S(1)}, bf16[3,192,768]{2,1,0:T(8,128)(2,1)S(1)}, u32[]{:S(2)}, u32[]{:S(2)}) collective-permute-start(bf16[3,192,768]{2,1,0:T(8,128)(2,1)S(1)} %pad_maximum_fusion.refs_0_), channel_id=1, source_target_pairs={{0,64},{4,20},{8,72},{12,28},{16,80},{20,4},{24,88},{28,12},{32,96... | collective-permute-start | bytes 2654216 | tf_op jit(solution)/shard_map/ppermute | solution.py:527
  41.4 0.9 collective-permute-start.11
  42.9 1.9 %copy-done = bf16[6144,256]{1,0:T(8,128)(2,1)S(1)} copy-done((bf16[6144,256]{1,0:T(8,128)(2,1)S(1)}, bf16[6144,256]{1,0:T(8,128)(2,1)}, u32[]{:S(2)}) %copy-start) | copy-done | bytes 3145752
  44.8 1.9 %copy-done.1 = bf16[6144,256]{1,0:T(8,128)(2,1)S(1)} copy-done((bf16[6144,256]{1,0:T(8,128)(2,1)S(1)}, bf16[6144,256]{1,0:T(8,128)(2,1)}, u32[]{:S(2)}) %copy-start.1) | copy-done | bytes 3145752
  46.7 1.9 %copy-done.2 = bf16[6144,256]{1,0:T(8,128)(2,1)S(1)} copy-done((bf16[6144,256]{1,0:T(8,128)(2,1)S(1)}, bf16[6144,256]{1,0:T(8,128)(2,1)}, u32[]{:S(2)}) %copy-start.2) | copy-done | bytes 3145752
  48.6 1.4 %copy-done.3 = bf16[1024,768]{1,0:T(8,128)(2,1)S(1)} copy-done((bf16[1024,768]{1,0:T(8,128)(2,1)S(1)}, bf16[1024,768]{1,0:T(8,128)(2,1)}, u32[]{:S(2)}) %copy-start.3) | copy-done | bytes 1572888
  50.0 7.1 %project_own.1.refs_3_ = bf16[1024,1536]{1,0:T(8,128)(2,1)S(1)} custom-call(bf16[1024,768]{1,0:T(8,128)(2,1)S(1)} %copy-done.3, bf16[6144,256]{1,0:T(8,128)(2,1)S(1)} %copy-done, bf16[6144,256]{1,0:T(8,128)(2,1)S(1)} %copy-done.1, bf16[6144,256]{1,0:T(8,128)(2,1)S(1)} %copy-done.2), custom_call_target="tpu_custom_call" | custom-call | flops 1 | bytes 1 | tf_op jit(solution)/shard_map/project_own/pallas_call | solution.py:402
  57.1 12.9 %collective-permute-done.5.refs_0_ = bf16[1024,768]{1,0:T(8,128)(2,1)S(1)} collective-permute-done((bf16[1024,768]{1,0:T(8,128)(2,1)}, bf16[1024,768]{1,0:T(8,128)(2,1)S(1)}, u32[]{:S(2)}, u32[]{:S(2)}) %collective-permute-start.5) | collective-permute-done | bytes 1572896 | tf_op jit(solution)/shard_map/ppermute | solution.py:522
  70.0 3.4 %collective-permute-done.6.refs_1_ = bf16[1024,768]{1,0:T(8,128)(2,1)S(1)} collective-permute-done((bf16[1024,768]{1,0:T(8,128)(2,1)}, bf16[1024,768]{1,0:T(8,128)(2,1)S(1)}, u32[]{:S(2)}, u32[]{:S(2)}) %collective-permute-start.6) | collective-permute-done | bytes 1572896 | tf_op jit(solution)/shard_map/ppermute | solution.py:522
  73.6 0.9 collective-permute-start.12
  75.2 2.4 %collective-permute-start.14 = (bf16[256,768]{1,0:T(8,128)(2,1)S(1)}, bf16[256,768]{1,0:T(8,128)(2,1)S(1)}, u32[]{:S(2)}, u32[]{:S(2)}) collective-permute-start(bf16[256,768]{1,0:T(8,128)(2,1)S(1)} %get-tuple-element.49), channel_id=1, source_target_pairs={{0,1},{1,2},{2,3},{3,0},{4,7},{5,4},{6,5},{7,6},{8,9},{9,10},{10,1... | collective-permute-start | bytes 1179656 | tf_op jit(solution)/shard_map/ppermute | solution.py:522
  77.6 2.7 %collective-permute-start.8 = (bf16[256,768]{1,0:T(8,128)(2,1)S(1)}, bf16[256,768]{1,0:T(8,128)(2,1)S(1)}, u32[]{:S(2)}, u32[]{:S(2)}) collective-permute-start(bf16[256,768]{1,0:T(8,128)(2,1)S(1)} %get-tuple-element.50), channel_id=1, source_target_pairs={{0,1},{1,2},{2,3},{3,0},{4,7},{5,4},{6,5},{7,6},{8,9},{9,10},{10,1... | collective-permute-start | bytes 1179656 | tf_op jit(solution)/shard_map/ppermute | solution.py:522
  80.3 2.7 %project_others.2.refs_3_ = bf16[1024,1536]{1,0:T(8,128)(2,1)S(1)} custom-call(bf16[1024,768]{1,0:T(8,128)(2,1)S(1)} %collective-permute-done.5.refs_0_, bf16[1024,768]{1,0:T(8,128)(2,1)S(1)} %collective-permute-done.6.refs_1_, bf16[3,768,768]{2,1,0:T(8,128)(2,1)S(1)} %arrange.1.refs_2_, ...), custom_call_target="tpu_custom_call", output_to_operand_aliasing={{}: (3, {})} | custom-call | flops 1 | bytes 1 | tf_op jit(solution)/shard_map/project_others/pallas_call | solution.py:461
  83.0 2.7 %project_others.3.refs_4_ = bf16[1024,1536]{1,0:T(8,128)(2,1)S(1)} custom-call(bf16[1024,768]{1,0:T(8,128)(2,1)S(1)} %collective-permute-done.5.refs_0_, bf16[1024,768]{1,0:T(8,128)(2,1)S(1)} %collective-permute-done.6.refs_1_, bf16[3,768,768]{2,1,0:T(8,128)(2,1)S(1)} %collective-permute-done.12.refs_2_.refs_3_, ...), custom_call_target="tpu_custom_call", output_to_operand_aliasing={{}: (3, {})} | custom-call | flops 1 | bytes 1 | tf_op jit(solution)/shard_map/project_others/pallas_call | solution.py:461
  86.4 2.3 %project_last.2.refs_5_ = bf16[1024,1536]{1,0:T(8,128)(2,1)} custom-call(bf16[256,768]{1,0:T(8,128)(2,1)S(1)} %collective-permute-done.13.refs_0_, bf16[256,768]{1,0:T(8,128)(2,1)S(1)} %collective-permute-done.14.refs_1_, bf16[3,768,768]{2,1,0:T(8,128)(2,1)S(1)} %arrange.1.refs_2_, bf16[3,768,768]{2,1,0:T(8,128)(2,1)S(1)} %collective-permute-done.12.refs_2_.refs_3_, ...), custom_call_target="tpu_custom_call" | custom-call | flops 1 | bytes 1 | tf_op jit(solution)/shard_map/project_last/pallas_call | solution.py:499
  88.8 3.2 %collective-permute-done.7.refs_0_ = bf16[256,768]{1,0:T(8,128)(2,1)S(1)} collective-permute-done((bf16[256,768]{1,0:T(8,128)(2,1)S(1)}, bf16[256,768]{1,0:T(8,128)(2,1)S(1)}, u32[]{:S(2)}, u32[]{:S(2)}) %collective-permute-start.7) | collective-permute-done | bytes 393248 | tf_op jit(solution)/shard_map/ppermute | solution.py:522
  91.9 2.8 %collective-permute-done.8.refs_1_ = bf16[256,768]{1,0:T(8,128)(2,1)S(1)} collective-permute-done((bf16[256,768]{1,0:T(8,128)(2,1)S(1)}, bf16[256,768]{1,0:T(8,128)(2,1)S(1)}, u32[]{:S(2)}, u32[]{:S(2)}) %collective-permute-start.8) | collective-permute-done | bytes 393248 | tf_op jit(solution)/shard_map/ppermute | solution.py:522
  94.7 2.3 %project_last.3 = bf16[1024,1536]{1,0:T(8,128)(2,1)} custom-call(bf16[256,768]{1,0:T(8,128)(2,1)S(1)} %collective-permute-done.7.refs_0_, bf16[256,768]{1,0:T(8,128)(2,1)S(1)} %collective-permute-done.8.refs_1_, bf16[3,768,768]{2,1,0:T(8,128)(2,1)S(1)} %arrange.1.refs_2_, ...), custom_call_target="tpu_custom_call", output_to_operand_aliasing={{}: (5, {})} | custom-call | flops 1 | bytes 1 | tf_op jit(solution)/shard_map/project_last/pallas_call | solution.py:499
  (30 shorter events, 4.6 us)
Async XLA Ops:
  4.4 23.7 %copy-start.5 = (s32[2]{0:T(128)S(1)}, s32[2]{0:T(128)}, u32[]{:S(2)}) copy-start(s32[2]{0:T(128)} %decay_code.3) | copy-start | bytes 28
  4.4 2.7 %collective-permute-start = (bf16[2,2,128,128]{3,2,1,0:T(8,128)(2,1)}, bf16[2,2,128,128]{3,2,1,0:T(8,128)(2,1)S(1)}, u32[]{:S(2)}, u32[]{:S(2)}) collective-permute-start(bf16[2,2,128,128]{3,2,1,0:T(8,128)(2,1)} %get-tuple-element.28.mine_at), channel_id=1, source_target_pairs={{0,4},{4,0},{8,12},{12,8},{16,20},{20,16},{24,28},{28,24},{32,36},... | collective-permute-start | bytes 393224 | tf_op jit(solution)/shard_map/ppermute | solution.py:527
  7.1 0.6 copy-start.6
  9.7 18.4 %all-to-all-start = ((bf16[16,1,128,128]{3,2,1,0:T(8,128)(2,1)}), bf16[16,1,128,128]{3,2,1,0:T(8,128)(2,1)S(1)}, u32[]{:S(2)}, u32[]{:S(2)}) async-start(bf16[16,1,128,128]{3,2,1,0:T(8,128)(2,1)} %join.1), calls=%async_computation | async-start | bytes 1048576 | tf_op jit(solution)/shard_map/all_to_all | solution.py:554
  17.4 18.4 %collective-permute-start.2 = (bf16[192,768]{1,0:T(8,128)(2,1)}, bf16[192,768]{1,0:T(8,128)(2,1)S(1)}, u32[]{:S(2)}, u32[]{:S(2)}) collective-permute-start(bf16[192,768]{1,0:T(8,128)(2,1)} %get-tuple-element.35), channel_id=1, source_target_pairs={{0,1},{1,2},{2,3},{3,0},{4,5},{5,6},{6,7},{7,4},{8,9},{9,10},{10,1... | collective-permute-start | bytes 884744 | tf_op jit(solution)/shard_map/ppermute | solution.py:513
  18.8 17.1 %collective-permute-start.3 = (bf16[192,768]{1,0:T(8,128)(2,1)}, bf16[192,768]{1,0:T(8,128)(2,1)S(1)}, u32[]{:S(2)}, u32[]{:S(2)}) collective-permute-start(bf16[192,768]{1,0:T(8,128)(2,1)} %get-tuple-element.36), channel_id=1, source_target_pairs={{0,3},{1,0},{2,1},{3,2},{4,7},{5,4},{6,5},{7,6},{8,11},{9,8},{10,9... | collective-permute-start | bytes 884744 | tf_op jit(solution)/shard_map/ppermute | solution.py:513
  20.3 15.6 %collective-permute-start.4 = (bf16[192,768]{1,0:T(8,128)(2,1)}, bf16[192,768]{1,0:T(8,128)(2,1)S(1)}, u32[]{:S(2)}, u32[]{:S(2)}) collective-permute-start(bf16[192,768]{1,0:T(8,128)(2,1)} %get-tuple-element.37), channel_id=1, source_target_pairs={{0,2},{1,3},{2,0},{3,1},{4,6},{5,7},{6,4},{7,5},{8,10},{9,11},{10,... | collective-permute-start | bytes 884744 | tf_op jit(solution)/shard_map/ppermute | solution.py:513
  28.9 2.8 %copy-start.4 = (bf16[2,128,128]{2,1,0:T(8,128)(2,1)}, bf16[2,128,128]{2,1,0:T(8,128)(2,1)S(1)}, u32[]{:S(2)}) copy-start(bf16[2,128,128]{2,1,0:T(8,128)(2,1)S(1)} %gather.1.refs_1_) | copy-start | bytes 196612
  28.9 2.7 %collective-permute-start.1 = (bf16[2,128,128]{2,1,0:T(8,128)(2,1)S(1)}, bf16[2,128,128]{2,1,0:T(8,128)(2,1)S(1)}, u32[]{:S(2)}, u32[]{:S(2)}) collective-permute-start(bf16[2,128,128]{2,1,0:T(8,128)(2,1)S(1)} %gather.1.refs_1_), channel_id=1, source_target_pairs={{0,4},{4,0},{8,12},{12,8},{16,20},{20,16},{24,28},{28,24},{32,36},... | collective-permute-start | bytes 196616 | tf_op jit(solution)/shard_map/ppermute | solution.py:527
  31.7 0.6 copy-start.7
  35.8 34.1 %collective-permute-start.5 = (bf16[1024,768]{1,0:T(8,128)(2,1)}, bf16[1024,768]{1,0:T(8,128)(2,1)S(1)}, u32[]{:S(2)}, u32[]{:S(2)}) collective-permute-start(bf16[1024,768]{1,0:T(8,128)(2,1)} %attend.1.done), channel_id=1, source_target_pairs={{0,3},{1,0},{2,1},{3,2},{4,5},{5,6},{6,7},{7,4},{8,11},{9,8},{10,9... | collective-permute-start | bytes 4718600 | tf_op jit(solution)/shard_map/ppermute | solution.py:522
  37.2 36.1 %collective-permute-start.6 = (bf16[1024,768]{1,0:T(8,128)(2,1)}, bf16[1024,768]{1,0:T(8,128)(2,1)S(1)}, u32[]{:S(2)}, u32[]{:S(2)}) collective-permute-start(bf16[1024,768]{1,0:T(8,128)(2,1)} %attend.1.done), channel_id=1, source_target_pairs={{0,1},{1,2},{2,3},{3,0},{4,7},{5,4},{6,5},{7,6},{8,9},{9,10},{10,1... | collective-permute-start | bytes 4718600 | tf_op jit(solution)/shard_map/ppermute | solution.py:522
  38.8 34.5 %collective-permute-start.10 = (bf16[3,192,768]{2,1,0:T(8,128)(2,1)S(1)}, bf16[3,192,768]{2,1,0:T(8,128)(2,1)S(1)}, u32[]{:S(2)}, u32[]{:S(2)}) collective-permute-start(bf16[3,192,768]{2,1,0:T(8,128)(2,1)S(1)} %pad_maximum_fusion.refs_0_), channel_id=1, source_target_pairs={{0,64},{4,20},{8,72},{12,28},{16,80},{20,4},{24,88},{28,12},{32,96... | collective-permute-start | bytes 2654216 | tf_op jit(solution)/shard_map/ppermute | solution.py:527
  41.4 31.9 %collective-permute-start.11 = (bf16[3,192,768]{2,1,0:T(8,128)(2,1)S(1)}, bf16[3,192,768]{2,1,0:T(8,128)(2,1)S(1)}, u32[]{:S(2)}, u32[]{:S(2)}) collective-permute-start(bf16[3,192,768]{2,1,0:T(8,128)(2,1)S(1)} %pad_maximum_fusion.refs_0_), channel_id=1, source_target_pairs={{0,96},{4,28},{8,104},{12,4},{16,112},{20,12},{24,120},{28,20},{32... | collective-permute-start | bytes 2654216 | tf_op jit(solution)/shard_map/ppermute | solution.py:527
  42.3 31.0 %collective-permute-start.9 = (bf16[3,192,768]{2,1,0:T(8,128)(2,1)S(1)}, bf16[3,192,768]{2,1,0:T(8,128)(2,1)S(1)}, u32[]{:S(2)}, u32[]{:S(2)}) collective-permute-start(bf16[3,192,768]{2,1,0:T(8,128)(2,1)S(1)} %pad_maximum_fusion.refs_0_), channel_id=1, source_target_pairs={{0,32},{4,12},{8,40},{12,20},{16,48},{20,28},{24,56},{28,4},{32,64... | collective-permute-start | bytes 2654216 | tf_op jit(solution)/shard_map/ppermute | solution.py:527
  42.9 1.9 %copy-start = (bf16[6144,256]{1,0:T(8,128)(2,1)S(1)}, bf16[6144,256]{1,0:T(8,128)(2,1)}, u32[]{:S(2)}) copy-start(bf16[6144,256]{1,0:T(8,128)(2,1)} %wq.1) | copy-start | bytes 9437188
  44.8 1.9 %copy-start.1 = (bf16[6144,256]{1,0:T(8,128)(2,1)S(1)}, bf16[6144,256]{1,0:T(8,128)(2,1)}, u32[]{:S(2)}) copy-start(bf16[6144,256]{1,0:T(8,128)(2,1)} %wk.1) | copy-start | bytes 9437188
  46.7 1.9 %copy-start.2 = (bf16[6144,256]{1,0:T(8,128)(2,1)S(1)}, bf16[6144,256]{1,0:T(8,128)(2,1)}, u32[]{:S(2)}) copy-start(bf16[6144,256]{1,0:T(8,128)(2,1)} %wv.1) | copy-start | bytes 9437188
  48.6 1.4 %copy-start.3 = (bf16[1024,768]{1,0:T(8,128)(2,1)S(1)}, bf16[1024,768]{1,0:T(8,128)(2,1)}, u32[]{:S(2)}) copy-start(bf16[1024,768]{1,0:T(8,128)(2,1)} %attend.1.done) | copy-start | bytes 4718596
  73.6 9.3 %collective-permute-start.12 = (bf16[3,768,768]{2,1,0:T(8,128)(2,1)S(1)}, bf16[3,768,768]{2,1,0:T(8,128)(2,1)S(1)}, u32[]{:S(2)}, u32[]{:S(2)}) collective-permute-start(bf16[3,768,768]{2,1,0:T(8,128)(2,1)S(1)} %arrange.1.refs_2_), channel_id=1, source_target_pairs={{0,4},{4,0},{8,12},{12,8},{16,20},{20,16},{24,28},{28,24},{32,36},... | collective-permute-start | bytes 10616840 | tf_op jit(solution)/shard_map/ppermute | solution.py:527
  74.6 11.0 %collective-permute-start.13 = (bf16[256,768]{1,0:T(8,128)(2,1)S(1)}, bf16[256,768]{1,0:T(8,128)(2,1)S(1)}, u32[]{:S(2)}, u32[]{:S(2)}) collective-permute-start(bf16[256,768]{1,0:T(8,128)(2,1)S(1)} %get-tuple-element.51), channel_id=1, source_target_pairs={{0,3},{1,0},{2,1},{3,2},{4,5},{5,6},{6,7},{7,4},{8,11},{9,8},{10,9... | collective-permute-start | bytes 1179656 | tf_op jit(solution)/shard_map/ppermute | solution.py:522
  75.2 11.3 %collective-permute-start.14 = (bf16[256,768]{1,0:T(8,128)(2,1)S(1)}, bf16[256,768]{1,0:T(8,128)(2,1)S(1)}, u32[]{:S(2)}, u32[]{:S(2)}) collective-permute-start(bf16[256,768]{1,0:T(8,128)(2,1)S(1)} %get-tuple-element.49), channel_id=1, source_target_pairs={{0,1},{1,2},{2,3},{3,0},{4,7},{5,4},{6,5},{7,6},{8,9},{9,10},{10,1... | collective-permute-start | bytes 1179656 | tf_op jit(solution)/shard_map/ppermute | solution.py:522
  77.6 14.3 %collective-permute-start.7 = (bf16[256,768]{1,0:T(8,128)(2,1)S(1)}, bf16[256,768]{1,0:T(8,128)(2,1)S(1)}, u32[]{:S(2)}, u32[]{:S(2)}) collective-permute-start(bf16[256,768]{1,0:T(8,128)(2,1)S(1)} %get-tuple-element.52), channel_id=1, source_target_pairs={{0,3},{1,0},{2,1},{3,2},{4,5},{5,6},{6,7},{7,4},{8,11},{9,8},{10,9... | collective-permute-start | bytes 1179656 | tf_op jit(solution)/shard_map/ppermute | solution.py:522
  77.6 17.1 %collective-permute-start.8 = (bf16[256,768]{1,0:T(8,128)(2,1)S(1)}, bf16[256,768]{1,0:T(8,128)(2,1)S(1)}, u32[]{:S(2)}, u32[]{:S(2)}) collective-permute-start(bf16[256,768]{1,0:T(8,128)(2,1)S(1)} %get-tuple-element.50), channel_id=1, source_target_pairs={{0,1},{1,2},{2,3},{3,0},{4,7},{5,4},{6,5},{7,6},{8,9},{9,10},{10,1... | collective-permute-start | bytes 1179656 | tf_op jit(solution)/shard_map/ppermute | solution.py:522
